TPU v7x, 32 devices: a whole 2x2x4 slice. The times are simulated.
32 devices in a mesh: section: 4 (over y, core), dom: 8 (over z, x).
Axes of the slice: x: 2, y: 2, z: 4, core: 2. Of those that a mesh axis runs over, the one named last changes fastest.
Arguments:
- carry_h: bfloat16 [4, 8192, 512], P('section', 'dom'), may hold values from -6 to 6
- carry_h0: bfloat16 [4, 8192, 512], P('section', 'dom'), may hold values from -6 to 6
- new_h0: bfloat16 [3, 8192, 512], P(None, 'dom'), may hold values from -6 to 6
- weights: bfloat16 [4, 512, 512], P('section'), may hold values from -0.25 to 0.25
- adj_blocks: bfloat16 [64, 24, 128, 128], P('dom'), may hold values from -0.109375 to 0.109375
- col_index: int32 [64, 24], P('dom'), may hold values from 0 to 15
- counts: int32 [64], P('dom'), may hold values from 1 to 24, as said below
- send_list: int32 [8, 8], replicated, may hold values from 0 to 7
Outputs:
- layer_out: bfloat16 [4, 4, 8192, 512], P('section', None, 'dom')
Inputs may be any that keep to these rules, and one draw needn't show every extreme that they name: `counts`: every graph part has a row block with exactly 24 live blocks; parts differ in their mean load.
All inputs are finite; a program needn't handle non-finite values.
Results may differ from a plain program's by a relative error of at most 0.0052.
Values may be sent and summed in bfloat16 or wider, within the bound.
No kernel may reach another device: no remote copies, remote signals or barrier semaphores. Data moves between devices by JAX's collectives and lax.ppermute only.
A program may use at most 128 MiB of HBM per device.

v0:
```python
import jax
import jax.numpy as jnp
from jax import lax
from jax.sharding import PartitionSpec as P

BLOCK = 128
STEPS = 4


teleport = 0.2
strength = 1.5


def shifted_2(value, axis, by):
    length = lax.axis_size(axis)
    pairs = [(i, i + by) for i in range(length) if 0 <= i + by < length]
    return lax.ppermute(value, axis, pairs)


def body(carry_h, carry_h0, new_h0, weights, adj_blocks, col_index, counts, send_list):
    section_pos = lax.axis_index("section")
    part_index = lax.axis_index("dom")
    row_count = carry_h.shape[1]
    feature_width = carry_h.shape[2]
    block_count = row_count // BLOCK
    weight = weights[0]
    layer_beta = jnp.log(1.0 + strength / (section_pos.astype(jnp.float32) + 1.0))
    slot_ids = jnp.arange(adj_blocks.shape[1])
    live_slots = slot_ids[None, :] < counts[:, None]
    masked_adj = jnp.where(
        live_slots[:, :, None, None], adj_blocks, jnp.zeros((), adj_blocks.dtype)
    )
    outgoing_ids = lax.dynamic_index_in_dim(send_list, part_index, 0, keepdims=False)
    first_section = section_pos == 0
    current = carry_h[0]
    anchor = carry_h0[0]
    results = []
    delayed = [carry_h0[0]]
    for step_lag in range(1, STEPS):
        delayed.append(shifted_2(carry_h0[0], "section", step_lag))
    for step in range(STEPS):
        if step > 0:
            shifted = shifted_2(results[-1], "section", 1)
            current = jnp.where(first_section, new_h0[step - 1], shifted)
            fresh_index = jnp.clip(step - section_pos - 1, 0, new_h0.shape[0] - 1)
            fresh_anchor = lax.dynamic_index_in_dim(new_h0, fresh_index, 0, keepdims=False)
            anchor = jnp.where(section_pos >= step, delayed[step], fresh_anchor)
        own_blocks = current.reshape(block_count, BLOCK, feature_width)
        outgoing = jnp.take(own_blocks, outgoing_ids, axis=0)
        incoming = lax.all_to_all(outgoing, "dom", split_axis=0, concat_axis=0, tiled=True)
        lookup = jnp.concatenate([own_blocks, incoming], axis=0)
        picked = jnp.take(lookup, col_index, axis=0)
        gathered = jnp.einsum(
            "rkij,rkjd->rid", masked_adj, picked, preferred_element_type=jnp.float32
        )
        gathered = gathered.reshape(row_count, feature_width)
        mixture = ((1.0 - teleport) * gathered + teleport * anchor.astype(jnp.float32)).astype(
            jnp.bfloat16
        )
        product = jnp.dot(mixture, weight, preferred_element_type=jnp.float32)
        results.append(
            jax.nn.relu(
                (1.0 - layer_beta) * mixture.astype(jnp.float32) + layer_beta * product
            ).astype(jnp.bfloat16)
        )
    return jnp.stack(results)[None]


def solution(mesh):
    in_specs = (
        P("section", "dom", None),
        P("section", "dom", None),
        P(None, "dom", None),
        P("section", None, None),
        P("dom", None, None, None),
        P("dom", None),
        P("dom"),
        P(),
    )
    out_specs = P("section", None, "dom", None)
    return jax.shard_map(body, mesh=mesh, in_specs=in_specs, out_specs=out_specs, check_vma=False)
```

profile of v0, /device:TPU:1, one launch (start us, length us, event | category | flops | bytes accessed | tf_op | source)
XLA Modules:
  0.0 267.4 jit_solution(16854702832833732868)
XLA Ops:
  0.8 1.8 gather_fusion
  3.8 6.4 %all-to-all-start = ((bf16[8,128,512]{2,1,0:T(8,128)(2,1)}), bf16[8,128,512]{2,1,0:T(8,128)(2,1)}, u32[]{:S(2)}, u32[]{:S(2)}) async-start(bf16[8,128,512]{2,1,0:T(8,128)(2,1)} %broadcast_select_fusion.16), calls=%async_computation | async-start | bytes 2097152 | tf_op jit(solution)/shard_map/all_to_all | solution.py:50
  10.4 2.8 %convert_multiply_fusion = f32[1,1024,512]{2,1,0:T(8,128)} fusion(bf16[1,1024,512]{2,1,0:T(8,128)(2,1)} %param.13), kind=kLoop, calls=%fused_computation.51 | loop fusion | flops 1048576 | bytes 3145728 | tf_op jit(solution)/shard_map/mul | solution.py:57
  13.3 21.6 %all-to-all-done = bf16[8,128,512]{2,1,0:T(8,128)(2,1)} async-done(((bf16[8,128,512]{2,1,0:T(8,128)(2,1)}), bf16[8,128,512]{2,1,0:T(8,128)(2,1)}, u32[]{:S(2)}, u32[]{:S(2)}) %all-to-all-start) | async-done | bytes 1048608 | tf_op jit(solution)/shard_map/all_to_all | solution.py:50
  34.8 1.7 pad_maximum_fusion
  36.6 11.2 %gather_fusion.1 = bf16[192,128,512]{2,1,0:T(8,128)(2,1)} fusion(bf16[16,128,512]{2,1,0:T(8,128)(2,1)S(1)} %pad_maximum_fusion, s32[1024]{0:T(1024)S(1)} %pad_clamp_fusion), kind=kCustom, calls=%fused_computation.1.clone | custom fusion | bytes 50332416 | tf_op jit(solution)/shard_map/jit(_take)/gather | solution.py:52
  47.8 13.6 %add_convert_fusion = (bf16[8,128,512]{2,1,0:T(8,128)(2,1)}, f32[8,128,512]{2,1,0:T(8,128)S(1)}) fusion(f32[8,128,512]{2,1,0:T(8,128)} %bitcast.95, bf16[8,24,128,512]{3,2,1,0:T(8,128)(2,1)} %bitcast.83, pred[8,24]{1,0:T(8,128)(4,1)S(1)} %get-tuple-element.12, bf16[8,24,128,128]{3,2,1,0:T(8,128)(2,1)} %param.16, pred[8,24]{1,0:T(8,128)(4,1)S(1)} %get-tuple-element.11), kind=kOutput, calls=%fused_computation.50 | convolution fusion | flops 3238526976 | bytes 36700544 | tf_op jit(solution)/shard_map/rkij,rkjd->rid/dot_general | solution.py:53
  61.3 1.8 fusion.23
  64.0 5.1 %collective-permute-start = (bf16[1024,512]{1,0:T(8,128)(2,1)S(1)}, bf16[1024,512]{1,0:T(8,128)(2,1)S(1)}, u32[]{:S(2)}, u32[]{:S(2)}) collective-permute-start(bf16[1024,512]{1,0:T(8,128)(2,1)S(1)} %maximum_convert_fusion.3), channel_id=1, source_target_pairs={{0,8},{8,16},{16,24},{1,9},{9,17},{17,25},{2,10},{10,18},{18,26},{... | collective-permute-start | bytes 3145736 | tf_op jit(solution)/shard_map/ppermute | solution.py:17
  69.1 11.7 %collective-permute-done = bf16[1024,512]{1,0:T(8,128)(2,1)S(1)} collective-permute-done((bf16[1024,512]{1,0:T(8,128)(2,1)S(1)}, bf16[1024,512]{1,0:T(8,128)(2,1)S(1)}, u32[]{:S(2)}, u32[]{:S(2)}) %collective-permute-start) | collective-permute-done | bytes 1048608 | tf_op jit(solution)/shard_map/ppermute | solution.py:17
  83.9 4.2 %all-to-all-start.1 = ((bf16[8,128,512]{2,1,0:T(8,128)(2,1)}), bf16[8,128,512]{2,1,0:T(8,128)(2,1)}, u32[]{:S(2)}, u32[]{:S(2)}) async-start(bf16[8,128,512]{2,1,0:T(8,128)(2,1)} %broadcast_select_fusion.15), calls=%async_computation.1 | async-start | bytes 2097152 | tf_op jit(solution)/shard_map/all_to_all | solution.py:50
  88.2 4.4 %collective-permute-start.1 = (bf16[1024,512]{1,0:T(8,128)(2,1)}, bf16[1024,512]{1,0:T(8,128)(2,1)}, u32[]{:S(2)}, u32[]{:S(2)}) collective-permute-start(bf16[1024,512]{1,0:T(8,128)(2,1)} %bitcast.6), channel_id=1, source_target_pairs={{0,8},{8,16},{16,24},{1,9},{9,17},{17,25},{2,10},{10,18},{18,26},{... | collective-permute-start | bytes 3145736 | tf_op jit(solution)/shard_map/ppermute | solution.py:17
  92.6 11.4 %all-to-all-done.1 = bf16[8,128,512]{2,1,0:T(8,128)(2,1)} async-done(((bf16[8,128,512]{2,1,0:T(8,128)(2,1)}), bf16[8,128,512]{2,1,0:T(8,128)(2,1)}, u32[]{:S(2)}, u32[]{:S(2)}) %all-to-all-start.1) | async-done | bytes 1048608 | tf_op jit(solution)/shard_map/all_to_all | solution.py:50
  104.0 1.7 pad_maximum_fusion.1
  105.7 11.2 %gather_fusion.3 = bf16[192,128,512]{2,1,0:T(8,128)(2,1)} fusion(bf16[16,128,512]{2,1,0:T(8,128)(2,1)S(1)} %pad_maximum_fusion.1, s32[1024]{0:T(1024)S(1)} %pad_clamp_fusion), kind=kCustom, calls=%fused_computation.5.clone | custom fusion | bytes 50332416 | tf_op jit(solution)/shard_map/jit(_take)/gather | solution.py:52
  116.9 12.2 %bitcast_multiply_fusion.2 = f32[8,128,512]{2,1,0:T(8,128)S(1)} fusion(bf16[8,24,128,512]{3,2,1,0:T(8,128)(2,1)} %bitcast.85, pred[8,24]{1,0:T(8,128)(4,1)S(1)} %get-tuple-element.12, bf16[8,24,128,128]{3,2,1,0:T(8,128)(2,1)} %param.16, pred[8,24]{1,0:T(8,128)(4,1)S(1)} %get-tuple-element.11), kind=kOutput, calls=%fused_computation.42 | convolution fusion | flops 3237478400 | bytes 33554816 | tf_op jit(solution)/shard_map/rkij,rkjd->rid/dot_general | solution.py:53
  129.2 1.9 fusion.22
  131.9 5.0 %collective-permute-start.2 = (bf16[1024,512]{1,0:T(8,128)(2,1)S(1)}, bf16[1024,512]{1,0:T(8,128)(2,1)S(1)}, u32[]{:S(2)}, u32[]{:S(2)}) collective-permute-start(bf16[1024,512]{1,0:T(8,128)(2,1)S(1)} %maximum_convert_fusion.2), channel_id=1, source_target_pairs={{0,8},{8,16},{16,24},{1,9},{9,17},{17,25},{2,10},{10,18},{18,26},{... | collective-permute-start | bytes 3145736 | tf_op jit(solution)/shard_map/ppermute | solution.py:17
  136.9 11.7 %collective-permute-done.2 = bf16[1024,512]{1,0:T(8,128)(2,1)S(1)} collective-permute-done((bf16[1024,512]{1,0:T(8,128)(2,1)S(1)}, bf16[1024,512]{1,0:T(8,128)(2,1)S(1)}, u32[]{:S(2)}, u32[]{:S(2)}) %collective-permute-start.2) | collective-permute-done | bytes 1048608 | tf_op jit(solution)/shard_map/ppermute | solution.py:17
  150.5 4.2 %all-to-all-start.2 = ((bf16[8,128,512]{2,1,0:T(8,128)(2,1)}), bf16[8,128,512]{2,1,0:T(8,128)(2,1)}, u32[]{:S(2)}, u32[]{:S(2)}) async-start(bf16[8,128,512]{2,1,0:T(8,128)(2,1)} %broadcast_select_fusion.14), calls=%async_computation.2 | async-start | bytes 2097152 | tf_op jit(solution)/shard_map/all_to_all | solution.py:50
  154.8 2.3 collective-permute-start.3
  157.1 13.0 %all-to-all-done.2 = bf16[8,128,512]{2,1,0:T(8,128)(2,1)} async-done(((bf16[8,128,512]{2,1,0:T(8,128)(2,1)}), bf16[8,128,512]{2,1,0:T(8,128)(2,1)}, u32[]{:S(2)}, u32[]{:S(2)}) %all-to-all-start.2) | async-done | bytes 1048608 | tf_op jit(solution)/shard_map/all_to_all | solution.py:50
  171.8 11.2 %gather_fusion.5 = bf16[192,128,512]{2,1,0:T(8,128)(2,1)} fusion(bf16[16,128,512]{2,1,0:T(8,128)(2,1)S(1)} %pad_maximum_fusion.2, s32[1024]{0:T(1024)S(1)} %pad_clamp_fusion), kind=kCustom, calls=%fused_computation.6.clone | custom fusion | bytes 50332416 | tf_op jit(solution)/shard_map/jit(_take)/gather | solution.py:52
  183.0 12.2 %bitcast_multiply_fusion.1 = f32[8,128,512]{2,1,0:T(8,128)S(1)} fusion(bf16[8,24,128,512]{3,2,1,0:T(8,128)(2,1)} %bitcast.86, pred[8,24]{1,0:T(8,128)(4,1)S(1)} %get-tuple-element.12, bf16[8,24,128,128]{3,2,1,0:T(8,128)(2,1)} %param.16, pred[8,24]{1,0:T(8,128)(4,1)S(1)} %get-tuple-element.11), kind=kOutput, calls=%fused_computation.39 | convolution fusion | flops 3237478400 | bytes 33554816 | tf_op jit(solution)/shard_map/rkij,rkjd->rid/dot_general | solution.py:53
  196.8 6.7 %collective-permute-start.4 = (bf16[1024,512]{1,0:T(8,128)(2,1)S(1)}, bf16[1024,512]{1,0:T(8,128)(2,1)S(1)}, u32[]{:S(2)}, u32[]{:S(2)}) collective-permute-start(bf16[1024,512]{1,0:T(8,128)(2,1)S(1)} %maximum_convert_fusion.1), channel_id=1, source_target_pairs={{0,8},{8,16},{16,24},{1,9},{9,17},{17,25},{2,10},{10,18},{18,26},{... | collective-permute-start | bytes 3145736 | tf_op jit(solution)/shard_map/ppermute | solution.py:17
  203.5 11.7 %collective-permute-done.4 = bf16[1024,512]{1,0:T(8,128)(2,1)S(1)} collective-permute-done((bf16[1024,512]{1,0:T(8,128)(2,1)S(1)}, bf16[1024,512]{1,0:T(8,128)(2,1)S(1)}, u32[]{:S(2)}, u32[]{:S(2)}) %collective-permute-start.4) | collective-permute-done | bytes 1048608 | tf_op jit(solution)/shard_map/ppermute | solution.py:17
  217.1 4.2 %all-to-all-start.3 = ((bf16[8,128,512]{2,1,0:T(8,128)(2,1)}), bf16[8,128,512]{2,1,0:T(8,128)(2,1)}, u32[]{:S(2)}, u32[]{:S(2)}) async-start(bf16[8,128,512]{2,1,0:T(8,128)(2,1)} %broadcast_select_fusion.13), calls=%async_computation.3 | async-start | bytes 2097152 | tf_op jit(solution)/shard_map/all_to_all | solution.py:50
  223.0 13.3 %all-to-all-done.3 = bf16[8,128,512]{2,1,0:T(8,128)(2,1)} async-done(((bf16[8,128,512]{2,1,0:T(8,128)(2,1)}), bf16[8,128,512]{2,1,0:T(8,128)(2,1)}, u32[]{:S(2)}, u32[]{:S(2)}) %all-to-all-start.3) | async-done | bytes 1048608 | tf_op jit(solution)/shard_map/all_to_all | solution.py:50
  238.1 11.2 %gather_fusion.7 = bf16[192,128,512]{2,1,0:T(8,128)(2,1)} fusion(bf16[16,128,512]{2,1,0:T(8,128)(2,1)S(1)} %pad_maximum_fusion.3, s32[1024]{0:T(1024)S(1)} %pad_clamp_fusion), kind=kCustom, calls=%fused_computation.7.clone | custom fusion | bytes 50332416 | tf_op jit(solution)/shard_map/jit(_take)/gather | solution.py:52
  249.3 12.1 %bitcast_multiply_fusion = f32[8,128,512]{2,1,0:T(8,128)S(1)} fusion(bf16[8,24,128,512]{3,2,1,0:T(8,128)(2,1)} %bitcast.84, pred[8,24]{1,0:T(8,128)(4,1)S(1)} %get-tuple-element.12, bf16[8,24,128,128]{3,2,1,0:T(8,128)(2,1)} %param.16, pred[8,24]{1,0:T(8,128)(4,1)S(1)} %get-tuple-element.11), kind=kOutput, calls=%fused_computation.36 | convolution fusion | flops 3237478400 | bytes 33554816 | tf_op jit(solution)/shard_map/rkij,rkjd->rid/dot_general | solution.py:53
  261.4 1.9 fusion.20
  265.2 2.3 maximum_bitcast_fusion
  (57 shorter events, 18.9 us)
Async XLA Ops:
  0.0 63.2 %copy-start = (bf16[1,512,512]{2,1,0:T(8,128)(2,1)S(1)}, bf16[1,512,512]{2,1,0:T(8,128)(2,1)}, u32[]{:S(2)}) copy-start(bf16[1,512,512]{2,1,0:T(8,128)(2,1)} %param.15) | copy-start | bytes 1572868
  2.6 7.5 %copy-start.12 = (s32[8,24]{1,0:T(8,128)S(1)}, s32[8,24]{1,0:T(8,128)}, u32[]{:S(2)}) copy-start(s32[8,24]{1,0:T(8,128)} %param.17) | copy-start | bytes 2308
  2.6 7.7 %copy-start.13 = (s32[8]{0:T(128)S(1)}, s32[8]{0:T(128)}, u32[]{:S(2)}) copy-start(s32[8]{0:T(128)} %param.18) | copy-start | bytes 100
  3.8 31.1 %all-to-all-start = ((bf16[8,128,512]{2,1,0:T(8,128)(2,1)}), bf16[8,128,512]{2,1,0:T(8,128)(2,1)}, u32[]{:S(2)}, u32[]{:S(2)}) async-start(bf16[8,128,512]{2,1,0:T(8,128)(2,1)} %broadcast_select_fusion.16), calls=%async_computation | async-start | bytes 2097152 | tf_op jit(solution)/shard_map/all_to_all | solution.py:50
  61.3 1.9 copy-start.14
  64.0 5.2 %copy-start.6 = (bf16[1024,512]{1,0:T(8,128)(2,1)}, bf16[1024,512]{1,0:T(8,128)(2,1)S(1)}, u32[]{:S(2)}) copy-start(bf16[1024,512]{1,0:T(8,128)(2,1)S(1)} %maximum_convert_fusion.3) | copy-start | bytes 3145732
  64.0 16.9 %collective-permute-start = (bf16[1024,512]{1,0:T(8,128)(2,1)S(1)}, bf16[1024,512]{1,0:T(8,128)(2,1)S(1)}, u32[]{:S(2)}, u32[]{:S(2)}) collective-permute-start(bf16[1024,512]{1,0:T(8,128)(2,1)S(1)} %maximum_convert_fusion.3), channel_id=1, source_target_pairs={{0,8},{8,16},{16,24},{1,9},{9,17},{17,25},{2,10},{10,18},{18,26},{... | collective-permute-start | bytes 3145736 | tf_op jit(solution)/shard_map/ppermute | solution.py:17
  82.2 1.8 copy-start.5
  83.9 20.1 %all-to-all-start.1 = ((bf16[8,128,512]{2,1,0:T(8,128)(2,1)}), bf16[8,128,512]{2,1,0:T(8,128)(2,1)}, u32[]{:S(2)}, u32[]{:S(2)}) async-start(bf16[8,128,512]{2,1,0:T(8,128)(2,1)} %broadcast_select_fusion.15), calls=%async_computation.1 | async-start | bytes 2097152 | tf_op jit(solution)/shard_map/all_to_all | solution.py:50
  88.2 41.0 %collective-permute-start.1 = (bf16[1024,512]{1,0:T(8,128)(2,1)}, bf16[1024,512]{1,0:T(8,128)(2,1)}, u32[]{:S(2)}, u32[]{:S(2)}) collective-permute-start(bf16[1024,512]{1,0:T(8,128)(2,1)} %bitcast.6), channel_id=1, source_target_pairs={{0,8},{8,16},{16,24},{1,9},{9,17},{17,25},{2,10},{10,18},{18,26},{... | collective-permute-start | bytes 3145736 | tf_op jit(solution)/shard_map/ppermute | solution.py:17
  116.9 12.3 %copy-start.1 = (bf16[3,1024,512]{2,1,0:T(8,128)(2,1)S(1)}, bf16[3,1024,512]{2,1,0:T(8,128)(2,1)}, u32[]{:S(2)}) copy-start(bf16[3,1024,512]{2,1,0:T(8,128)(2,1)} %param.14) | copy-start | bytes 9437188
  131.9 16.9 %copy-start.8 = (bf16[1024,512]{1,0:T(8,128)(2,1)}, bf16[1024,512]{1,0:T(8,128)(2,1)S(1)}, u32[]{:S(2)}) copy-start(bf16[1024,512]{1,0:T(8,128)(2,1)S(1)} %maximum_convert_fusion.2) | copy-start | bytes 3145732
  131.9 16.7 %collective-permute-start.2 = (bf16[1024,512]{1,0:T(8,128)(2,1)S(1)}, bf16[1024,512]{1,0:T(8,128)(2,1)S(1)}, u32[]{:S(2)}, u32[]{:S(2)}) collective-permute-start(bf16[1024,512]{1,0:T(8,128)(2,1)S(1)} %maximum_convert_fusion.2), channel_id=1, source_target_pairs={{0,8},{8,16},{16,24},{1,9},{9,17},{17,25},{2,10},{10,18},{18,26},{... | collective-permute-start | bytes 3145736 | tf_op jit(solution)/shard_map/ppermute | solution.py:17
  148.7 1.8 copy-start.4
  150.5 19.6 %all-to-all-start.2 = ((bf16[8,128,512]{2,1,0:T(8,128)(2,1)}), bf16[8,128,512]{2,1,0:T(8,128)(2,1)}, u32[]{:S(2)}, u32[]{:S(2)}) async-start(bf16[8,128,512]{2,1,0:T(8,128)(2,1)} %broadcast_select_fusion.14), calls=%async_computation.2 | async-start | bytes 2097152 | tf_op jit(solution)/shard_map/all_to_all | solution.py:50
  154.8 40.5 %collective-permute-start.3 = (bf16[1024,512]{1,0:T(8,128)(2,1)}, bf16[1024,512]{1,0:T(8,128)(2,1)}, u32[]{:S(2)}, u32[]{:S(2)}) collective-permute-start(bf16[1024,512]{1,0:T(8,128)(2,1)} %bitcast.6), channel_id=1, source_target_pairs={{0,16},{8,24},{1,17},{9,25},{2,18},{10,26},{3,19},{11,27},{4,20},{... | collective-permute-start | bytes 3145736 | tf_op jit(solution)/shard_map/ppermute | solution.py:17
  183.0 12.3 %copy-start.2 = (bf16[3,1024,512]{2,1,0:T(8,128)(2,1)S(1)}, bf16[3,1024,512]{2,1,0:T(8,128)(2,1)}, u32[]{:S(2)}) copy-start(bf16[3,1024,512]{2,1,0:T(8,128)(2,1)} %param.14) | copy-start | bytes 9437188
  196.8 18.6 %copy-start.10 = (bf16[1024,512]{1,0:T(8,128)(2,1)}, bf16[1024,512]{1,0:T(8,128)(2,1)S(1)}, u32[]{:S(2)}) copy-start(bf16[1024,512]{1,0:T(8,128)(2,1)S(1)} %maximum_convert_fusion.1) | copy-start | bytes 3145732
  196.8 18.4 %collective-permute-start.4 = (bf16[1024,512]{1,0:T(8,128)(2,1)S(1)}, bf16[1024,512]{1,0:T(8,128)(2,1)S(1)}, u32[]{:S(2)}, u32[]{:S(2)}) collective-permute-start(bf16[1024,512]{1,0:T(8,128)(2,1)S(1)} %maximum_convert_fusion.1), channel_id=1, source_target_pairs={{0,8},{8,16},{16,24},{1,9},{9,17},{17,25},{2,10},{10,18},{18,26},{... | collective-permute-start | bytes 3145736 | tf_op jit(solution)/shard_map/ppermute | solution.py:17
  215.3 1.8 copy-start.3
  217.1 19.2 %all-to-all-start.3 = ((bf16[8,128,512]{2,1,0:T(8,128)(2,1)}), bf16[8,128,512]{2,1,0:T(8,128)(2,1)}, u32[]{:S(2)}, u32[]{:S(2)}) async-start(bf16[8,128,512]{2,1,0:T(8,128)(2,1)} %broadcast_select_fusion.13), calls=%async_computation.3 | async-start | bytes 2097152 | tf_op jit(solution)/shard_map/all_to_all | solution.py:50
  221.3 40.0 %collective-permute-start.5 = (bf16[1024,512]{1,0:T(8,128)(2,1)}, bf16[1024,512]{1,0:T(8,128)(2,1)}, u32[]{:S(2)}, u32[]{:S(2)}) collective-permute-start(bf16[1024,512]{1,0:T(8,128)(2,1)} %bitcast.6), channel_id=1, source_target_pairs={{0,24},{1,25},{2,26},{3,27},{4,28},{5,29},{6,30},{7,31}} | collective-permute-start | bytes 3145736 | tf_op jit(solution)/shard_map/ppermute | solution.py:17
  263.3 1.2 copy-start.7
  263.3 1.5 copy-start.9
  263.3 1.8 copy-start.11
where the time goes:
time: 269 us; the launch traced here: 267 us
  waiting for transfers between devices  94.5 us (35%)
  matrix products  53.3 us (20%)
  local copies, waits for them, and re-layouts  49.7 us (18%)
  starting transfers between devices  44.2 us (16%)
  other arithmetic  25.3 us (9%)
    all_to_all x4, waiting for transfers between devices, body(): lax.all_to_all(outgoing, 'dom', split_axis=0, concat_axis=0, tiled=True)  59.3 us
    dot_general x4, matrix products, body(): jnp.einsum('rkij,rkjd->rid', masked_adj, picked, preferred_element_type=j...  50.2 us
    gather x4, local copies, waits for them, and re-layouts, body(): picked = jnp.take(lookup, col_index, axis=0)  44.8 us
    ppermute x6, waiting for transfers between devices, shifted_2(): return lax.ppermute(value, axis, pairs)  35.2 us
    ppermute x6, starting transfers between devices, shifted_2(): return lax.ppermute(value, axis, pairs)  25.1 us
    all_to_all x4, starting transfers between devices, body(): lax.all_to_all(outgoing, 'dom', split_axis=0, concat_axis=0, tiled=True)  19.1 us
    concatenate x4, other arithmetic, body(): lookup = jnp.concatenate([own_blocks, incoming], axis=0)  6.89 us
    convert_element_type x4, other arithmetic, body(): ((1.0 - teleport) * gathered + teleport * anchor.astype(jnp.float32)).ast...  6.32 us
  transfers between devices with their start and end apart: 10, of which 7 were waited for; matrix products, arithmetic and copies ran while one was open for 29% of the time, Pallas kernels for 0%

commit v1 on v0

v1 whole, which is shorter than its diff:
```python
import jax
import jax.numpy as jnp
from jax import lax
from jax.experimental import pallas as pl
from jax.experimental.pallas import tpu as pltpu
from jax.sharding import PartitionSpec as P

STEPS = 4
TILE = 256

teleport = 0.2
strength = 1.5

VMEM = pl.BlockSpec(memory_space=pltpu.VMEM)
SMEM = pl.BlockSpec(memory_space=pltpu.SMEM)
ANY = pl.BlockSpec(memory_space=pl.ANY)
LIMIT = pltpu.CompilerParams(vmem_limit_bytes=24 * 2**20)


def send_kernel(ids, blocks, outgoing, sems):
    copies = [
        pltpu.make_async_copy(blocks.at[ids[q]], outgoing.at[q], sems.at[q])
        for q in range(outgoing.shape[0])
    ]
    for copy in copies:
        copy.start()
    for copy in copies:
        copy.wait()


def first_outgoing(ids, blocks):
    return pl.pallas_call(
        send_kernel,
        out_shape=jax.ShapeDtypeStruct((ids.shape[0],) + blocks.shape[1:], blocks.dtype),
        in_specs=[SMEM, ANY],
        out_specs=ANY,
        scratch_shapes=[pltpu.SemaphoreType.DMA((ids.shape[0],))],
    )(ids, blocks)


def merge_kernel(col, counts, adj, own, other, total):
    row = pl.program_id(0)
    block = adj.shape[-1]
    total[...] = jnp.zeros_like(total)

    def add(k, carry):
        total[col[row, k]] += adj[0, k].astype(jnp.float32)
        return carry

    lax.fori_loop(0, counts[row], add, 0)
    mine = own.shape[1] // block
    for entry in range(total.shape[0]):
        value = total[entry].astype(own.dtype)
        if entry < mine:
            own[:, entry * block : (entry + 1) * block] = value
        else:
            at = (entry - mine) * block
            other[:, at : at + block] = value


def merged(col, counts, adj, table):
    rows, slots, block, _ = adj.shape
    return pl.pallas_call(
        merge_kernel,
        grid=(rows,),
        out_shape=[
            jax.ShapeDtypeStruct((rows * block, rows * block), adj.dtype),
            jax.ShapeDtypeStruct((rows * block, (table - rows) * block), adj.dtype),
        ],
        in_specs=[SMEM, SMEM, pl.BlockSpec((1, slots, block, block), lambda r: (r, 0, 0, 0))],
        out_specs=[
            pl.BlockSpec((block, rows * block), lambda r: (r, 0)),
            pl.BlockSpec((block, (table - rows) * block), lambda r: (r, 0)),
        ],
        scratch_shapes=[pltpu.VMEM((table, block, block), jnp.float32)],
        compiler_params=LIMIT,
    )(col, counts, adj)


def own_kernel(flags, current, fresh, carried, new_h0, adj, partial, x, h0, sems):
    def pull(source, target, sem):
        copy = pltpu.make_async_copy(source, target, sem)
        copy.start()
        copy.wait()

    @pl.when(flags[0] == 1)
    def _():
        pull(fresh, x, sems.at[0])

    @pl.when(flags[0] == 0)
    def _():
        pull(current, x, sems.at[0])

    @pl.when(flags[1] == 1)
    def _():
        pull(new_h0.at[flags[2]], h0, sems.at[1])

    @pl.when(flags[1] == 0)
    def _():
        pull(carried, h0, sems.at[1])

    for at in range(0, x.shape[0], TILE):
        rows = slice(at, at + TILE)
        agg = jnp.dot(adj[rows], x[...], preferred_element_type=jnp.float32)
        partial[rows] = (1.0 - teleport) * agg + teleport * h0[rows].astype(jnp.float32)


def own_part(flags, current, fresh, carried, new_h0, adj):
    return pl.pallas_call(
        own_kernel,
        out_shape=jax.ShapeDtypeStruct(current.shape, jnp.float32),
        in_specs=[SMEM, ANY, ANY, ANY, ANY, VMEM],
        out_specs=VMEM,
        scratch_shapes=[
            pltpu.VMEM(current.shape, current.dtype),
            pltpu.VMEM(current.shape, current.dtype),
            pltpu.SemaphoreType.DMA((2,)),
        ],
        compiler_params=LIMIT,
    )(flags, current, fresh, carried, new_h0, adj)


def layer_kernel(last, flags, ids, beta, incoming, adj, partial, weight, fresh, *rest):
    out = rest[0]
    for at in range(0, out.shape[0], TILE):
        rows = slice(at, at + TILE)
        agg = jnp.dot(adj[rows], incoming[...], preferred_element_type=jnp.float32)
        mixture = (partial[rows] + (1.0 - teleport) * agg).astype(jnp.bfloat16)
        product = jnp.dot(mixture, weight[...], preferred_element_type=jnp.float32)
        value = (1.0 - beta[0]) * mixture.astype(jnp.float32) + beta[0] * product
        out[rows] = jnp.maximum(value, 0.0).astype(out.dtype)
    if last:
        return
    outgoing, sems = rest[1:]
    block = outgoing.shape[1]

    def send(source):
        copies = [
            pltpu.make_async_copy(
                source.at[pl.ds(pl.multiple_of(ids[q] * block, block), block)], outgoing.at[q], sems.at[q]
            )
            for q in range(outgoing.shape[0])
        ]
        for copy in copies:
            copy.start()
        for copy in copies:
            copy.wait()

    @pl.when(flags[0] == 1)
    def _():
        send(fresh)

    @pl.when(flags[0] == 0)
    def _():
        send(out)


def layer(last, flags, ids, beta, incoming, adj, partial, weight, fresh):
    parts, block, width = incoming.shape
    shapes = [jax.ShapeDtypeStruct(partial.shape, incoming.dtype)]
    if not last:
        shapes.append(jax.ShapeDtypeStruct(incoming.shape, incoming.dtype))
    return pl.pallas_call(
        lambda *refs: layer_kernel(last, *refs),
        out_shape=shapes,
        in_specs=[SMEM, SMEM, SMEM, VMEM, VMEM, VMEM, VMEM, ANY],
        out_specs=[VMEM, ANY][: len(shapes)],
        scratch_shapes=[] if last else [pltpu.SemaphoreType.DMA((parts,))],
        compiler_params=LIMIT,
    )(flags, ids, beta, incoming.reshape(parts * block, width), adj, partial, weight, fresh)


def moved(value, by):
    length = lax.axis_size("section")
    if by % length == 0:
        return value
    return lax.ppermute(value, "section", [((i + by) % length, i) for i in range(length)])


def body(carry_h, carry_h0, new_h0, weights, adj_blocks, col_index, counts, send_list):
    section = lax.axis_index("section")
    sections = lax.axis_size("section")
    row_count, width = carry_h.shape[1:]
    block_count, _, block, _ = adj_blocks.shape
    parts = send_list.shape[0]
    ids = lax.dynamic_index_in_dim(send_list, lax.axis_index("dom"), 0, keepdims=False)
    layers = (section + jnp.arange(STEPS + 1, dtype=jnp.int32)) % sections
    betas = jnp.log(1.0 + strength / (layers.astype(jnp.float32) + 1.0))
    wrapped = (section + jnp.arange(STEPS + 1, dtype=jnp.int32) >= sections).astype(jnp.int32)
    starts = (layers == 0).astype(jnp.int32).at[0].set(0)
    source = jnp.clip(sections - section - 1, 0, new_h0.shape[0] - 1)
    flags = [jnp.stack([starts[t], wrapped[t], source]) for t in range(STEPS + 1)]

    outgoing = first_outgoing(ids, carry_h[0].reshape(block_count, block, width))
    current = carry_h[0]
    layer_weights = [moved(weights[0], t) for t in range(STEPS)]
    own_adj = None
    results = []
    for t in range(STEPS):
        last = t == STEPS - 1
        incoming = lax.all_to_all(outgoing, "dom", split_axis=0, concat_axis=0, tiled=True)
        if own_adj is None:
            own_adj, other_adj = merged(col_index, counts, adj_blocks, block_count + parts)
        partial = own_part(flags[t], current, new_h0[max(t - 1, 0)], carry_h0[0], new_h0, own_adj)
        made = layer(
            last, flags[t + 1], ids, betas[t : t + 1], incoming, other_adj, partial, layer_weights[t],
            new_h0[min(t, new_h0.shape[0] - 1)],
        )
        current = made[0]
        if not last:
            outgoing = made[1]
        results.append(moved(current, -t))
    return jnp.stack(results)[None]


def solution(mesh):
    in_specs = (
        P("section", "dom", None),
        P("section", "dom", None),
        P(None, "dom", None),
        P("section", None, None),
        P("dom", None, None, None),
        P("dom", None),
        P("dom"),
        P(),
    )
    out_specs = P("section", None, "dom", None)
    return jax.shard_map(body, mesh=mesh, in_specs=in_specs, out_specs=out_specs, check_vma=False)
```

time: 269 us -> 229 us (0.85)
  Pallas kernels: 0 us -> 67.1 us
  matrix products: 53.3 us -> 0 us
  waiting for transfers between devices: 94.5 us -> 60.8 us
  other arithmetic: 25.3 us -> 10.4 us
  starting transfers between devices: 44.2 us -> 31.1 us
  local copies, waits for them, and re-layouts: 49.7 us -> 58 us
    pallas_call x0 -> x10, Pallas kernels: none -> 67.1 us  [the longest x1 33.6 us: first_outgoing(): pl.pallas_call(send_kernel, out_shape=jax.ShapeDtypeStruct((ids.shape[0],...]
    dot_general x8 -> x0, matrix products: 53.3 us -> none  [the longest x4 50.2 us: body(): jnp.einsum('rkij,rkjd->rid', masked_adj, picked, preferred_element_type=j...]
    unnamed x30 -> x100, local copies, waits for them, and re-layouts: 1.11 us -> 53.8 us
    gather x8 -> x0, local copies, waits for them, and re-layouts: 48.5 us -> none  [the longest x4 44.8 us: body(): picked = jnp.take(lookup, col_index, axis=0)]
    all_to_all x4, waiting for transfers between devices: 59.3 us -> 41.9 us  [body(): lax.all_to_all(outgoing, 'dom', split_axis=0, concat_axis=0, tiled=True)]
    ppermute x6, waiting for transfers between devices: 35.2 us -> 18.9 us  [moved(): lax.ppermute(value, 'section', [((i + by) % length, i) for i in range(len...]
    ppermute x6, starting transfers between devices: 25.1 us -> 9.5 us  [moved(): lax.ppermute(value, 'section', [((i + by) % length, i) for i in range(len...]
    concatenate x4 -> x0, other arithmetic: 6.89 us -> none  [body(): lookup = jnp.concatenate([own_blocks, incoming], axis=0)]
  transfers between devices with their start and end apart: 10 -> 10, of which waited for: 7 -> 7; matrix products, arithmetic and copies ran while one was open for 29% -> 5% of each run, Pallas kernels for 0% -> 7%
where the time goes in v1:
time: 229 us; the launch traced here: 228 us
  Pallas kernels  67.1 us (29%)
  waiting for transfers between devices  60.8 us (27%)
  local copies, waits for them, and re-layouts  58 us (25%)
  starting transfers between devices  31.1 us (14%)
  other arithmetic  10.4 us (5%)
    unnamed x100, local copies, waits for them, and re-layouts  53.8 us
    all_to_all x4, waiting for transfers between devices, body(): lax.all_to_all(outgoing, 'dom', split_axis=0, concat_axis=0, tiled=True)  41.9 us
    pallas_call x1, Pallas kernels, first_outgoing(): pl.pallas_call(send_kernel, out_shape=jax.ShapeDtypeStruct((ids.shape[0],...  33.6 us
    all_to_all x4, starting transfers between devices, body(): lax.all_to_all(outgoing, 'dom', split_axis=0, concat_axis=0, tiled=True)  21.6 us
    pallas_call x4, Pallas kernels, layer(): pl.pallas_call(lambda *refs: layer_kernel(last, *refs), out_shape=shapes,...  21.4 us
    ppermute x6, waiting for transfers between devices, moved(): lax.ppermute(value, 'section', [((i + by) % length, i) for i in range(len...  18.9 us
    ppermute x6, starting transfers between devices, moved(): lax.ppermute(value, 'section', [((i + by) % length, i) for i in range(len...  9.5 us
    pallas_call x4, Pallas kernels, own_part(): pl.pallas_call(own_kernel, out_shape=jax.ShapeDtypeStruct(current.shape,...  8.5 us
  transfers between devices with their start and end apart: 10, of which 7 were waited for; matrix products, arithmetic and copies ran while one was open for 5% of the time, Pallas kernels for 7%

profile of v1, /device:TPU:1, one launch (start us, length us, event | category | flops | bytes accessed | tf_op | source)
XLA Modules:
  0.0 227.7 jit_solution(14817530303365828776)
XLA Ops:
  1.3 33.6 %shard_map.82 = bf16[8,128,512]{2,1,0:T(8,128)(2,1)} custom-call(s32[8]{0:T(128)} %dynamic-slice_bitcast_fusion.ids.refs_1_, bf16[8,128,512]{2,1,0:T(8,128)(2,1)} %bitcast.27), custom_call_target="tpu_custom_call" | custom-call | tf_op jit(solution)/shard_map/pallas_call | solution.py:32
  34.9 6.6 %all-to-all-start = ((bf16[8,128,512]{2,1,0:T(8,128)(2,1)}), bf16[8,128,512]{2,1,0:T(8,128)(2,1)}, u32[]{:S(2)}, u32[]{:S(2)}) async-start(bf16[8,128,512]{2,1,0:T(8,128)(2,1)} %shard_map.82), calls=%async_computation | async-start | bytes 2097152 | tf_op jit(solution)/shard_map/all_to_all | solution.py:201
  41.5 2.8 %copy-done.31 = bf16[8,24,128,128]{3,2,1,0:T(8,128)(2,1)S(1)} copy-done((bf16[8,24,128,128]{3,2,1,0:T(8,128)(2,1)S(1)}, bf16[8,24,128,128]{3,2,1,0:T(8,128)(2,1)}, u32[]{:S(2)}) %copy-start.31) | copy-done | bytes 6291480
  44.3 3.6 %shard_map.83 = (bf16[1024,1024]{1,0:T(8,128)(2,1)S(1)}, bf16[1024,1024]{1,0:T(8,128)(2,1)S(1)}) custom-call(s32[8,24]{1,0:T(8,128)S(1)} %copy-done.48, s32[8]{0:T(128)S(1)} %copy-done.49, bf16[8,24,128,128]{3,2,1,0:T(8,128)(2,1)S(1)} %copy-done.31), custom_call_target="tpu_custom_call" | custom-call | tf_op jit(solution)/shard_map/pallas_call | solution.py:63
  52.9 2.1 shard_map.84.refs_5_
  59.0 7.2 %all-to-all-done = bf16[8,128,512]{2,1,0:T(8,128)(2,1)} async-done(((bf16[8,128,512]{2,1,0:T(8,128)(2,1)}), bf16[8,128,512]{2,1,0:T(8,128)(2,1)}, u32[]{:S(2)}, u32[]{:S(2)}) %all-to-all-start) | async-done | bytes 1048608 | tf_op jit(solution)/shard_map/all_to_all | solution.py:201
  66.2 1.6 copy-done.3
  71.7 5.4 %shard_map.85 = (bf16[1024,512]{1,0:T(8,128)(2,1)S(1)}, bf16[8,128,512]{2,1,0:T(8,128)(2,1)S(1)}) custom-call(s32[3]{0:T(128)S(1)} %add_add_fusion.refs_0_.flags, s32[8]{0:T(128)S(1)} %copy-done.47, f32[1]{0:T(128)} %get-tuple-element.41.refs_2_, bf16[1024,512]{1,0:T(8,128)(2,1)} %bitcast.3.refs_3_, bf16[1024,1024]{1,0:T(8,128)(2,1)S(1)} %copy-done.3, ...), custom_call_target="tpu_custom_call" | custom-call | tf_op jit(solution)/shard_map/pallas_call | solution.py:163
  79.1 4.9 %all-to-all-start.1 = ((bf16[8,128,512]{2,1,0:T(8,128)(2,1)}), bf16[8,128,512]{2,1,0:T(8,128)(2,1)}, u32[]{:S(2)}, u32[]{:S(2)}) async-start(bf16[8,128,512]{2,1,0:T(8,128)(2,1)} %copy-done.37), calls=%async_computation.1 | async-start | bytes 2097152 | tf_op jit(solution)/shard_map/all_to_all | solution.py:201
  87.0 1.6 copy-done.8
  92.2 2.1 shard_map.86.refs_5_
  96.5 12.3 %all-to-all-done.1 = bf16[8,128,512]{2,1,0:T(8,128)(2,1)} async-done(((bf16[8,128,512]{2,1,0:T(8,128)(2,1)}), bf16[8,128,512]{2,1,0:T(8,128)(2,1)}, u32[]{:S(2)}, u32[]{:S(2)}) %all-to-all-start.1) | async-done | bytes 1048608 | tf_op jit(solution)/shard_map/all_to_all | solution.py:201
  108.8 1.6 copy-done.4
  114.2 5.5 %shard_map.87 = (bf16[1024,512]{1,0:T(8,128)(2,1)S(1)}, bf16[8,128,512]{2,1,0:T(8,128)(2,1)S(1)}) custom-call(s32[3]{0:T(128)S(1)} %add_add_fusion.2.refs_0_.flags, s32[8]{0:T(128)S(1)} %copy-done.47, f32[1]{0:T(128)} %get-tuple-element.44.refs_2_, bf16[1024,512]{1,0:T(8,128)(2,1)} %bitcast.9.refs_3_, bf16[1024,1024]{1,0:T(8,128)(2,1)S(1)} %copy-done.4, ...), custom_call_target="tpu_custom_call" | custom-call | tf_op jit(solution)/shard_map/pallas_call | solution.py:163
  121.8 4.9 %all-to-all-start.2 = ((bf16[8,128,512]{2,1,0:T(8,128)(2,1)}), bf16[8,128,512]{2,1,0:T(8,128)(2,1)}, u32[]{:S(2)}, u32[]{:S(2)}) async-start(bf16[8,128,512]{2,1,0:T(8,128)(2,1)} %copy-done.36), calls=%async_computation.2 | async-start | bytes 2097152 | tf_op jit(solution)/shard_map/all_to_all | solution.py:201
  129.3 1.6 copy-done.9
  134.6 2.1 shard_map.88.refs_5_
  139.5 11.8 %all-to-all-done.2 = bf16[8,128,512]{2,1,0:T(8,128)(2,1)} async-done(((bf16[8,128,512]{2,1,0:T(8,128)(2,1)}), bf16[8,128,512]{2,1,0:T(8,128)(2,1)}, u32[]{:S(2)}, u32[]{:S(2)}) %all-to-all-start.2) | async-done | bytes 1048608 | tf_op jit(solution)/shard_map/all_to_all | solution.py:201
  151.3 1.6 copy-done.5
  154.1 1.6 copy-done.26
  156.7 6.5 %shard_map.89 = (bf16[1024,512]{1,0:T(8,128)(2,1)}, bf16[8,128,512]{2,1,0:T(8,128)(2,1)S(1)}) custom-call(s32[3]{0:T(128)S(1)} %add_add_fusion.3.refs_0_.flags, s32[8]{0:T(128)S(1)} %copy-done.47, f32[1]{0:T(128)} %get-tuple-element.43.refs_2_, bf16[1024,512]{1,0:T(8,128)(2,1)} %bitcast.12.refs_3_, bf16[1024,1024]{1,0:T(8,128)(2,1)S(1)} %copy-done.5, ...), custom_call_target="tpu_custom_call" | custom-call | tf_op jit(solution)/shard_map/pallas_call | solution.py:163
  164.2 5.1 %all-to-all-start.3 = ((bf16[8,128,512]{2,1,0:T(8,128)(2,1)}), bf16[8,128,512]{2,1,0:T(8,128)(2,1)}, u32[]{:S(2)}, u32[]{:S(2)}) async-start(bf16[8,128,512]{2,1,0:T(8,128)(2,1)} %copy-done.35), calls=%async_computation.3 | async-start | bytes 2097152 | tf_op jit(solution)/shard_map/all_to_all | solution.py:201
  169.3 2.8 %collective-permute-start.4 = (bf16[512,512]{1,0:T(8,128)(2,1)}, bf16[512,512]{1,0:T(8,128)(2,1)S(1)}, u32[]{:S(2)}, u32[]{:S(2)}) collective-permute-start(bf16[512,512]{1,0:T(8,128)(2,1)} %bitcast.32), channel_id=1, source_target_pairs={{24,0},{0,8},{8,16},{16,24},{25,1},{1,9},{9,17},{17,25},{26,2},{2,... | collective-permute-start | bytes 1572872 | tf_op jit(solution)/shard_map/ppermute | solution.py:177
  177.4 2.3 shard_map.90.refs_5_
  183.2 10.6 %all-to-all-done.3 = bf16[8,128,512]{2,1,0:T(8,128)(2,1)} async-done(((bf16[8,128,512]{2,1,0:T(8,128)(2,1)}), bf16[8,128,512]{2,1,0:T(8,128)(2,1)}, u32[]{:S(2)}, u32[]{:S(2)}) %all-to-all-start.3) | async-done | bytes 1048608 | tf_op jit(solution)/shard_map/all_to_all | solution.py:201
  193.8 1.6 copy-done.6
  196.7 1.6 copy-done.30
  199.3 4.0 %shard_map.91 = bf16[1024,512]{1,0:T(8,128)(2,1)S(1)} custom-call(s32[3]{0:T(128)S(1)} %add_add_fusion.4.refs_0_, s32[8]{0:T(128)S(1)} %copy-done.47, f32[1]{0:T(128)} %get-tuple-element.42.refs_2_, bf16[1024,512]{1,0:T(8,128)(2,1)} %bitcast.15.refs_3_, bf16[1024,1024]{1,0:T(8,128)(2,1)S(1)} %copy-done.6, f32[1024,512]{1,0:T(8,128)S(1)} %copy-done.30, ...), custom_call_target="tpu_custom_call" | custom-call | tf_op jit(solution)/shard_map/pallas_call | solution.py:163
  203.3 2.6 %collective-permute-start.5 = (bf16[1024,512]{1,0:T(8,128)(2,1)S(1)}, bf16[1024,512]{1,0:T(8,128)(2,1)S(1)}, u32[]{:S(2)}, u32[]{:S(2)}) collective-permute-start(bf16[1024,512]{1,0:T(8,128)(2,1)S(1)} %shard_map.91), channel_id=1, source_target_pairs={{8,0},{16,8},{24,16},{0,24},{9,1},{17,9},{25,17},{1,25},{10,2},{18... | collective-permute-start | bytes 3145736 | tf_op jit(solution)/shard_map/ppermute | solution.py:177
  205.8 12.0 %collective-permute-done.3 = bf16[1024,512]{1,0:T(8,128)(2,1)} collective-permute-done((bf16[1024,512]{1,0:T(8,128)(2,1)}, bf16[1024,512]{1,0:T(8,128)(2,1)}, u32[]{:S(2)}, u32[]{:S(2)}) %collective-permute-start.3) | collective-permute-done | bytes 1048608 | tf_op jit(solution)/shard_map/ppermute | solution.py:177
  217.8 6.3 %collective-permute-done.5 = bf16[1024,512]{1,0:T(8,128)(2,1)S(1)} collective-permute-done((bf16[1024,512]{1,0:T(8,128)(2,1)S(1)}, bf16[1024,512]{1,0:T(8,128)(2,1)S(1)}, u32[]{:S(2)}, u32[]{:S(2)}) %collective-permute-start.5) | collective-permute-done | bytes 1048608 | tf_op jit(solution)/shard_map/ppermute | solution.py:177
  224.1 3.6 %maximum_bitcast_fusion = bf16[1,4,1024,512]{3,2,1,0:T(8,128)(2,1)} fusion(bf16[1,1024,512]{2,1,0:T(8,128)(2,1)S(1)} %bitcast.34, bf16[1,1024,512]{2,1,0:T(8,128)(2,1)} %bitcast.14, bf16[1,1024,512]{2,1,0:T(8,128)(2,1)} %bitcast.11, bf16[1,1024,512]{2,1,0:T(8,128)(2,1)} %bitcast.29), kind=kLoop, calls=%fused_computation | loop fusion | flops 6291456 | bytes 8388608 | tf_op jit(solution)/shard_map/broadcast_in_dim | solution.py:213
  (111 shorter events, 54.1 us)
Async XLA Ops:
  0.0 41.5 %copy-start.48 = (s32[8,24]{1,0:T(8,128)S(1)}, s32[8,24]{1,0:T(8,128)}, u32[]{:S(2)}) copy-start(s32[8,24]{1,0:T(8,128)} %col.1) | copy-start | bytes 2308
  0.0 41.5 %copy-start.49 = (s32[8]{0:T(128)S(1)}, s32[8]{0:T(128)}, u32[]{:S(2)}) copy-start(s32[8]{0:T(128)} %counts.1) | copy-start | bytes 100
  34.9 16.5 %copy-start.1 = (bf16[3,1024,512]{2,1,0:T(8,128)(2,1)S(1)}, bf16[3,1024,512]{2,1,0:T(8,128)(2,1)}, u32[]{:S(2)}) copy-start(bf16[3,1024,512]{2,1,0:T(8,128)(2,1)} %new_h0.7) | copy-start | bytes 9437188
  34.9 31.3 %all-to-all-start = ((bf16[8,128,512]{2,1,0:T(8,128)(2,1)}), bf16[8,128,512]{2,1,0:T(8,128)(2,1)}, u32[]{:S(2)}, u32[]{:S(2)}) async-start(bf16[8,128,512]{2,1,0:T(8,128)(2,1)} %shard_map.82), calls=%async_computation | async-start | bytes 2097152 | tf_op jit(solution)/shard_map/all_to_all | solution.py:201
  41.5 2.8 %copy-start.31 = (bf16[8,24,128,128]{3,2,1,0:T(8,128)(2,1)S(1)}, bf16[8,24,128,128]{3,2,1,0:T(8,128)(2,1)}, u32[]{:S(2)}) copy-start(bf16[8,24,128,128]{3,2,1,0:T(8,128)(2,1)} %adj.1) | copy-start | bytes 18874372
  49.2 5.7 %copy-start.7 = (bf16[1024,1024]{1,0:T(8,128)(2,1)}, bf16[1024,1024]{1,0:T(8,128)(2,1)S(1)}, u32[]{:S(2)}) copy-start(bf16[1024,1024]{1,0:T(8,128)(2,1)S(1)} %get-tuple-element.26.adj) | copy-start | bytes 6291460
  49.2 3.7 %copy-start.17 = (bf16[1,1024,512]{2,1,0:T(8,128)(2,1)S(1)}, bf16[1,1024,512]{2,1,0:T(8,128)(2,1)}, u32[]{:S(2)}) copy-start(bf16[1,1024,512]{2,1,0:T(8,128)(2,1)} %param.11) | copy-start | bytes 3145732
  49.2 3.7 %copy-start.32 = (bf16[1,1024,512]{2,1,0:T(8,128)(2,1)S(1)}, bf16[1,1024,512]{2,1,0:T(8,128)(2,1)}, u32[]{:S(2)}) copy-start(bf16[1,1024,512]{2,1,0:T(8,128)(2,1)} %param.10) | copy-start | bytes 3145732
  52.9 2.1 copy-start.14
  52.9 13.3 %copy-start.47 = (s32[8]{0:T(128)S(1)}, s32[8]{0:T(128)}, u32[]{:S(2)}) copy-start(s32[8]{0:T(128)} %dynamic-slice_bitcast_fusion.ids.refs_1_) | copy-start | bytes 100
  55.0 1.3 copy-start.23
  66.2 1.6 copy-start.3
  69.0 1.6 copy-start.24
  79.1 29.7 %all-to-all-start.1 = ((bf16[8,128,512]{2,1,0:T(8,128)(2,1)}), bf16[8,128,512]{2,1,0:T(8,128)(2,1)}, u32[]{:S(2)}, u32[]{:S(2)}) async-start(bf16[8,128,512]{2,1,0:T(8,128)(2,1)} %copy-done.37), calls=%async_computation.1 | async-start | bytes 2097152 | tf_op jit(solution)/shard_map/all_to_all | solution.py:201
  84.0 11.6 %collective-permute-start = (bf16[512,512]{1,0:T(8,128)(2,1)}, bf16[512,512]{1,0:T(8,128)(2,1)S(1)}, u32[]{:S(2)}, u32[]{:S(2)}) collective-permute-start(bf16[512,512]{1,0:T(8,128)(2,1)} %bitcast.30), channel_id=1, source_target_pairs={{8,0},{16,8},{24,16},{0,24},{9,1},{17,9},{25,17},{1,25},{10,2},{18... | collective-permute-start | bytes 1572872 | tf_op jit(solution)/shard_map/ppermute | solution.py:177
  86.9 1.6 copy-start.8
  108.8 1.6 copy-start.4
  111.6 1.6 copy-start.28
  121.8 29.4 %all-to-all-start.2 = ((bf16[8,128,512]{2,1,0:T(8,128)(2,1)}), bf16[8,128,512]{2,1,0:T(8,128)(2,1)}, u32[]{:S(2)}, u32[]{:S(2)}) async-start(bf16[8,128,512]{2,1,0:T(8,128)(2,1)} %copy-done.36), calls=%async_computation.2 | async-start | bytes 2097152 | tf_op jit(solution)/shard_map/all_to_all | solution.py:201
  126.7 12.0 %collective-permute-start.2 = (bf16[512,512]{1,0:T(8,128)(2,1)}, bf16[512,512]{1,0:T(8,128)(2,1)S(1)}, u32[]{:S(2)}, u32[]{:S(2)}) collective-permute-start(bf16[512,512]{1,0:T(8,128)(2,1)} %bitcast.31), channel_id=1, source_target_pairs={{16,0},{24,8},{0,16},{8,24},{17,1},{25,9},{1,17},{9,25},{18,2},{26... | collective-permute-start | bytes 1572872 | tf_op jit(solution)/shard_map/ppermute | solution.py:177
  129.3 1.6 copy-start.9
  136.7 1.3 copy-start.25
  151.2 1.6 copy-start.5
  154.1 1.6 copy-start.26
  164.2 29.6 %all-to-all-start.3 = ((bf16[8,128,512]{2,1,0:T(8,128)(2,1)}), bf16[8,128,512]{2,1,0:T(8,128)(2,1)}, u32[]{:S(2)}, u32[]{:S(2)}) async-start(bf16[8,128,512]{2,1,0:T(8,128)(2,1)} %copy-done.35), calls=%async_computation.3 | async-start | bytes 2097152 | tf_op jit(solution)/shard_map/all_to_all | solution.py:201
  169.3 13.1 %collective-permute-start.4 = (bf16[512,512]{1,0:T(8,128)(2,1)}, bf16[512,512]{1,0:T(8,128)(2,1)S(1)}, u32[]{:S(2)}, u32[]{:S(2)}) collective-permute-start(bf16[512,512]{1,0:T(8,128)(2,1)} %bitcast.32), channel_id=1, source_target_pairs={{24,0},{0,8},{8,16},{16,24},{25,1},{1,9},{9,17},{17,25},{26,2},{2,... | collective-permute-start | bytes 1572872 | tf_op jit(solution)/shard_map/ppermute | solution.py:177
  173.4 32.5 %collective-permute-start.1 = (bf16[1024,512]{1,0:T(8,128)(2,1)}, bf16[1024,512]{1,0:T(8,128)(2,1)}, u32[]{:S(2)}, u32[]{:S(2)}) collective-permute-start(bf16[1024,512]{1,0:T(8,128)(2,1)} %copy-done.38), channel_id=1, source_target_pairs={{24,0},{0,8},{8,16},{16,24},{25,1},{1,9},{9,17},{17,25},{26,2},{2,... | collective-permute-start | bytes 3145736 | tf_op jit(solution)/shard_map/ppermute | solution.py:177
  173.4 1.6 copy-start.10
  181.0 36.8 %collective-permute-start.3 = (bf16[1024,512]{1,0:T(8,128)(2,1)}, bf16[1024,512]{1,0:T(8,128)(2,1)}, u32[]{:S(2)}, u32[]{:S(2)}) collective-permute-start(bf16[1024,512]{1,0:T(8,128)(2,1)} %get-tuple-element.31.current), channel_id=1, source_target_pairs={{16,0},{24,8},{0,16},{8,24},{17,1},{25,9},{1,17},{9,25},{18,2},{26... | collective-permute-start | bytes 3145736 | tf_op jit(solution)/shard_map/ppermute | solution.py:177
  193.8 1.6 copy-start.6
  196.7 1.6 copy-start.30
  203.3 20.8 %collective-permute-start.5 = (bf16[1024,512]{1,0:T(8,128)(2,1)S(1)}, bf16[1024,512]{1,0:T(8,128)(2,1)S(1)}, u32[]{:S(2)}, u32[]{:S(2)}) collective-permute-start(bf16[1024,512]{1,0:T(8,128)(2,1)S(1)} %shard_map.91), channel_id=1, source_target_pairs={{8,0},{16,8},{24,16},{0,24},{9,1},{17,9},{25,17},{1,25},{10,2},{18... | collective-permute-start | bytes 3145736 | tf_op jit(solution)/shard_map/ppermute | solution.py:177
  (28 other events, 30.9 us)

commit v2 on v0

v2 whole, which is shorter than its diff:
```python
import jax
import jax.numpy as jnp
from jax import lax
from jax.experimental import pallas as pl
from jax.experimental.pallas import tpu as pltpu
from jax.sharding import PartitionSpec as P

STEPS = 4
TILE = 256

teleport = 0.2
strength = 1.5

PART, SOURCE, STARTS, WRAPPED, IDS = 0, 1, 2, 2 + STEPS, 2 + 2 * STEPS

VMEM = pl.BlockSpec(memory_space=pltpu.VMEM)
SMEM = pl.BlockSpec(memory_space=pltpu.SMEM)
HBM = pl.BlockSpec(memory_space=pltpu.HBM)
LIMIT = pltpu.CompilerParams(vmem_limit_bytes=16 * 2**20)


def fast(value):
    return pltpu.with_memory_space_constraint(value, pltpu.VMEM)


def far(value):
    return pltpu.with_memory_space_constraint(value, pltpu.HBM)


def run(copies):
    for copy in copies:
        copy.start()
    for copy in copies:
        copy.wait()


def relays(parts):
    quarter = parts // 4
    if quarter == 0:
        return {}
    hops = {}
    for k in range(2 * quarter, 3 * quarter):
        across = k - 2 * quarter
        hops[k] = (quarter + across, 3 * quarter) if across % 2 == 0 else (3 * quarter + across, quarter)
    return hops


def bundles(parts):
    via = {}
    for k, (first, _) in relays(parts).items():
        via.setdefault(first, []).append(k)
    order = sorted(via) + [k for k in range(1, parts) if k not in via and k not in relays(parts)]
    return [(hop, [hop] + via.get(hop, [])) for hop in order]


def swapped(value, offset):
    parts = lax.axis_size("dom")
    return lax.ppermute(value, "dom", [(i, i ^ offset) for i in range(parts)])


def exchanged(sent, parts):
    hops = relays(parts)
    arrays, offsets = [], []
    for (hop, carried), value in zip(bundles(parts), sent):
        got = swapped(value, hop)
        arrays.append(got)
        offsets.append(hop)
        for place, k in enumerate(carried[1:], 1):
            arrays.append(swapped(got[place : place + 1], hops[k][1]))
            offsets.append(k)
    return arrays, offsets


def pick(info, source, targets, parts):
    block = targets[0].shape[1]
    for (_, carried), target in zip(bundles(parts), targets):
        for place, k in enumerate(carried):
            row = info[IDS + jnp.bitwise_xor(info[PART], k)]
            target[place] = source[pl.ds(pl.multiple_of(row * block, block), block)]


def sent_shapes(parts, block, width, dtype):
    return [pltpu.VMEM((len(carried), block, width), dtype) for _, carried in bundles(parts)]


def first_kernel(parts, info, current, x, *rest):
    sent, sem = rest[:-1], rest[-1]
    run([pltpu.make_async_copy(current, x, sem)])
    pick(info, x, sent, parts)


def first(info, current, parts, block):
    shapes = [pltpu.VMEM(current.shape, current.dtype)]
    shapes += sent_shapes(parts, block, current.shape[1], current.dtype)
    return pl.pallas_call(
        lambda *refs: first_kernel(parts, *refs),
        out_shape=shapes,
        in_specs=[SMEM, HBM],
        out_specs=[VMEM] * len(shapes),
        scratch_shapes=[pltpu.SemaphoreType.DMA],
        compiler_params=LIMIT,
    )(info, far(current))


def merge_kernel(info, col, counts, adj, own, other, fetched, total, sems):
    rows, block = adj.shape[0], adj.shape[-1]

    def fetch(row):
        return pltpu.make_async_copy(adj.at[row], fetched.at[row % 2], sems.at[row % 2])

    fetch(0).start()
    for row in range(rows):
        if row + 1 < rows:
            fetch(row + 1).start()
        total[...] = jnp.zeros_like(total)
        fetch(row).wait()

        def add(k, carry):
            entry = col[row, k]
            offset = jnp.bitwise_xor(jnp.maximum(entry - rows, 0), info[PART])
            afar = jnp.where(offset == 0, info[IDS + info[PART]], rows + offset - 1)
            total[jnp.where(entry < rows, entry, afar)] += fetched[row % 2, k].astype(jnp.float32)
            return carry

        lax.fori_loop(0, counts[row], add, 0)
        at = slice(row * block, (row + 1) * block)
        for entry in range(total.shape[0]):
            value = total[entry].astype(own.dtype)
            if entry < rows:
                own[at, entry * block : (entry + 1) * block] = value
            else:
                other[at, (entry - rows) * block : (entry - rows + 1) * block] = value


def merged(info, col, counts, adj, parts):
    rows, slots, block, _ = adj.shape
    return pl.pallas_call(
        merge_kernel,
        out_shape=[
            pltpu.VMEM((rows * block, rows * block), adj.dtype),
            pltpu.VMEM((rows * block, (parts - 1) * block), adj.dtype),
        ],
        in_specs=[SMEM, SMEM, SMEM, HBM],
        out_specs=[VMEM, VMEM],
        scratch_shapes=[
            pltpu.VMEM((2, slots, block, block), adj.dtype),
            pltpu.VMEM((rows + parts - 1, block, block), jnp.float32),
            pltpu.SemaphoreType.DMA((2,)),
        ],
        compiler_params=LIMIT,
    )(info, col, counts, far(adj))


def own_kernel(step, info, x, carried, new_h0, adj, partial, h0, sem):
    @pl.when(info[WRAPPED + step] == 1)
    def _():
        run([pltpu.make_async_copy(new_h0.at[info[SOURCE]], h0, sem)])

    @pl.when(info[WRAPPED + step] == 0)
    def _():
        run([pltpu.make_async_copy(carried, h0, sem)])

    for at in range(0, x.shape[0], TILE):
        rows = slice(at, at + TILE)
        agg = jnp.dot(adj[rows], x[...], preferred_element_type=jnp.float32)
        partial[rows] = (1.0 - teleport) * agg + teleport * h0[rows].astype(jnp.float32)


def own_part(step, info, x, carried, new_h0, adj):
    return pl.pallas_call(
        lambda *refs: own_kernel(step, *refs),
        out_shape=pltpu.VMEM(x.shape, jnp.float32),
        in_specs=[SMEM, VMEM, HBM, HBM, VMEM],
        out_specs=VMEM,
        scratch_shapes=[pltpu.VMEM(x.shape, x.dtype), pltpu.SemaphoreType.DMA],
        compiler_params=LIMIT,
    )(info, fast(x), far(carried), far(new_h0), fast(adj))


def layer_kernel(step, parts, offsets, info, beta, adj, partial, weight, new_h0, *rest):
    incoming, rest = rest[: len(offsets)], rest[len(offsets) :]
    block = incoming[0].shape[1]
    more = step < STEPS - 1
    out, following, sent = rest[0], rest[1], rest[2 : 2 + len(bundles(parts))]
    table, sem = rest[-2:]
    if more:
        fresh = pltpu.make_async_copy(new_h0.at[step], following, sem)

        @pl.when(info[STARTS + step + 1] == 1)
        def _():
            fresh.start()

    for offset, value in zip(offsets, incoming):
        table[(offset - 1) * block : offset * block] = value[0]
    scale = beta[step]
    for at in range(0, out.shape[0], TILE):
        rows = slice(at, at + TILE)
        agg = jnp.dot(adj[rows], table[...], preferred_element_type=jnp.float32)
        mixture = (partial[rows] + (1.0 - teleport) * agg).astype(jnp.bfloat16)
        product = jnp.dot(mixture, weight[...], preferred_element_type=jnp.float32)
        value = (1.0 - scale) * mixture.astype(jnp.float32) + scale * product
        out[rows] = jnp.maximum(value, 0.0).astype(out.dtype)
    if not more:
        return

    @pl.when(info[STARTS + step + 1] == 1)
    def _():
        fresh.wait()

    @pl.when(info[STARTS + step + 1] == 0)
    def _():
        following[...] = out[...]

    pick(info, following, sent, parts)


def layer(step, parts, info, beta, adj, partial, weight, new_h0, incoming, offsets):
    _, block, width = incoming[0].shape
    made = pltpu.VMEM(partial.shape, incoming[0].dtype)
    shapes = [made]
    if step < STEPS - 1:
        shapes += [made] + sent_shapes(parts, block, width, made.dtype)
    scratch = [pltpu.VMEM(((parts - 1) * block, width), made.dtype), pltpu.SemaphoreType.DMA]
    return pl.pallas_call(
        lambda *refs: layer_kernel(step, parts, offsets, *refs),
        out_shape=shapes,
        in_specs=[SMEM, SMEM, VMEM, VMEM, VMEM, HBM] + [VMEM] * len(incoming),
        out_specs=[VMEM] * len(shapes),
        scratch_shapes=scratch,
        compiler_params=LIMIT,
    )(info, beta, fast(adj), fast(partial), fast(weight), far(new_h0), *[fast(value) for value in incoming])


def keep_kernel(step, value, *rest):
    held, sem = rest[-2:]
    run([pltpu.make_async_copy(value, held.at[0, step], sem)])


def kept(step, value, held):
    return pl.pallas_call(
        lambda *refs: keep_kernel(step, *refs),
        out_shape=pltpu.HBM((1, STEPS) + value.shape, value.dtype),
        in_specs=[VMEM] if held is None else [VMEM, HBM],
        out_specs=HBM,
        scratch_shapes=[pltpu.SemaphoreType.DMA],
        input_output_aliases={} if held is None else {1: 0},
        compiler_params=LIMIT,
    )(*([fast(value)] if held is None else [fast(value), held]))


def moved(value, by):
    length = lax.axis_size("section")
    if by % length == 0:
        return value
    return lax.ppermute(value, "section", [((i + by) % length, i) for i in range(length)])


def body(carry_h, carry_h0, new_h0, weights, adj_blocks, col_index, counts, send_list):
    section = lax.axis_index("section")
    sections = lax.axis_size("section")
    part = lax.axis_index("dom")
    parts = send_list.shape[0]
    block = adj_blocks.shape[-1]
    place = section + jnp.arange(STEPS, dtype=jnp.int32)
    layers = place % sections
    beta = jnp.log(1.0 + strength / (layers.astype(jnp.float32) + 1.0))
    source = jnp.clip(sections - section - 1, 0, new_h0.shape[0] - 1)
    info = jnp.concatenate(
        [
            jnp.stack([part, source]).astype(jnp.int32),
            (place == sections).astype(jnp.int32),
            (place >= sections).astype(jnp.int32),
            lax.dynamic_index_in_dim(send_list, part, 0, keepdims=False),
        ]
    )
    current, *sent = first(info, carry_h[0], parts, block)
    layer_weights = [moved(weights[0], t) for t in range(STEPS)]
    own_adj = None
    held = None
    for t in range(STEPS):
        incoming, offsets = exchanged(sent, parts)
        if own_adj is None:
            own_adj, other_adj = merged(info, col_index, counts, adj_blocks, parts)
        partial = own_part(t, info, current, carry_h0[0], new_h0, own_adj)
        made, *rest = layer(
            t, parts, info, beta, other_adj, partial, layer_weights[t], new_h0, incoming, offsets
        )
        if rest:
            current, *sent = rest
        held = kept(t, moved(made, -t), held)
    return held


def solution(mesh):
    in_specs = (
        P("section", "dom", None),
        P("section", "dom", None),
        P(None, "dom", None),
        P("section", None, None),
        P("dom", None, None, None),
        P("dom", None),
        P("dom"),
        P(),
    )
    out_specs = P("section", None, "dom", None)
    return jax.shard_map(body, mesh=mesh, in_specs=in_specs, out_specs=out_specs, check_vma=False)
```

time: 269 us -> 169 us (0.63)
  matrix products: 53.3 us -> 0 us
  local copies, waits for them, and re-layouts: 49.7 us -> 2.18 us
  Pallas kernels: 0 us -> 36.9 us
  other arithmetic: 25.3 us -> 0.02 us
  waiting for transfers between devices: 94.5 us -> 70.2 us
  starting transfers between devices: 44.2 us -> 56.5 us
    all_to_all x4 -> x0, waiting for transfers between devices: 59.3 us -> none  [body(): lax.all_to_all(outgoing, 'dom', split_axis=0, concat_axis=0, tiled=True)]
    dot_general x8 -> x0, matrix products: 53.3 us -> none  [the longest x4 50.2 us: body(): jnp.einsum('rkij,rkjd->rid', masked_adj, picked, preferred_element_type=j...]
    gather x8 -> x0, local copies, waits for them, and re-layouts: 48.5 us -> none  [the longest x4 44.8 us: body(): picked = jnp.take(lookup, col_index, axis=0)]
    pallas_call x0 -> x14, Pallas kernels: none -> 36.9 us  [the longest x4 12.5 us: own_part(): pl.pallas_call(lambda *refs: own_kernel(step, *refs), out_shape=pltpu.VME...]
    ppermute x6 -> x34, waiting for transfers between devices: 35.2 us -> 70.2 us  [the longest x6 38.6 us: moved(): lax.ppermute(value, 'section', [((i + by) % length, i) for i in range(len...]
    ppermute x6 -> x34, starting transfers between devices: 25.1 us -> 56.5 us  [the longest x28 34.6 us: swapped(): return lax.ppermute(value, 'dom', [(i, i ^ offset) for i in range(parts)])]
    all_to_all x4 -> x0, starting transfers between devices: 19.1 us -> none  [body(): lax.all_to_all(outgoing, 'dom', split_axis=0, concat_axis=0, tiled=True)]
    concatenate x4 -> x0, other arithmetic: 6.89 us -> none  [body(): lookup = jnp.concatenate([own_blocks, incoming], axis=0)]
  transfers between devices with their start and end apart: 10 -> 34, of which waited for: 7 -> 14; matrix products, arithmetic and copies ran while one was open for 29% -> 0% of each run, Pallas kernels for 0% -> 21%
where the time goes in v2:
time: 169 us; the launch traced here: 166 us
  waiting for transfers between devices  70.2 us (42%)
  starting transfers between devices  56.5 us (33%)
  Pallas kernels  36.9 us (22%)
  local copies, waits for them, and re-layouts  2.18 us (1%)
    ppermute x6, waiting for transfers between devices, moved(): lax.ppermute(value, 'section', [((i + by) % length, i) for i in range(len...  38.6 us
    ppermute x28, starting transfers between devices, swapped(): return lax.ppermute(value, 'dom', [(i, i ^ offset) for i in range(parts)])  34.6 us
    ppermute x28, waiting for transfers between devices, swapped(): return lax.ppermute(value, 'dom', [(i, i ^ offset) for i in range(parts)])  31.6 us
    ppermute x6, starting transfers between devices, moved(): lax.ppermute(value, 'section', [((i + by) % length, i) for i in range(len...  21.9 us
    pallas_call x4, Pallas kernels, own_part(): pl.pallas_call(lambda *refs: own_kernel(step, *refs), out_shape=pltpu.VME...  12.5 us
    pallas_call x4, Pallas kernels, layer(): pl.pallas_call(lambda *refs: layer_kernel(step, parts, offsets, *refs), o...  12.3 us
    pallas_call x1, Pallas kernels, merged(): pl.pallas_call(merge_kernel, out_shape=[pltpu.VMEM((rows * block, rows *...  6.35 us
    pallas_call x4, Pallas kernels, kept(): pl.pallas_call(lambda *refs: keep_kernel(step, *refs), out_shape=pltpu.HB...  3.91 us
  transfers between devices with their start and end apart: 34, of which 14 were waited for; matrix products, arithmetic and copies ran while one was open for 0% of the time, Pallas kernels for 21%

profile of v2, /device:TPU:1, one launch (start us, length us, event | category | flops | bytes accessed | tf_op | source)
XLA Modules:
  0.0 166.3 jit_solution(17946230280299370295)
XLA Ops:
  0.8 1.8 %shard_map.83 = (bf16[1024,512]{1,0:T(8,128)(2,1)S(1)}, bf16[2,128,512]{2,1,0:T(8,128)(2,1)S(1)}, bf16[2,128,512]{2,1,0:T(8,128)(2,1)S(1)}, bf16[1,128,512]{2,1,...) custom-call(s32[18]{0:T(128)S(1)} %concatenate.3.info.refs_0_, ...), custom_call_target="tpu_custom_call" | custom-call | tf_op jit(solution)/shard_map/pallas_call | solution.py:95
  2.6 2.2 %collective-permute-start = (bf16[2,128,512]{2,1,0:T(8,128)(2,1)S(1)}, bf16[2,128,512]{2,1,0:T(8,128)(2,1)S(1)}, u32[]{:S(2)}, u32[]{:S(2)}) collective-permute-start(bf16[2,128,512]{2,1,0:T(8,128)(2,1)S(1)} %get-tuple-element.37), channel_id=1, source_target_pairs={{0,2},{1,3},{2,0},{3,1},{4,6},{5,7},{6,4},{7,5},{8,10},{9,11},{10,... | collective-permute-start | bytes 786440 | tf_op jit(solution)/shard_map/ppermute | solution.py:58
  4.8 3.1 %collective-permute-start.2 = (bf16[2,128,512]{2,1,0:T(8,128)(2,1)S(1)}, bf16[2,128,512]{2,1,0:T(8,128)(2,1)S(1)}, u32[]{:S(2)}, u32[]{:S(2)}) collective-permute-start(bf16[2,128,512]{2,1,0:T(8,128)(2,1)S(1)} %get-tuple-element.38), channel_id=1, source_target_pairs={{0,7},{1,6},{2,5},{3,4},{4,3},{5,2},{6,1},{7,0},{8,15},{9,14},{10,... | collective-permute-start | bytes 786440 | tf_op jit(solution)/shard_map/ppermute | solution.py:58
  11.0 3.2 %collective-permute-start.6 = (bf16[1,128,512]{2,1,0:T(8,128)(2,1)S(1)}, bf16[1,128,512]{2,1,0:T(8,128)(2,1)S(1)}, u32[]{:S(2)}, u32[]{:S(2)}) collective-permute-start(bf16[1,128,512]{2,1,0:T(8,128)(2,1)S(1)} %get-tuple-element.41), channel_id=1, source_target_pairs={{0,6},{1,7},{2,4},{3,5},{4,2},{5,3},{6,0},{7,1},{8,14},{9,15},{10,... | collective-permute-start | bytes 393224 | tf_op jit(solution)/shard_map/ppermute | solution.py:58
  14.2 5.1 %collective-permute-done.2.refs_8_ = bf16[2,128,512]{2,1,0:T(8,128)(2,1)S(1)} collective-permute-done((bf16[2,128,512]{2,1,0:T(8,128)(2,1)S(1)}, bf16[2,128,512]{2,1,0:T(8,128)(2,1)S(1)}, u32[]{:S(2)}, u32[]{:S(2)}) %collective-permute-start.2) | collective-permute-done | bytes 262176 | tf_op jit(solution)/shard_map/ppermute | solution.py:58
  21.8 6.4 %shard_map.82 = (bf16[1024,1024]{1,0:T(8,128)(2,1)S(1)}, bf16[1024,896]{1,0:T(8,128)(2,1)S(1)}) custom-call(s32[18]{0:T(128)S(1)} %concatenate.3.info.refs_0_, s32[8,24]{1,0:T(8,128)S(1)} %copy-done.2, s32[8]{0:T(128)S(1)} %copy-done.3, bf16[8,24,128,128]{3,2,1,0:T(8,128)(2,1)} %adj.1), custom_call_target="tpu_custom_call" | custom-call | tf_op jit(solution)/shard_map/pallas_call | solution.py:137
  28.2 3.2 %shard_map.84.refs_3_ = f32[1024,512]{1,0:T(8,128)S(1)} custom-call(s32[18]{0:T(128)S(1)} %concatenate.3.info.refs_0_, bf16[1024,512]{1,0:T(8,128)(2,1)S(1)} %get-tuple-element.35.refs_1_, bf16[1024,512]{1,0:T(8,128)(2,1)} %bitcast.11, bf16[3,1024,512]{2,1,0:T(8,128)(2,1)} %refs_5_.7, bf16[1024,1024]{1,0:T(8,128)(2,1)S(1)} %get-tuple-element.36.refs_4_), custom_call_target="tpu_custom_call" | custom-call | tf_op jit(solution)/shard_map/pallas_call | solution.py:170
  31.4 2.8 %shard_map.85 = (bf16[1024,512]{1,0:T(8,128)(2,1)S(1)}, bf16[1024,512]{1,0:T(8,128)(2,1)S(1)}, bf16[2,128,512]{2,1,0:T(8,128)(2,1)S(1)}, bf16[2,128,512]{2,1,0:T...) custom-call(s32[18]{0:T(128)S(1)} %concatenate.3.info.refs_0_, ...), custom_call_target="tpu_custom_call" | custom-call | tf_op jit(solution)/shard_map/pallas_call | solution.py:224
  35.8 2.4 %collective-permute-start.10 = (bf16[2,128,512]{2,1,0:T(8,128)(2,1)S(1)}, bf16[2,128,512]{2,1,0:T(8,128)(2,1)S(1)}, u32[]{:S(2)}, u32[]{:S(2)}) collective-permute-start(bf16[2,128,512]{2,1,0:T(8,128)(2,1)S(1)} %get-tuple-element.44), channel_id=1, source_target_pairs={{0,7},{1,6},{2,5},{3,4},{4,3},{5,2},{6,1},{7,0},{8,15},{9,14},{10,... | collective-permute-start | bytes 786440 | tf_op jit(solution)/shard_map/ppermute | solution.py:58
  39.2 2.2 %collective-permute-start.15 = (bf16[512,512]{1,0:T(8,128)(2,1)S(1)}, bf16[512,512]{1,0:T(8,128)(2,1)S(1)}, u32[]{:S(2)}, u32[]{:S(2)}) collective-permute-start(bf16[512,512]{1,0:T(8,128)(2,1)S(1)} %bitcast.9), channel_id=1, source_target_pairs={{16,0},{24,8},{0,16},{8,24},{17,1},{25,9},{1,17},{9,25},{18,2},{26... | collective-permute-start | bytes 1572872 | tf_op jit(solution)/shard_map/ppermute | solution.py:255
  41.4 3.4 %collective-permute-done.10.refs_8_ = bf16[2,128,512]{2,1,0:T(8,128)(2,1)S(1)} collective-permute-done((bf16[2,128,512]{2,1,0:T(8,128)(2,1)S(1)}, bf16[2,128,512]{2,1,0:T(8,128)(2,1)S(1)}, u32[]{:S(2)}, u32[]{:S(2)}) %collective-permute-start.10) | collective-permute-done | bytes 262176 | tf_op jit(solution)/shard_map/ppermute | solution.py:58
  46.1 2.1 %collective-permute-start.9 = (bf16[1,128,512]{2,1,0:T(8,128)(2,1)S(1)}, bf16[1,128,512]{2,1,0:T(8,128)(2,1)S(1)}, u32[]{:S(2)}, u32[]{:S(2)}) collective-permute-start(bf16[1,128,512]{2,1,0:T(8,128)(2,1)S(1)} %slice.34), channel_id=1, source_target_pairs={{0,6},{1,7},{2,4},{3,5},{4,2},{5,3},{6,0},{7,1},{8,14},{9,15},{10,... | collective-permute-start | bytes 393224 | tf_op jit(solution)/shard_map/ppermute | solution.py:58
  48.2 3.1 %shard_map.86.refs_3_ = f32[1024,512]{1,0:T(8,128)S(1)} custom-call(s32[18]{0:T(128)S(1)} %concatenate.3.info.refs_0_, bf16[1024,512]{1,0:T(8,128)(2,1)S(1)} %get-tuple-element.42.refs_1_, bf16[1024,512]{1,0:T(8,128)(2,1)} %bitcast.12, bf16[3,1024,512]{2,1,0:T(8,128)(2,1)} %refs_5_.7, bf16[1024,1024]{1,0:T(8,128)(2,1)S(1)} %get-tuple-element.36.refs_4_), custom_call_target="tpu_custom_call" | custom-call | tf_op jit(solution)/shard_map/pallas_call | solution.py:170
  52.3 2.4 %collective-permute-done.9.refs_7_ = bf16[1,128,512]{2,1,0:T(8,128)(2,1)S(1)} collective-permute-done((bf16[1,128,512]{2,1,0:T(8,128)(2,1)S(1)}, bf16[1,128,512]{2,1,0:T(8,128)(2,1)S(1)}, u32[]{:S(2)}, u32[]{:S(2)}) %collective-permute-start.9) | collective-permute-done | bytes 131104 | tf_op jit(solution)/shard_map/ppermute | solution.py:58
  54.6 2.9 %collective-permute-done.11.refs_9_ = bf16[1,128,512]{2,1,0:T(8,128)(2,1)S(1)} collective-permute-done((bf16[1,128,512]{2,1,0:T(8,128)(2,1)S(1)}, bf16[1,128,512]{2,1,0:T(8,128)(2,1)S(1)}, u32[]{:S(2)}, u32[]{:S(2)}) %collective-permute-start.11) | collective-permute-done | bytes 131104 | tf_op jit(solution)/shard_map/ppermute | solution.py:58
  57.5 2.9 %shard_map.87 = (bf16[1024,512]{1,0:T(8,128)(2,1)S(1)}, bf16[1024,512]{1,0:T(8,128)(2,1)S(1)}, bf16[2,128,512]{2,1,0:T(8,128)(2,1)S(1)}, bf16[2,128,512]{2,1,0:T...) custom-call(s32[18]{0:T(128)S(1)} %concatenate.3.info.refs_0_, ...), custom_call_target="tpu_custom_call" | custom-call | tf_op jit(solution)/shard_map/pallas_call | solution.py:224
  62.1 2.0 %collective-permute-start.20 = (bf16[1,128,512]{2,1,0:T(8,128)(2,1)S(1)}, bf16[1,128,512]{2,1,0:T(8,128)(2,1)S(1)}, u32[]{:S(2)}, u32[]{:S(2)}) collective-permute-start(bf16[1,128,512]{2,1,0:T(8,128)(2,1)S(1)} %get-tuple-element.51), channel_id=1, source_target_pairs={{0,1},{1,0},{2,3},{3,2},{4,5},{5,4},{6,7},{7,6},{8,9},{9,8},{10,11... | collective-permute-start | bytes 393224 | tf_op jit(solution)/shard_map/ppermute | solution.py:58
  64.0 10.9 %collective-permute-start.23 = (bf16[512,512]{1,0:T(8,128)(2,1)S(1)}, bf16[512,512]{1,0:T(8,128)(2,1)S(1)}, u32[]{:S(2)}, u32[]{:S(2)}) collective-permute-start(bf16[512,512]{1,0:T(8,128)(2,1)S(1)} %bitcast.10), channel_id=1, source_target_pairs={{24,0},{0,8},{8,16},{16,24},{25,1},{1,9},{9,17},{17,25},{26,2},{2,... | collective-permute-start | bytes 1572872 | tf_op jit(solution)/shard_map/ppermute | solution.py:255
  77.3 2.0 %collective-permute-start.17 = (bf16[1,128,512]{2,1,0:T(8,128)(2,1)S(1)}, bf16[1,128,512]{2,1,0:T(8,128)(2,1)S(1)}, u32[]{:S(2)}, u32[]{:S(2)}) collective-permute-start(bf16[1,128,512]{2,1,0:T(8,128)(2,1)S(1)} %slice.36), channel_id=1, source_target_pairs={{0,6},{1,7},{2,4},{3,5},{4,2},{5,3},{6,0},{7,1},{8,14},{9,15},{10,... | collective-permute-start | bytes 393224 | tf_op jit(solution)/shard_map/ppermute | solution.py:58
  79.3 3.1 %shard_map.88.refs_3_ = f32[1024,512]{1,0:T(8,128)S(1)} custom-call(s32[18]{0:T(128)S(1)} %concatenate.3.info.refs_0_, bf16[1024,512]{1,0:T(8,128)(2,1)S(1)} %get-tuple-element.48.refs_1_, bf16[1024,512]{1,0:T(8,128)(2,1)} %bitcast.13, bf16[3,1024,512]{2,1,0:T(8,128)(2,1)} %refs_5_.7, bf16[1024,1024]{1,0:T(8,128)(2,1)S(1)} %get-tuple-element.36.refs_4_), custom_call_target="tpu_custom_call" | custom-call | tf_op jit(solution)/shard_map/pallas_call | solution.py:170
  84.0 2.5 %collective-permute-done.17.refs_7_ = bf16[1,128,512]{2,1,0:T(8,128)(2,1)S(1)} collective-permute-done((bf16[1,128,512]{2,1,0:T(8,128)(2,1)S(1)}, bf16[1,128,512]{2,1,0:T(8,128)(2,1)S(1)}, u32[]{:S(2)}, u32[]{:S(2)}) %collective-permute-start.17) | collective-permute-done | bytes 131104 | tf_op jit(solution)/shard_map/ppermute | solution.py:58
  86.5 3.7 %collective-permute-done.19.refs_9_ = bf16[1,128,512]{2,1,0:T(8,128)(2,1)S(1)} collective-permute-done((bf16[1,128,512]{2,1,0:T(8,128)(2,1)S(1)}, bf16[1,128,512]{2,1,0:T(8,128)(2,1)S(1)}, u32[]{:S(2)}, u32[]{:S(2)}) %collective-permute-start.19) | collective-permute-done | bytes 131104 | tf_op jit(solution)/shard_map/ppermute | solution.py:58
  90.2 3.8 %shard_map.89 = (bf16[1024,512]{1,0:T(8,128)(2,1)S(1)}, bf16[1024,512]{1,0:T(8,128)(2,1)S(1)}, bf16[2,128,512]{2,1,0:T(8,128)(2,1)S(1)}, bf16[2,128,512]{2,1,0:T...) custom-call(s32[18]{0:T(128)S(1)} %concatenate.3.info.refs_0_, ...), custom_call_target="tpu_custom_call" | custom-call | tf_op jit(solution)/shard_map/pallas_call | solution.py:224
  94.2 2.9 %collective-permute-start.26 = (bf16[2,128,512]{2,1,0:T(8,128)(2,1)S(1)}, bf16[2,128,512]{2,1,0:T(8,128)(2,1)S(1)}, u32[]{:S(2)}, u32[]{:S(2)}) collective-permute-start(bf16[2,128,512]{2,1,0:T(8,128)(2,1)S(1)} %get-tuple-element.56), channel_id=1, source_target_pairs={{0,7},{1,6},{2,5},{3,4},{4,3},{5,2},{6,1},{7,0},{8,15},{9,14},{10,... | collective-permute-start | bytes 786440 | tf_op jit(solution)/shard_map/ppermute | solution.py:58
  98.7 3.1 %collective-permute-done.24.refs_6_ = bf16[2,128,512]{2,1,0:T(8,128)(2,1)S(1)} collective-permute-done((bf16[2,128,512]{2,1,0:T(8,128)(2,1)S(1)}, bf16[2,128,512]{2,1,0:T(8,128)(2,1)S(1)}, u32[]{:S(2)}, u32[]{:S(2)}) %collective-permute-start.24) | collective-permute-done | bytes 262176 | tf_op jit(solution)/shard_map/ppermute | solution.py:58
  101.9 1.5 collective-permute-start.30
  103.4 5.7 %collective-permute-done.26.refs_8_ = bf16[2,128,512]{2,1,0:T(8,128)(2,1)S(1)} collective-permute-done((bf16[2,128,512]{2,1,0:T(8,128)(2,1)S(1)}, bf16[2,128,512]{2,1,0:T(8,128)(2,1)S(1)}, u32[]{:S(2)}, u32[]{:S(2)}) %collective-permute-start.26) | collective-permute-done | bytes 262176 | tf_op jit(solution)/shard_map/ppermute | solution.py:58
  110.1 3.1 %shard_map.90.refs_3_ = f32[1024,512]{1,0:T(8,128)S(1)} custom-call(s32[18]{0:T(128)S(1)} %concatenate.3.info.refs_0_, bf16[1024,512]{1,0:T(8,128)(2,1)S(1)} %get-tuple-element.54.refs_1_, bf16[1024,512]{1,0:T(8,128)(2,1)} %bitcast.14, bf16[3,1024,512]{2,1,0:T(8,128)(2,1)} %refs_5_.7, bf16[1024,1024]{1,0:T(8,128)(2,1)S(1)} %get-tuple-element.36.refs_4_), custom_call_target="tpu_custom_call" | custom-call | tf_op jit(solution)/shard_map/pallas_call | solution.py:170
  113.2 6.1 %collective-permute-start.33 = (bf16[1024,512]{1,0:T(8,128)(2,1)S(1)}, bf16[1024,512]{1,0:T(8,128)(2,1)S(1)}, u32[]{:S(2)}, u32[]{:S(2)}) collective-permute-start(bf16[1024,512]{1,0:T(8,128)(2,1)S(1)} %get-tuple-element.61), channel_id=1, source_target_pairs={{24,0},{0,8},{8,16},{16,24},{25,1},{1,9},{9,17},{17,25},{26,2},{2,... | collective-permute-start | bytes 3145736 | tf_op jit(solution)/shard_map/ppermute | solution.py:255
  119.6 2.8 %shard_map.91 = bf16[1024,512]{1,0:T(8,128)(2,1)S(1)} custom-call(s32[18]{0:T(128)S(1)} %concatenate.3.info.refs_0_, f32[4]{0:T(128)S(1)} %fusion.4.refs_1_, bf16[1024,896]{1,0:T(8,128)(2,1)S(1)} %get-tuple-element.34.refs_2_, f32[1024,512]{1,0:T(8,128)S(1)} %shard_map.90.refs_3_, bf16[512,512]{1,0:T(8,128)(2,1)S(1)} %collective-permute-done.23.refs_4_, ...), custom_call_target="tpu_custom_call" | custom-call | tf_op jit(solution)/shard_map/pallas_call | solution.py:224
  124.5 17.1 %collective-permute-done.33.refs_0_ = bf16[1024,512]{1,0:T(8,128)(2,1)S(1)} collective-permute-done((bf16[1024,512]{1,0:T(8,128)(2,1)S(1)}, bf16[1024,512]{1,0:T(8,128)(2,1)S(1)}, u32[]{:S(2)}, u32[]{:S(2)}) %collective-permute-start.33) | collective-permute-done | bytes 1048608 | tf_op jit(solution)/shard_map/ppermute | solution.py:255
  142.7 21.5 %collective-permute-done.32.refs_0_ = bf16[1024,512]{1,0:T(8,128)(2,1)S(1)} collective-permute-done((bf16[1024,512]{1,0:T(8,128)(2,1)S(1)}, bf16[1024,512]{1,0:T(8,128)(2,1)S(1)}, u32[]{:S(2)}, u32[]{:S(2)}) %collective-permute-start.32) | collective-permute-done | bytes 1048608 | tf_op jit(solution)/shard_map/ppermute | solution.py:255
  (70 shorter events, 24.8 us)
Async XLA Ops:
  2.6 8.4 %collective-permute-start = (bf16[2,128,512]{2,1,0:T(8,128)(2,1)S(1)}, bf16[2,128,512]{2,1,0:T(8,128)(2,1)S(1)}, u32[]{:S(2)}, u32[]{:S(2)}) collective-permute-start(bf16[2,128,512]{2,1,0:T(8,128)(2,1)S(1)} %get-tuple-element.37), channel_id=1, source_target_pairs={{0,2},{1,3},{2,0},{3,1},{4,6},{5,7},{6,4},{7,5},{8,10},{9,11},{10,... | collective-permute-start | bytes 786440 | tf_op jit(solution)/shard_map/ppermute | solution.py:58
  4.8 14.5 %collective-permute-start.2 = (bf16[2,128,512]{2,1,0:T(8,128)(2,1)S(1)}, bf16[2,128,512]{2,1,0:T(8,128)(2,1)S(1)}, u32[]{:S(2)}, u32[]{:S(2)}) collective-permute-start(bf16[2,128,512]{2,1,0:T(8,128)(2,1)S(1)} %get-tuple-element.38), channel_id=1, source_target_pairs={{0,7},{1,6},{2,5},{3,4},{4,3},{5,2},{6,1},{7,0},{8,15},{9,14},{10,... | collective-permute-start | bytes 786440 | tf_op jit(solution)/shard_map/ppermute | solution.py:58
  7.9 12.5 %collective-permute-start.4 = (bf16[1,128,512]{2,1,0:T(8,128)(2,1)S(1)}, bf16[1,128,512]{2,1,0:T(8,128)(2,1)S(1)}, u32[]{:S(2)}, u32[]{:S(2)}) collective-permute-start(bf16[1,128,512]{2,1,0:T(8,128)(2,1)S(1)} %get-tuple-element.39), channel_id=1, source_target_pairs={{0,1},{1,0},{2,3},{3,2},{4,5},{5,4},{6,7},{7,6},{8,9},{9,8},{10,11... | collective-permute-start | bytes 393224 | tf_op jit(solution)/shard_map/ppermute | solution.py:58
  8.2 37.9 %collective-permute-start.7 = (bf16[512,512]{1,0:T(8,128)(2,1)}, bf16[512,512]{1,0:T(8,128)(2,1)S(1)}, u32[]{:S(2)}, u32[]{:S(2)}) collective-permute-start(bf16[512,512]{1,0:T(8,128)(2,1)} %bitcast.7), channel_id=1, source_target_pairs={{8,0},{16,8},{24,16},{0,24},{9,1},{17,9},{25,17},{1,25},{10,2},{18... | collective-permute-start | bytes 1572872 | tf_op jit(solution)/shard_map/ppermute | solution.py:255
  9.7 21.7 %collective-permute-start.5 = (bf16[1,128,512]{2,1,0:T(8,128)(2,1)S(1)}, bf16[1,128,512]{2,1,0:T(8,128)(2,1)S(1)}, u32[]{:S(2)}, u32[]{:S(2)}) collective-permute-start(bf16[1,128,512]{2,1,0:T(8,128)(2,1)S(1)} %get-tuple-element.40), channel_id=1, source_target_pairs={{0,3},{1,2},{2,1},{3,0},{4,7},{5,6},{6,5},{7,4},{8,11},{9,10},{10,... | collective-permute-start | bytes 393224 | tf_op jit(solution)/shard_map/ppermute | solution.py:58
  11.0 20.4 %collective-permute-start.6 = (bf16[1,128,512]{2,1,0:T(8,128)(2,1)S(1)}, bf16[1,128,512]{2,1,0:T(8,128)(2,1)S(1)}, u32[]{:S(2)}, u32[]{:S(2)}) collective-permute-start(bf16[1,128,512]{2,1,0:T(8,128)(2,1)S(1)} %get-tuple-element.41), channel_id=1, source_target_pairs={{0,6},{1,7},{2,4},{3,5},{4,2},{5,3},{6,0},{7,1},{8,14},{9,15},{10,... | collective-permute-start | bytes 393224 | tf_op jit(solution)/shard_map/ppermute | solution.py:58
  19.3 12.1 %collective-permute-start.1 = (bf16[1,128,512]{2,1,0:T(8,128)(2,1)S(1)}, bf16[1,128,512]{2,1,0:T(8,128)(2,1)S(1)}, u32[]{:S(2)}, u32[]{:S(2)}) collective-permute-start(bf16[1,128,512]{2,1,0:T(8,128)(2,1)S(1)} %slice.32), channel_id=1, source_target_pairs={{0,6},{1,7},{2,4},{3,5},{4,2},{5,3},{6,0},{7,1},{8,14},{9,15},{10,... | collective-permute-start | bytes 393224 | tf_op jit(solution)/shard_map/ppermute | solution.py:58
  20.4 11.0 %collective-permute-start.3 = (bf16[1,128,512]{2,1,0:T(8,128)(2,1)S(1)}, bf16[1,128,512]{2,1,0:T(8,128)(2,1)S(1)}, u32[]{:S(2)}, u32[]{:S(2)}) collective-permute-start(bf16[1,128,512]{2,1,0:T(8,128)(2,1)S(1)} %slice.33), channel_id=1, source_target_pairs={{0,2},{1,3},{2,0},{3,1},{4,6},{5,7},{6,4},{7,5},{8,10},{9,11},{10,... | collective-permute-start | bytes 393224 | tf_op jit(solution)/shard_map/ppermute | solution.py:58
  35.8 9.0 %collective-permute-start.10 = (bf16[2,128,512]{2,1,0:T(8,128)(2,1)S(1)}, bf16[2,128,512]{2,1,0:T(8,128)(2,1)S(1)}, u32[]{:S(2)}, u32[]{:S(2)}) collective-permute-start(bf16[2,128,512]{2,1,0:T(8,128)(2,1)S(1)} %get-tuple-element.44), channel_id=1, source_target_pairs={{0,7},{1,6},{2,5},{3,4},{4,3},{5,2},{6,1},{7,0},{8,15},{9,14},{10,... | collective-permute-start | bytes 786440 | tf_op jit(solution)/shard_map/ppermute | solution.py:58
  38.2 10.0 %collective-permute-start.12 = (bf16[1,128,512]{2,1,0:T(8,128)(2,1)S(1)}, bf16[1,128,512]{2,1,0:T(8,128)(2,1)S(1)}, u32[]{:S(2)}, u32[]{:S(2)}) collective-permute-start(bf16[1,128,512]{2,1,0:T(8,128)(2,1)S(1)} %get-tuple-element.45), channel_id=1, source_target_pairs={{0,1},{1,0},{2,3},{3,2},{4,5},{5,4},{6,7},{7,6},{8,9},{9,8},{10,11... | collective-permute-start | bytes 393224 | tf_op jit(solution)/shard_map/ppermute | solution.py:58
  39.2 38.1 %collective-permute-start.15 = (bf16[512,512]{1,0:T(8,128)(2,1)S(1)}, bf16[512,512]{1,0:T(8,128)(2,1)S(1)}, u32[]{:S(2)}, u32[]{:S(2)}) collective-permute-start(bf16[512,512]{1,0:T(8,128)(2,1)S(1)} %bitcast.9), channel_id=1, source_target_pairs={{16,0},{24,8},{0,16},{8,24},{17,1},{25,9},{1,17},{9,25},{18,2},{26... | collective-permute-start | bytes 1572872 | tf_op jit(solution)/shard_map/ppermute | solution.py:255
  41.4 9.9 %collective-permute-start.13 = (bf16[1,128,512]{2,1,0:T(8,128)(2,1)S(1)}, bf16[1,128,512]{2,1,0:T(8,128)(2,1)S(1)}, u32[]{:S(2)}, u32[]{:S(2)}) collective-permute-start(bf16[1,128,512]{2,1,0:T(8,128)(2,1)S(1)} %get-tuple-element.46), channel_id=1, source_target_pairs={{0,3},{1,2},{2,1},{3,0},{4,7},{5,6},{6,5},{7,4},{8,11},{9,10},{10,... | collective-permute-start | bytes 393224 | tf_op jit(solution)/shard_map/ppermute | solution.py:58
  46.1 8.5 %collective-permute-start.9 = (bf16[1,128,512]{2,1,0:T(8,128)(2,1)S(1)}, bf16[1,128,512]{2,1,0:T(8,128)(2,1)S(1)}, u32[]{:S(2)}, u32[]{:S(2)}) collective-permute-start(bf16[1,128,512]{2,1,0:T(8,128)(2,1)S(1)} %slice.34), channel_id=1, source_target_pairs={{0,6},{1,7},{2,4},{3,5},{4,2},{5,3},{6,0},{7,1},{8,14},{9,15},{10,... | collective-permute-start | bytes 393224 | tf_op jit(solution)/shard_map/ppermute | solution.py:58
  48.2 9.3 %collective-permute-start.11 = (bf16[1,128,512]{2,1,0:T(8,128)(2,1)S(1)}, bf16[1,128,512]{2,1,0:T(8,128)(2,1)S(1)}, u32[]{:S(2)}, u32[]{:S(2)}) collective-permute-start(bf16[1,128,512]{2,1,0:T(8,128)(2,1)S(1)} %slice.35), channel_id=1, source_target_pairs={{0,2},{1,3},{2,0},{3,1},{4,6},{5,7},{6,4},{7,5},{8,10},{9,11},{10,... | collective-permute-start | bytes 393224 | tf_op jit(solution)/shard_map/ppermute | solution.py:58
  60.4 14.6 %collective-permute-start.16 = (bf16[2,128,512]{2,1,0:T(8,128)(2,1)S(1)}, bf16[2,128,512]{2,1,0:T(8,128)(2,1)S(1)}, u32[]{:S(2)}, u32[]{:S(2)}) collective-permute-start(bf16[2,128,512]{2,1,0:T(8,128)(2,1)S(1)} %get-tuple-element.49), channel_id=1, source_target_pairs={{0,2},{1,3},{2,0},{3,1},{4,6},{5,7},{6,4},{7,5},{8,10},{9,11},{10,... | collective-permute-start | bytes 786440 | tf_op jit(solution)/shard_map/ppermute | solution.py:58
  60.9 14.9 %collective-permute-start.18 = (bf16[2,128,512]{2,1,0:T(8,128)(2,1)S(1)}, bf16[2,128,512]{2,1,0:T(8,128)(2,1)S(1)}, u32[]{:S(2)}, u32[]{:S(2)}) collective-permute-start(bf16[2,128,512]{2,1,0:T(8,128)(2,1)S(1)} %get-tuple-element.50), channel_id=1, source_target_pairs={{0,7},{1,6},{2,5},{3,4},{4,3},{5,2},{6,1},{7,0},{8,15},{9,14},{10,... | collective-permute-start | bytes 786440 | tf_op jit(solution)/shard_map/ppermute | solution.py:58
  62.1 17.2 %collective-permute-start.20 = (bf16[1,128,512]{2,1,0:T(8,128)(2,1)S(1)}, bf16[1,128,512]{2,1,0:T(8,128)(2,1)S(1)}, u32[]{:S(2)}, u32[]{:S(2)}) collective-permute-start(bf16[1,128,512]{2,1,0:T(8,128)(2,1)S(1)} %get-tuple-element.51), channel_id=1, source_target_pairs={{0,1},{1,0},{2,3},{3,2},{4,5},{5,4},{6,7},{7,6},{8,9},{9,8},{10,11... | collective-permute-start | bytes 393224 | tf_op jit(solution)/shard_map/ppermute | solution.py:58
  64.0 45.1 %collective-permute-start.23 = (bf16[512,512]{1,0:T(8,128)(2,1)S(1)}, bf16[512,512]{1,0:T(8,128)(2,1)S(1)}, u32[]{:S(2)}, u32[]{:S(2)}) collective-permute-start(bf16[512,512]{1,0:T(8,128)(2,1)S(1)} %bitcast.10), channel_id=1, source_target_pairs={{24,0},{0,8},{8,16},{16,24},{25,1},{1,9},{9,17},{17,25},{26,2},{2,... | collective-permute-start | bytes 1572872 | tf_op jit(solution)/shard_map/ppermute | solution.py:255
  75.0 7.7 %collective-permute-start.21 = (bf16[1,128,512]{2,1,0:T(8,128)(2,1)S(1)}, bf16[1,128,512]{2,1,0:T(8,128)(2,1)S(1)}, u32[]{:S(2)}, u32[]{:S(2)}) collective-permute-start(bf16[1,128,512]{2,1,0:T(8,128)(2,1)S(1)} %get-tuple-element.52), channel_id=1, source_target_pairs={{0,3},{1,2},{2,1},{3,0},{4,7},{5,6},{6,5},{7,4},{8,11},{9,10},{10,... | collective-permute-start | bytes 393224 | tf_op jit(solution)/shard_map/ppermute | solution.py:58
  75.9 8.2 %collective-permute-start.22 = (bf16[1,128,512]{2,1,0:T(8,128)(2,1)S(1)}, bf16[1,128,512]{2,1,0:T(8,128)(2,1)S(1)}, u32[]{:S(2)}, u32[]{:S(2)}) collective-permute-start(bf16[1,128,512]{2,1,0:T(8,128)(2,1)S(1)} %get-tuple-element.53), channel_id=1, source_target_pairs={{0,6},{1,7},{2,4},{3,5},{4,2},{5,3},{6,0},{7,1},{8,14},{9,15},{10,... | collective-permute-start | bytes 393224 | tf_op jit(solution)/shard_map/ppermute | solution.py:58
  77.3 9.2 %collective-permute-start.17 = (bf16[1,128,512]{2,1,0:T(8,128)(2,1)S(1)}, bf16[1,128,512]{2,1,0:T(8,128)(2,1)S(1)}, u32[]{:S(2)}, u32[]{:S(2)}) collective-permute-start(bf16[1,128,512]{2,1,0:T(8,128)(2,1)S(1)} %slice.36), channel_id=1, source_target_pairs={{0,6},{1,7},{2,4},{3,5},{4,2},{5,3},{6,0},{7,1},{8,14},{9,15},{10,... | collective-permute-start | bytes 393224 | tf_op jit(solution)/shard_map/ppermute | solution.py:58
  79.3 10.9 %collective-permute-start.19 = (bf16[1,128,512]{2,1,0:T(8,128)(2,1)S(1)}, bf16[1,128,512]{2,1,0:T(8,128)(2,1)S(1)}, u32[]{:S(2)}, u32[]{:S(2)}) collective-permute-start(bf16[1,128,512]{2,1,0:T(8,128)(2,1)S(1)} %slice.37), channel_id=1, source_target_pairs={{0,2},{1,3},{2,0},{3,1},{4,6},{5,7},{6,4},{7,5},{8,10},{9,11},{10,... | collective-permute-start | bytes 393224 | tf_op jit(solution)/shard_map/ppermute | solution.py:58
  94.1 7.8 %collective-permute-start.24 = (bf16[2,128,512]{2,1,0:T(8,128)(2,1)S(1)}, bf16[2,128,512]{2,1,0:T(8,128)(2,1)S(1)}, u32[]{:S(2)}, u32[]{:S(2)}) collective-permute-start(bf16[2,128,512]{2,1,0:T(8,128)(2,1)S(1)} %get-tuple-element.55), channel_id=1, source_target_pairs={{0,2},{1,3},{2,0},{3,1},{4,6},{5,7},{6,4},{7,5},{8,10},{9,11},{10,... | collective-permute-start | bytes 786440 | tf_op jit(solution)/shard_map/ppermute | solution.py:58
  94.2 14.9 %collective-permute-start.26 = (bf16[2,128,512]{2,1,0:T(8,128)(2,1)S(1)}, bf16[2,128,512]{2,1,0:T(8,128)(2,1)S(1)}, u32[]{:S(2)}, u32[]{:S(2)}) collective-permute-start(bf16[2,128,512]{2,1,0:T(8,128)(2,1)S(1)} %get-tuple-element.56), channel_id=1, source_target_pairs={{0,7},{1,6},{2,5},{3,4},{4,3},{5,2},{6,1},{7,0},{8,15},{9,14},{10,... | collective-permute-start | bytes 786440 | tf_op jit(solution)/shard_map/ppermute | solution.py:58
  97.1 16.2 %collective-permute-start.28 = (bf16[1,128,512]{2,1,0:T(8,128)(2,1)S(1)}, bf16[1,128,512]{2,1,0:T(8,128)(2,1)S(1)}, u32[]{:S(2)}, u32[]{:S(2)}) collective-permute-start(bf16[1,128,512]{2,1,0:T(8,128)(2,1)S(1)} %get-tuple-element.57), channel_id=1, source_target_pairs={{0,1},{1,0},{2,3},{3,2},{4,5},{5,4},{6,7},{7,6},{8,9},{9,8},{10,11... | collective-permute-start | bytes 393224 | tf_op jit(solution)/shard_map/ppermute | solution.py:58
  98.1 21.2 %collective-permute-start.29 = (bf16[1,128,512]{2,1,0:T(8,128)(2,1)S(1)}, bf16[1,128,512]{2,1,0:T(8,128)(2,1)S(1)}, u32[]{:S(2)}, u32[]{:S(2)}) collective-permute-start(bf16[1,128,512]{2,1,0:T(8,128)(2,1)S(1)} %get-tuple-element.58), channel_id=1, source_target_pairs={{0,3},{1,2},{2,1},{3,0},{4,7},{5,6},{6,5},{7,4},{8,11},{9,10},{10,... | collective-permute-start | bytes 393224 | tf_op jit(solution)/shard_map/ppermute | solution.py:58
  101.9 17.5 %collective-permute-start.30 = (bf16[1,128,512]{2,1,0:T(8,128)(2,1)S(1)}, bf16[1,128,512]{2,1,0:T(8,128)(2,1)S(1)}, u32[]{:S(2)}, u32[]{:S(2)}) collective-permute-start(bf16[1,128,512]{2,1,0:T(8,128)(2,1)S(1)} %get-tuple-element.59), channel_id=1, source_target_pairs={{0,6},{1,7},{2,4},{3,5},{4,2},{5,3},{6,0},{7,1},{8,14},{9,15},{10,... | collective-permute-start | bytes 393224 | tf_op jit(solution)/shard_map/ppermute | solution.py:58
  109.1 10.2 %collective-permute-start.25 = (bf16[1,128,512]{2,1,0:T(8,128)(2,1)S(1)}, bf16[1,128,512]{2,1,0:T(8,128)(2,1)S(1)}, u32[]{:S(2)}, u32[]{:S(2)}) collective-permute-start(bf16[1,128,512]{2,1,0:T(8,128)(2,1)S(1)} %slice.38), channel_id=1, source_target_pairs={{0,6},{1,7},{2,4},{3,5},{4,2},{5,3},{6,0},{7,1},{8,14},{9,15},{10,... | collective-permute-start | bytes 393224 | tf_op jit(solution)/shard_map/ppermute | solution.py:58
  109.1 10.5 %collective-permute-start.27 = (bf16[1,128,512]{2,1,0:T(8,128)(2,1)S(1)}, bf16[1,128,512]{2,1,0:T(8,128)(2,1)S(1)}, u32[]{:S(2)}, u32[]{:S(2)}) collective-permute-start(bf16[1,128,512]{2,1,0:T(8,128)(2,1)S(1)} %slice.39), channel_id=1, source_target_pairs={{0,2},{1,3},{2,0},{3,1},{4,6},{5,7},{6,4},{7,5},{8,10},{9,11},{10,... | collective-permute-start | bytes 393224 | tf_op jit(solution)/shard_map/ppermute | solution.py:58
  113.2 28.4 %collective-permute-start.33 = (bf16[1024,512]{1,0:T(8,128)(2,1)S(1)}, bf16[1024,512]{1,0:T(8,128)(2,1)S(1)}, u32[]{:S(2)}, u32[]{:S(2)}) collective-permute-start(bf16[1024,512]{1,0:T(8,128)(2,1)S(1)} %get-tuple-element.61), channel_id=1, source_target_pairs={{24,0},{0,8},{8,16},{16,24},{25,1},{1,9},{9,17},{17,25},{26,2},{2,... | collective-permute-start | bytes 3145736 | tf_op jit(solution)/shard_map/ppermute | solution.py:255
  119.3 44.8 %collective-permute-start.32 = (bf16[1024,512]{1,0:T(8,128)(2,1)S(1)}, bf16[1024,512]{1,0:T(8,128)(2,1)S(1)}, u32[]{:S(2)}, u32[]{:S(2)}) collective-permute-start(bf16[1024,512]{1,0:T(8,128)(2,1)S(1)} %get-tuple-element.60), channel_id=1, source_target_pairs={{16,0},{24,8},{0,16},{8,24},{17,1},{25,9},{1,17},{9,25},{18,2},{26... | collective-permute-start | bytes 3145736 | tf_op jit(solution)/shard_map/ppermute | solution.py:255
  122.4 42.8 %collective-permute-start.31 = (bf16[1024,512]{1,0:T(8,128)(2,1)S(1)}, bf16[1024,512]{1,0:T(8,128)(2,1)S(1)}, u32[]{:S(2)}, u32[]{:S(2)}) collective-permute-start(bf16[1024,512]{1,0:T(8,128)(2,1)S(1)} %shard_map.91), channel_id=1, source_target_pairs={{8,0},{16,8},{24,16},{0,24},{9,1},{17,9},{25,17},{1,25},{10,2},{18... | collective-permute-start | bytes 3145736 | tf_op jit(solution)/shard_map/ppermute | solution.py:255
  (6 other events, 19.8 us)

commit v3 on v2

--- a/solution.py
+++ b/solution.py
@@ -6,12 +6,12 @@
 from jax.sharding import PartitionSpec as P
 
 STEPS = 4
-TILE = 256
+TILE = 512
 
 teleport = 0.2
 strength = 1.5
 
-PART, SOURCE, STARTS, WRAPPED, IDS = 0, 1, 2, 2 + STEPS, 2 + 2 * STEPS
+PART, STARTS, IDS = 0, 1, 1 + STEPS
 
 VMEM = pl.BlockSpec(memory_space=pltpu.VMEM)
 SMEM = pl.BlockSpec(memory_space=pltpu.SMEM)
@@ -58,15 +58,12 @@
     return lax.ppermute(value, "dom", [(i, i ^ offset) for i in range(parts)])
 
 
-def exchanged(sent, parts):
+def passed_on(got, parts):
     hops = relays(parts)
     arrays, offsets = [], []
-    for (hop, carried), value in zip(bundles(parts), sent):
-        got = swapped(value, hop)
-        arrays.append(got)
-        offsets.append(hop)
+    for (_, carried), value in zip(bundles(parts), got):
         for place, k in enumerate(carried[1:], 1):
-            arrays.append(swapped(got[place : place + 1], hops[k][1]))
+            arrays.append(swapped(value[place : place + 1], hops[k][1]))
             offsets.append(k)
     return arrays, offsets
 
@@ -83,23 +80,28 @@
     return [pltpu.VMEM((len(carried), block, width), dtype) for _, carried in bundles(parts)]
 
 
-def first_kernel(parts, info, current, x, *rest):
-    sent, sem = rest[:-1], rest[-1]
-    run([pltpu.make_async_copy(current, x, sem)])
+def first_kernel(parts, info, current, carried, x, h0, *rest):
+    sent, sems = rest[:-1], rest[-1]
+    spans = [slice(at, at + TILE) for at in range(0, x.shape[0], TILE)]
+    copies = [pltpu.make_async_copy(current.at[rows], x.at[rows], sems.at[at]) for at, rows in enumerate(spans)]
+    anchor = pltpu.make_async_copy(carried, h0, sems.at[len(spans)])
+    run(copies)
+    anchor.start()
     pick(info, x, sent, parts)
-
-
-def first(info, current, parts, block):
-    shapes = [pltpu.VMEM(current.shape, current.dtype)]
+    anchor.wait()
+
+
+def first(info, current, carried, parts, block):
+    shapes = [pltpu.VMEM(current.shape, current.dtype)] * 2
     shapes += sent_shapes(parts, block, current.shape[1], current.dtype)
     return pl.pallas_call(
         lambda *refs: first_kernel(parts, *refs),
         out_shape=shapes,
-        in_specs=[SMEM, HBM],
+        in_specs=[SMEM, HBM, HBM],
         out_specs=[VMEM] * len(shapes),
-        scratch_shapes=[pltpu.SemaphoreType.DMA],
-        compiler_params=LIMIT,
-    )(info, far(current))
+        scratch_shapes=[pltpu.SemaphoreType.DMA((current.shape[0] // TILE + 1,))],
+        compiler_params=LIMIT,
+    )(info, far(current), far(carried))
 
 
 def merge_kernel(info, col, counts, adj, own, other, fetched, total, sems):
@@ -151,37 +153,28 @@
     )(info, col, counts, far(adj))
 
 
-def own_kernel(step, info, x, carried, new_h0, adj, partial, h0, sem):
-    @pl.when(info[WRAPPED + step] == 1)
-    def _():
-        run([pltpu.make_async_copy(new_h0.at[info[SOURCE]], h0, sem)])
-
-    @pl.when(info[WRAPPED + step] == 0)
-    def _():
-        run([pltpu.make_async_copy(carried, h0, sem)])
-
+def own_kernel(x, h0, adj, partial):
     for at in range(0, x.shape[0], TILE):
         rows = slice(at, at + TILE)
         agg = jnp.dot(adj[rows], x[...], preferred_element_type=jnp.float32)
         partial[rows] = (1.0 - teleport) * agg + teleport * h0[rows].astype(jnp.float32)
 
 
-def own_part(step, info, x, carried, new_h0, adj):
-    return pl.pallas_call(
-        lambda *refs: own_kernel(step, *refs),
+def own_part(x, h0, adj):
+    return pl.pallas_call(
+        own_kernel,
         out_shape=pltpu.VMEM(x.shape, jnp.float32),
-        in_specs=[SMEM, VMEM, HBM, HBM, VMEM],
+        in_specs=[VMEM, VMEM, VMEM],
         out_specs=VMEM,
-        scratch_shapes=[pltpu.VMEM(x.shape, x.dtype), pltpu.SemaphoreType.DMA],
-        compiler_params=LIMIT,
-    )(info, fast(x), far(carried), far(new_h0), fast(adj))
-
-
-def layer_kernel(step, parts, offsets, info, beta, adj, partial, weight, new_h0, *rest):
+        compiler_params=LIMIT,
+    )(fast(x), fast(h0), fast(adj))
+
+
+def layer_kernel(step, parts, offsets, info, beta, adj, partial, weight, new_h0, h0, *rest):
     incoming, rest = rest[: len(offsets)], rest[len(offsets) :]
     block = incoming[0].shape[1]
     more = step < STEPS - 1
-    out, following, sent = rest[0], rest[1], rest[2 : 2 + len(bundles(parts))]
+    out, following, anchor, sent = rest[0], rest[1], rest[2], rest[3 : 3 + len(bundles(parts))]
     table, sem = rest[-2:]
     if more:
         fresh = pltpu.make_async_copy(new_h0.at[step], following, sem)
@@ -206,6 +199,7 @@
     @pl.when(info[STARTS + step + 1] == 1)
     def _():
         fresh.wait()
+        anchor[...] = following[...]
 
     @pl.when(info[STARTS + step + 1] == 0)
     def _():
@@ -214,21 +208,22 @@
     pick(info, following, sent, parts)
 
 
-def layer(step, parts, info, beta, adj, partial, weight, new_h0, incoming, offsets):
+def layer(step, parts, info, beta, adj, partial, weight, new_h0, h0, incoming, offsets):
     _, block, width = incoming[0].shape
     made = pltpu.VMEM(partial.shape, incoming[0].dtype)
     shapes = [made]
     if step < STEPS - 1:
-        shapes += [made] + sent_shapes(parts, block, width, made.dtype)
+        shapes += [made, made] + sent_shapes(parts, block, width, made.dtype)
     scratch = [pltpu.VMEM(((parts - 1) * block, width), made.dtype), pltpu.SemaphoreType.DMA]
     return pl.pallas_call(
         lambda *refs: layer_kernel(step, parts, offsets, *refs),
         out_shape=shapes,
-        in_specs=[SMEM, SMEM, VMEM, VMEM, VMEM, HBM] + [VMEM] * len(incoming),
+        in_specs=[SMEM, SMEM, VMEM, VMEM, VMEM, HBM, VMEM] + [VMEM] * len(incoming),
         out_specs=[VMEM] * len(shapes),
         scratch_shapes=scratch,
-        compiler_params=LIMIT,
-    )(info, beta, fast(adj), fast(partial), fast(weight), far(new_h0), *[fast(value) for value in incoming])
+        input_output_aliases={6: 2} if step < STEPS - 1 else {},
+        compiler_params=LIMIT,
+    )(info, beta, fast(adj), fast(partial), fast(weight), far(new_h0), fast(h0), *[fast(value) for value in incoming])
 
 
 def keep_kernel(step, value, *rest):
@@ -264,30 +259,45 @@
     place = section + jnp.arange(STEPS, dtype=jnp.int32)
     layers = place % sections
     beta = jnp.log(1.0 + strength / (layers.astype(jnp.float32) + 1.0))
-    source = jnp.clip(sections - section - 1, 0, new_h0.shape[0] - 1)
     info = jnp.concatenate(
         [
-            jnp.stack([part, source]).astype(jnp.int32),
+            jnp.stack([part]).astype(jnp.int32),
             (place == sections).astype(jnp.int32),
-            (place >= sections).astype(jnp.int32),
             lax.dynamic_index_in_dim(send_list, part, 0, keepdims=False),
         ]
     )
-    current, *sent = first(info, carry_h[0], parts, block)
-    layer_weights = [moved(weights[0], t) for t in range(STEPS)]
-    own_adj = None
+    current, h0, *sent = first(info, carry_h[0], carry_h0[0], parts, block)
+    hops = [hop for hop, _ in bundles(parts)]
+    weight = weights[0]
+    coming = {}
+    moving = {}
+    for t in range(STEPS):
+        got = [swapped(value, hop) for value, hop in zip(sent, hops)]
+        if t == 0:
+            counts, current = lax.optimization_barrier((counts, current))
+            own_adj, other_adj = merged(info, col_index, counts, adj_blocks, parts)
+        if t == 3:
+            current, moving[1] = lax.optimization_barrier((current, moving[1]))
+        partial = own_part(current, h0, own_adj)
+        passing = sum(len(carried) > 1 for _, carried in bundles(parts))
+        early, partial = lax.optimization_barrier((got[:passing], partial))
+        got = early + got[passing:]
+        passed, offsets = passed_on(got, parts)
+        if t + 1 < STEPS:
+            held_back, early, partial = lax.optimization_barrier((weights[0], early, partial))
+            coming[t + 1] = moved(held_back, t + 1)
+        if t > 0:
+            moving[t - 1] = moved(made, 1 - t)
+            if t == 3:
+                partial, moving[t - 1] = lax.optimization_barrier((partial, moving[t - 1]))
+        made, *rest = layer(t, parts, info, beta, other_adj, partial, weight, new_h0, h0, got + passed, hops + offsets)
+        if rest:
+            current, h0, *sent = rest
+            weight = coming[t + 1]
+    moving[STEPS - 1] = moved(made, 1 - STEPS)
     held = None
     for t in range(STEPS):
-        incoming, offsets = exchanged(sent, parts)
-        if own_adj is None:
-            own_adj, other_adj = merged(info, col_index, counts, adj_blocks, parts)
-        partial = own_part(t, info, current, carry_h0[0], new_h0, own_adj)
-        made, *rest = layer(
-            t, parts, info, beta, other_adj, partial, layer_weights[t], new_h0, incoming, offsets
-        )
-        if rest:
-            current, *sent = rest
-        held = kept(t, moved(made, -t), held)
+        held = kept(t, moving[t], held)
     return held
 
 

time: 169 us -> 142 us (0.84)
  waiting for transfers between devices: 70.2 us -> 52.7 us
  Pallas kernels: 36.9 us -> 29.4 us
    ppermute x6, waiting for transfers between devices: 38.6 us -> 16.6 us  [moved(): lax.ppermute(value, 'section', [((i + by) % length, i) for i in range(len...]
    pallas_call x4, Pallas kernels: 12.5 us -> 5.09 us  [own_part(): pl.pallas_call(own_kernel, out_shape=pltpu.VMEM(x.shape, jnp.float32), in...]
    ppermute x28, waiting for transfers between devices: 31.6 us -> 36.2 us  [swapped(): return lax.ppermute(value, 'dom', [(i, i ^ offset) for i in range(parts)])]
  transfers between devices with their start and end apart: 34 -> 34, of which waited for: 14 -> 15; matrix products, arithmetic and copies ran while one was open for 0% -> 0% of each run, Pallas kernels for 21% -> 16%
where the time goes in v3:
time: 142 us; the launch traced here: 141 us
  starting transfers between devices  56.1 us (40%)
  waiting for transfers between devices  52.7 us (37%)
  Pallas kernels  29.4 us (21%)
  local copies, waits for them, and re-layouts  2.11 us (1%)
    ppermute x28, waiting for transfers between devices, swapped(): return lax.ppermute(value, 'dom', [(i, i ^ offset) for i in range(parts)])  36.2 us
    ppermute x28, starting transfers between devices, swapped(): return lax.ppermute(value, 'dom', [(i, i ^ offset) for i in range(parts)])  35.7 us
    ppermute x6, starting transfers between devices, moved(): lax.ppermute(value, 'section', [((i + by) % length, i) for i in range(len...  20.4 us
    ppermute x6, waiting for transfers between devices, moved(): lax.ppermute(value, 'section', [((i + by) % length, i) for i in range(len...  16.6 us
    pallas_call x4, Pallas kernels, layer(): pl.pallas_call(lambda *refs: layer_kernel(step, parts, offsets, *refs), o...  10.8 us
    pallas_call x1, Pallas kernels, merged(): pl.pallas_call(merge_kernel, out_shape=[pltpu.VMEM((rows * block, rows *...  6.6 us
    pallas_call x4, Pallas kernels, own_part(): pl.pallas_call(own_kernel, out_shape=pltpu.VMEM(x.shape, jnp.float32), in...  5.09 us
    pallas_call x4, Pallas kernels, kept(): pl.pallas_call(lambda *refs: keep_kernel(step, *refs), out_shape=pltpu.HB...  3.92 us
  transfers between devices with their start and end apart: 34, of which 15 were waited for; matrix products, arithmetic and copies ran while one was open for 0% of the time, Pallas kernels for 16%

profile of v3, /device:TPU:1, one launch (start us, length us, event | category | flops | bytes accessed | tf_op | source)
XLA Modules:
  0.0 140.8 jit_solution(2842642655557483746)
XLA Ops:
  0.8 3.0 %shard_map.82 = (bf16[1024,512]{1,0:T(8,128)(2,1)S(1)}, bf16[1024,512]{1,0:T(8,128)(2,1)S(1)}, bf16[2,128,512]{2,1,0:T(8,128)(2,1)S(1)}, bf16[2,128,512]{2,1,0:T...) custom-call(s32[13]{0:T(128)S(1)} %pad_add_fusion.refs_0_.info, ...), custom_call_target="tpu_custom_call" | custom-call | tf_op jit(solution)/shard_map/pallas_call | solution.py:97
  3.8 2.2 %collective-permute-start = (bf16[2,128,512]{2,1,0:T(8,128)(2,1)S(1)}, bf16[2,128,512]{2,1,0:T(8,128)(2,1)S(1)}, u32[]{:S(2)}, u32[]{:S(2)}) collective-permute-start(bf16[2,128,512]{2,1,0:T(8,128)(2,1)S(1)} %get-tuple-element.65), channel_id=1, source_target_pairs={{0,2},{1,3},{2,0},{3,1},{4,6},{5,7},{6,4},{7,5},{8,10},{9,11},{10,... | collective-permute-start | bytes 786440 | tf_op jit(solution)/shard_map/ppermute | solution.py:58
  6.0 3.1 %collective-permute-start.1 = (bf16[2,128,512]{2,1,0:T(8,128)(2,1)S(1)}, bf16[2,128,512]{2,1,0:T(8,128)(2,1)S(1)}, u32[]{:S(2)}, u32[]{:S(2)}) collective-permute-start(bf16[2,128,512]{2,1,0:T(8,128)(2,1)S(1)} %get-tuple-element.66), channel_id=1, source_target_pairs={{0,7},{1,6},{2,5},{3,4},{4,3},{5,2},{6,1},{7,0},{8,15},{9,14},{10,... | collective-permute-start | bytes 786440 | tf_op jit(solution)/shard_map/ppermute | solution.py:58
  12.0 6.6 %shard_map.83 = (bf16[1024,1024]{1,0:T(8,128)(2,1)S(1)}, bf16[1024,896]{1,0:T(8,128)(2,1)S(1)}) custom-call(s32[13]{0:T(128)S(1)} %pad_add_fusion.refs_0_.info, s32[8,24]{1,0:T(8,128)S(1)} %copy-done.2, s32[8]{0:T(128)S(1)} %copy-done.3, bf16[8,24,128,128]{3,2,1,0:T(8,128)(2,1)} %adj.1), custom_call_target="tpu_custom_call" | custom-call | tf_op jit(solution)/shard_map/pallas_call | solution.py:139
  21.4 2.2 %collective-permute-start.5 = (bf16[1,128,512]{2,1,0:T(8,128)(2,1)S(1)}, bf16[1,128,512]{2,1,0:T(8,128)(2,1)S(1)}, u32[]{:S(2)}, u32[]{:S(2)}) collective-permute-start(bf16[1,128,512]{2,1,0:T(8,128)(2,1)S(1)} %slice.24), channel_id=1, source_target_pairs={{0,6},{1,7},{2,4},{3,5},{4,2},{5,3},{6,0},{7,1},{8,14},{9,15},{10,... | collective-permute-start | bytes 393224 | tf_op jit(solution)/shard_map/ppermute | solution.py:58
  23.6 4.3 %collective-permute-start.9 = (bf16[512,512]{1,0:T(8,128)(2,1)S(1)}, bf16[512,512]{1,0:T(8,128)(2,1)S(1)}, u32[]{:S(2)}, u32[]{:S(2)}) collective-permute-start(bf16[512,512]{1,0:T(8,128)(2,1)S(1)} %bitcast.6), channel_id=1, source_target_pairs={{8,0},{16,8},{24,16},{0,24},{9,1},{17,9},{25,17},{1,25},{10,2},{18... | collective-permute-start | bytes 1572872 | tf_op jit(solution)/shard_map/ppermute | solution.py:250
  28.9 2.5 %shard_map.85 = (bf16[1024,512]{1,0:T(8,128)(2,1)S(1)}, bf16[1024,512]{1,0:T(8,128)(2,1)S(1)}, bf16[1024,512]{1,0:T(8,128)(2,1)S(1)}, bf16[2,128,512]{2,1,0:T(8,...) custom-call(s32[13]{0:T(128)S(1)} %pad_add_fusion.refs_0_.info, ...), custom_call_target="tpu_custom_call", output_to_operand_aliasing={{2}: (6, {})} | custom-call | tf_op jit(solution)/shard_map/pallas_call | solution.py:218
  32.3 2.7 %collective-permute-start.8 = (bf16[2,128,512]{2,1,0:T(8,128)(2,1)S(1)}, bf16[2,128,512]{2,1,0:T(8,128)(2,1)S(1)}, u32[]{:S(2)}, u32[]{:S(2)}) collective-permute-start(bf16[2,128,512]{2,1,0:T(8,128)(2,1)S(1)} %get-tuple-element.78), channel_id=1, source_target_pairs={{0,7},{1,6},{2,5},{3,4},{4,3},{5,2},{6,1},{7,0},{8,15},{9,14},{10,... | collective-permute-start | bytes 786440 | tf_op jit(solution)/shard_map/ppermute | solution.py:58
  35.0 1.6 %collective-permute-start.10 = (bf16[1,128,512]{2,1,0:T(8,128)(2,1)S(1)}, bf16[1,128,512]{2,1,0:T(8,128)(2,1)S(1)}, u32[]{:S(2)}, u32[]{:S(2)}) collective-permute-start(bf16[1,128,512]{2,1,0:T(8,128)(2,1)S(1)} %get-tuple-element.86), channel_id=1, source_target_pairs={{0,1},{1,0},{2,3},{3,2},{4,5},{5,4},{6,7},{7,6},{8,9},{9,8},{10,11... | collective-permute-start | bytes 393224 | tf_op jit(solution)/shard_map/ppermute | solution.py:58
  39.4 3.0 %collective-permute-done.8.refs_8_ = bf16[2,128,512]{2,1,0:T(8,128)(2,1)S(1)} collective-permute-done((bf16[2,128,512]{2,1,0:T(8,128)(2,1)S(1)}, bf16[2,128,512]{2,1,0:T(8,128)(2,1)S(1)}, u32[]{:S(2)}, u32[]{:S(2)}) %collective-permute-start.8) | collective-permute-done | bytes 262176 | tf_op jit(solution)/shard_map/ppermute | solution.py:58
  42.5 2.6 %collective-permute-start.13 = (bf16[1,128,512]{2,1,0:T(8,128)(2,1)S(1)}, bf16[1,128,512]{2,1,0:T(8,128)(2,1)S(1)}, u32[]{:S(2)}, u32[]{:S(2)}) collective-permute-start(bf16[1,128,512]{2,1,0:T(8,128)(2,1)S(1)} %slice.26), channel_id=1, source_target_pairs={{0,6},{1,7},{2,4},{3,5},{4,2},{5,3},{6,0},{7,1},{8,14},{9,15},{10,... | collective-permute-start | bytes 393224 | tf_op jit(solution)/shard_map/ppermute | solution.py:58
  45.2 2.0 %collective-permute-start.17 = (bf16[512,512]{1,0:T(8,128)(2,1)S(1)}, bf16[512,512]{1,0:T(8,128)(2,1)S(1)}, u32[]{:S(2)}, u32[]{:S(2)}) collective-permute-start(bf16[512,512]{1,0:T(8,128)(2,1)S(1)} %bitcast.8), channel_id=1, source_target_pairs={{16,0},{24,8},{0,16},{8,24},{17,1},{25,9},{1,17},{9,25},{18,2},{26... | collective-permute-start | bytes 1572872 | tf_op jit(solution)/shard_map/ppermute | solution.py:250
  47.2 2.6 %collective-permute-done.12.refs_11_ = bf16[1,128,512]{2,1,0:T(8,128)(2,1)S(1)} collective-permute-done((bf16[1,128,512]{2,1,0:T(8,128)(2,1)S(1)}, bf16[1,128,512]{2,1,0:T(8,128)(2,1)S(1)}, u32[]{:S(2)}, u32[]{:S(2)}) %collective-permute-start.12) | collective-permute-done | bytes 131104 | tf_op jit(solution)/shard_map/ppermute | solution.py:58
  49.8 2.5 %collective-permute-done.14.refs_13_ = bf16[1,128,512]{2,1,0:T(8,128)(2,1)S(1)} collective-permute-done((bf16[1,128,512]{2,1,0:T(8,128)(2,1)S(1)}, bf16[1,128,512]{2,1,0:T(8,128)(2,1)S(1)}, u32[]{:S(2)}, u32[]{:S(2)}) %collective-permute-start.14) | collective-permute-done | bytes 131104 | tf_op jit(solution)/shard_map/ppermute | solution.py:58
  52.2 3.2 %collective-permute-done.13.refs_12_ = bf16[1,128,512]{2,1,0:T(8,128)(2,1)S(1)} collective-permute-done((bf16[1,128,512]{2,1,0:T(8,128)(2,1)S(1)}, bf16[1,128,512]{2,1,0:T(8,128)(2,1)S(1)}, u32[]{:S(2)}, u32[]{:S(2)}) %collective-permute-start.13) | collective-permute-done | bytes 131104 | tf_op jit(solution)/shard_map/ppermute | solution.py:58
  55.4 2.5 %shard_map.87 = (bf16[1024,512]{1,0:T(8,128)(2,1)S(1)}, bf16[1024,512]{1,0:T(8,128)(2,1)S(1)}, bf16[1024,512]{1,0:T(8,128)(2,1)S(1)}, bf16[2,128,512]{2,1,0:T(8,...) custom-call(s32[13]{0:T(128)S(1)} %pad_add_fusion.refs_0_.info, ...), custom_call_target="tpu_custom_call", output_to_operand_aliasing={{2}: (6, {})} | custom-call | tf_op jit(solution)/shard_map/pallas_call | solution.py:218
  58.0 2.7 %collective-permute-start.16 = (bf16[2,128,512]{2,1,0:T(8,128)(2,1)S(1)}, bf16[2,128,512]{2,1,0:T(8,128)(2,1)S(1)}, u32[]{:S(2)}, u32[]{:S(2)}) collective-permute-start(bf16[2,128,512]{2,1,0:T(8,128)(2,1)S(1)} %get-tuple-element.90), channel_id=1, source_target_pairs={{0,7},{1,6},{2,5},{3,4},{4,3},{5,2},{6,1},{7,0},{8,15},{9,14},{10,... | collective-permute-start | bytes 786440 | tf_op jit(solution)/shard_map/ppermute | solution.py:58
  64.2 4.3 %collective-permute-done.16.refs_8_ = bf16[2,128,512]{2,1,0:T(8,128)(2,1)S(1)} collective-permute-done((bf16[2,128,512]{2,1,0:T(8,128)(2,1)S(1)}, bf16[2,128,512]{2,1,0:T(8,128)(2,1)S(1)}, u32[]{:S(2)}, u32[]{:S(2)}) %collective-permute-start.16) | collective-permute-done | bytes 262176 | tf_op jit(solution)/shard_map/ppermute | solution.py:58
  68.5 11.2 %collective-permute-start.25 = (bf16[1024,512]{1,0:T(8,128)(2,1)S(1)}, bf16[1024,512]{1,0:T(8,128)(2,1)S(1)}, u32[]{:S(2)}, u32[]{:S(2)}) collective-permute-start(bf16[1024,512]{1,0:T(8,128)(2,1)S(1)} %get-tuple-element.104), channel_id=1, source_target_pairs={{24,0},{0,8},{8,16},{16,24},{25,1},{1,9},{9,17},{17,25},{26,2},{2,... | collective-permute-start | bytes 3145736 | tf_op jit(solution)/shard_map/ppermute | solution.py:250
  81.7 6.3 %collective-permute-done.22.refs_13_ = bf16[1,128,512]{2,1,0:T(8,128)(2,1)S(1)} collective-permute-done((bf16[1,128,512]{2,1,0:T(8,128)(2,1)S(1)}, bf16[1,128,512]{2,1,0:T(8,128)(2,1)S(1)}, u32[]{:S(2)}, u32[]{:S(2)}) %collective-permute-start.22) | collective-permute-done | bytes 131104 | tf_op jit(solution)/shard_map/ppermute | solution.py:58
  88.0 3.3 %shard_map.89 = (bf16[1024,512]{1,0:T(8,128)(2,1)S(1)}, bf16[1024,512]{1,0:T(8,128)(2,1)S(1)}, bf16[1024,512]{1,0:T(8,128)(2,1)S(1)}, bf16[2,128,512]{2,1,0:T(8,...) custom-call(s32[13]{0:T(128)S(1)} %pad_add_fusion.refs_0_.info, ...), custom_call_target="tpu_custom_call", output_to_operand_aliasing={{2}: (6, {})} | custom-call | tf_op jit(solution)/shard_map/pallas_call | solution.py:218
  94.2 3.4 %collective-permute-start.24 = (bf16[2,128,512]{2,1,0:T(8,128)(2,1)S(1)}, bf16[2,128,512]{2,1,0:T(8,128)(2,1)S(1)}, u32[]{:S(2)}, u32[]{:S(2)}) collective-permute-start(bf16[2,128,512]{2,1,0:T(8,128)(2,1)S(1)} %get-tuple-element.102), channel_id=1, source_target_pairs={{0,7},{1,6},{2,5},{3,4},{4,3},{5,2},{6,1},{7,0},{8,15},{9,14},{10,... | collective-permute-start | bytes 786440 | tf_op jit(solution)/shard_map/ppermute | solution.py:58
  98.8 2.4 %collective-permute-done.23.refs_7_ = bf16[2,128,512]{2,1,0:T(8,128)(2,1)S(1)} collective-permute-done((bf16[2,128,512]{2,1,0:T(8,128)(2,1)S(1)}, bf16[2,128,512]{2,1,0:T(8,128)(2,1)S(1)}, u32[]{:S(2)}, u32[]{:S(2)}) %collective-permute-start.23) | collective-permute-done | bytes 262176 | tf_op jit(solution)/shard_map/ppermute | solution.py:58
  101.3 1.7 %collective-permute-start.29 = (bf16[1,128,512]{2,1,0:T(8,128)(2,1)S(1)}, bf16[1,128,512]{2,1,0:T(8,128)(2,1)S(1)}, u32[]{:S(2)}, u32[]{:S(2)}) collective-permute-start(bf16[1,128,512]{2,1,0:T(8,128)(2,1)S(1)} %get-tuple-element.114), channel_id=1, source_target_pairs={{0,3},{1,2},{2,1},{3,0},{4,7},{5,6},{6,5},{7,4},{8,11},{9,10},{10,... | collective-permute-start | bytes 393224 | tf_op jit(solution)/shard_map/ppermute | solution.py:58
  103.0 6.7 %collective-permute-done.24.refs_8_ = bf16[2,128,512]{2,1,0:T(8,128)(2,1)S(1)} collective-permute-done((bf16[2,128,512]{2,1,0:T(8,128)(2,1)S(1)}, bf16[2,128,512]{2,1,0:T(8,128)(2,1)S(1)}, u32[]{:S(2)}, u32[]{:S(2)}) %collective-permute-start.24) | collective-permute-done | bytes 262176 | tf_op jit(solution)/shard_map/ppermute | solution.py:58
  110.6 1.5 %collective-permute-start.32 = (bf16[1,128,512]{2,1,0:T(8,128)(2,1)S(1)}, bf16[1,128,512]{2,1,0:T(8,128)(2,1)S(1)}, u32[]{:S(2)}, u32[]{:S(2)}) collective-permute-start(bf16[1,128,512]{2,1,0:T(8,128)(2,1)S(1)} %slice.31), channel_id=1, source_target_pairs={{0,2},{1,3},{2,0},{3,1},{4,6},{5,7},{6,4},{7,5},{8,10},{9,11},{10,... | collective-permute-start | bytes 393224 | tf_op jit(solution)/shard_map/ppermute | solution.py:58
  112.1 4.4 %collective-permute-done.26.refs_0_ = bf16[1024,512]{1,0:T(8,128)(2,1)S(1)} collective-permute-done((bf16[1024,512]{1,0:T(8,128)(2,1)S(1)}, bf16[1024,512]{1,0:T(8,128)(2,1)S(1)}, u32[]{:S(2)}, u32[]{:S(2)}) %collective-permute-start.26) | collective-permute-done | bytes 1048608 | tf_op jit(solution)/shard_map/ppermute | solution.py:250
  117.9 2.2 %collective-permute-done.27.refs_4_ = bf16[512,512]{1,0:T(8,128)(2,1)S(1)} collective-permute-done((bf16[512,512]{1,0:T(8,128)(2,1)S(1)}, bf16[512,512]{1,0:T(8,128)(2,1)S(1)}, u32[]{:S(2)}, u32[]{:S(2)}) %collective-permute-start.27) | collective-permute-done | bytes 524320 | tf_op jit(solution)/shard_map/ppermute | solution.py:250
  120.0 2.8 %collective-permute-done.31.refs_12_ = bf16[1,128,512]{2,1,0:T(8,128)(2,1)S(1)} collective-permute-done((bf16[1,128,512]{2,1,0:T(8,128)(2,1)S(1)}, bf16[1,128,512]{2,1,0:T(8,128)(2,1)S(1)}, u32[]{:S(2)}, u32[]{:S(2)}) %collective-permute-start.31) | collective-permute-done | bytes 131104 | tf_op jit(solution)/shard_map/ppermute | solution.py:58
  122.8 2.4 %shard_map.91 = bf16[1024,512]{1,0:T(8,128)(2,1)S(1)} custom-call(s32[13]{0:T(128)S(1)} %pad_add_fusion.refs_0_.info, f32[4]{0:T(128)S(1)} %fusion.4.refs_1_, bf16[1024,896]{1,0:T(8,128)(2,1)S(1)} %get-tuple-element.64.refs_2_, f32[1024,512]{1,0:T(8,128)S(1)} %shard_map.90.refs_3_, bf16[512,512]{1,0:T(8,128)(2,1)S(1)} %collective-permute-done.27.refs_4_, ...), custom_call_target="tpu_custom_call" | custom-call | tf_op jit(solution)/shard_map/pallas_call | solution.py:218
  125.2 1.6 %collective-permute-start.33 = (bf16[1024,512]{1,0:T(8,128)(2,1)S(1)}, bf16[1024,512]{1,0:T(8,128)(2,1)S(1)}, u32[]{:S(2)}, u32[]{:S(2)}) collective-permute-start(bf16[1024,512]{1,0:T(8,128)(2,1)S(1)} %shard_map.91), channel_id=1, source_target_pairs={{8,0},{16,8},{24,16},{0,24},{9,1},{17,9},{25,17},{1,25},{10,2},{18... | collective-permute-start | bytes 3145736 | tf_op jit(solution)/shard_map/ppermute | solution.py:250
  129.7 10.0 %collective-permute-done.33.refs_0_ = bf16[1024,512]{1,0:T(8,128)(2,1)S(1)} collective-permute-done((bf16[1024,512]{1,0:T(8,128)(2,1)S(1)}, bf16[1024,512]{1,0:T(8,128)(2,1)S(1)}, u32[]{:S(2)}, u32[]{:S(2)}) %collective-permute-start.33) | collective-permute-done | bytes 1048608 | tf_op jit(solution)/shard_map/ppermute | solution.py:250
  (70 shorter events, 26.9 us)
Async XLA Ops:
  3.8 16.2 %collective-permute-start = (bf16[2,128,512]{2,1,0:T(8,128)(2,1)S(1)}, bf16[2,128,512]{2,1,0:T(8,128)(2,1)S(1)}, u32[]{:S(2)}, u32[]{:S(2)}) collective-permute-start(bf16[2,128,512]{2,1,0:T(8,128)(2,1)S(1)} %get-tuple-element.65), channel_id=1, source_target_pairs={{0,2},{1,3},{2,0},{3,1},{4,6},{5,7},{6,4},{7,5},{8,10},{9,11},{10,... | collective-permute-start | bytes 786440 | tf_op jit(solution)/shard_map/ppermute | solution.py:58
  6.0 14.5 %collective-permute-start.1 = (bf16[2,128,512]{2,1,0:T(8,128)(2,1)S(1)}, bf16[2,128,512]{2,1,0:T(8,128)(2,1)S(1)}, u32[]{:S(2)}, u32[]{:S(2)}) collective-permute-start(bf16[2,128,512]{2,1,0:T(8,128)(2,1)S(1)} %get-tuple-element.66), channel_id=1, source_target_pairs={{0,7},{1,6},{2,5},{3,4},{4,3},{5,2},{6,1},{7,0},{8,15},{9,14},{10,... | collective-permute-start | bytes 786440 | tf_op jit(solution)/shard_map/ppermute | solution.py:58
  9.1 14.6 %collective-permute-start.2 = (bf16[1,128,512]{2,1,0:T(8,128)(2,1)S(1)}, bf16[1,128,512]{2,1,0:T(8,128)(2,1)S(1)}, u32[]{:S(2)}, u32[]{:S(2)}) collective-permute-start(bf16[1,128,512]{2,1,0:T(8,128)(2,1)S(1)} %get-tuple-element.74), channel_id=1, source_target_pairs={{0,1},{1,0},{2,3},{3,2},{4,5},{5,4},{6,7},{7,6},{8,9},{9,8},{10,11... | collective-permute-start | bytes 393224 | tf_op jit(solution)/shard_map/ppermute | solution.py:58
  9.3 18.6 %collective-permute-start.3 = (bf16[1,128,512]{2,1,0:T(8,128)(2,1)S(1)}, bf16[1,128,512]{2,1,0:T(8,128)(2,1)S(1)}, u32[]{:S(2)}, u32[]{:S(2)}) collective-permute-start(bf16[1,128,512]{2,1,0:T(8,128)(2,1)S(1)} %get-tuple-element.75), channel_id=1, source_target_pairs={{0,3},{1,2},{2,1},{3,0},{4,7},{5,6},{6,5},{7,4},{8,11},{9,10},{10,... | collective-permute-start | bytes 393224 | tf_op jit(solution)/shard_map/ppermute | solution.py:58
  10.7 17.3 %collective-permute-start.4 = (bf16[1,128,512]{2,1,0:T(8,128)(2,1)S(1)}, bf16[1,128,512]{2,1,0:T(8,128)(2,1)S(1)}, u32[]{:S(2)}, u32[]{:S(2)}) collective-permute-start(bf16[1,128,512]{2,1,0:T(8,128)(2,1)S(1)} %get-tuple-element.76), channel_id=1, source_target_pairs={{0,6},{1,7},{2,4},{3,5},{4,2},{5,3},{6,0},{7,1},{8,14},{9,15},{10,... | collective-permute-start | bytes 393224 | tf_op jit(solution)/shard_map/ppermute | solution.py:58
  20.5 7.5 %collective-permute-start.6 = (bf16[1,128,512]{2,1,0:T(8,128)(2,1)S(1)}, bf16[1,128,512]{2,1,0:T(8,128)(2,1)S(1)}, u32[]{:S(2)}, u32[]{:S(2)}) collective-permute-start(bf16[1,128,512]{2,1,0:T(8,128)(2,1)S(1)} %slice.25), channel_id=1, source_target_pairs={{0,2},{1,3},{2,0},{3,1},{4,6},{5,7},{6,4},{7,5},{8,10},{9,11},{10,... | collective-permute-start | bytes 393224 | tf_op jit(solution)/shard_map/ppermute | solution.py:58
  21.4 7.5 %collective-permute-start.5 = (bf16[1,128,512]{2,1,0:T(8,128)(2,1)S(1)}, bf16[1,128,512]{2,1,0:T(8,128)(2,1)S(1)}, u32[]{:S(2)}, u32[]{:S(2)}) collective-permute-start(bf16[1,128,512]{2,1,0:T(8,128)(2,1)S(1)} %slice.24), channel_id=1, source_target_pairs={{0,6},{1,7},{2,4},{3,5},{4,2},{5,3},{6,0},{7,1},{8,14},{9,15},{10,... | collective-permute-start | bytes 393224 | tf_op jit(solution)/shard_map/ppermute | solution.py:58
  23.6 26.1 %collective-permute-start.9 = (bf16[512,512]{1,0:T(8,128)(2,1)S(1)}, bf16[512,512]{1,0:T(8,128)(2,1)S(1)}, u32[]{:S(2)}, u32[]{:S(2)}) collective-permute-start(bf16[512,512]{1,0:T(8,128)(2,1)S(1)} %bitcast.6), channel_id=1, source_target_pairs={{8,0},{16,8},{24,16},{0,24},{9,1},{17,9},{25,17},{1,25},{10,2},{18... | collective-permute-start | bytes 1572872 | tf_op jit(solution)/shard_map/ppermute | solution.py:250
  31.5 6.5 %collective-permute-start.7 = (bf16[2,128,512]{2,1,0:T(8,128)(2,1)S(1)}, bf16[2,128,512]{2,1,0:T(8,128)(2,1)S(1)}, u32[]{:S(2)}, u32[]{:S(2)}) collective-permute-start(bf16[2,128,512]{2,1,0:T(8,128)(2,1)S(1)} %get-tuple-element.77), channel_id=1, source_target_pairs={{0,2},{1,3},{2,0},{3,1},{4,6},{5,7},{6,4},{7,5},{8,10},{9,11},{10,... | collective-permute-start | bytes 786440 | tf_op jit(solution)/shard_map/ppermute | solution.py:58
  32.3 10.1 %collective-permute-start.8 = (bf16[2,128,512]{2,1,0:T(8,128)(2,1)S(1)}, bf16[2,128,512]{2,1,0:T(8,128)(2,1)S(1)}, u32[]{:S(2)}, u32[]{:S(2)}) collective-permute-start(bf16[2,128,512]{2,1,0:T(8,128)(2,1)S(1)} %get-tuple-element.78), channel_id=1, source_target_pairs={{0,7},{1,6},{2,5},{3,4},{4,3},{5,2},{6,1},{7,0},{8,15},{9,14},{10,... | collective-permute-start | bytes 786440 | tf_op jit(solution)/shard_map/ppermute | solution.py:58
  35.0 7.5 %collective-permute-start.10 = (bf16[1,128,512]{2,1,0:T(8,128)(2,1)S(1)}, bf16[1,128,512]{2,1,0:T(8,128)(2,1)S(1)}, u32[]{:S(2)}, u32[]{:S(2)}) collective-permute-start(bf16[1,128,512]{2,1,0:T(8,128)(2,1)S(1)} %get-tuple-element.86), channel_id=1, source_target_pairs={{0,1},{1,0},{2,3},{3,2},{4,5},{5,4},{6,7},{7,6},{8,9},{9,8},{10,11... | collective-permute-start | bytes 393224 | tf_op jit(solution)/shard_map/ppermute | solution.py:58
  36.6 8.6 %collective-permute-start.11 = (bf16[1,128,512]{2,1,0:T(8,128)(2,1)S(1)}, bf16[1,128,512]{2,1,0:T(8,128)(2,1)S(1)}, u32[]{:S(2)}, u32[]{:S(2)}) collective-permute-start(bf16[1,128,512]{2,1,0:T(8,128)(2,1)S(1)} %get-tuple-element.87), channel_id=1, source_target_pairs={{0,3},{1,2},{2,1},{3,0},{4,7},{5,6},{6,5},{7,4},{8,11},{9,10},{10,... | collective-permute-start | bytes 393224 | tf_op jit(solution)/shard_map/ppermute | solution.py:58
  37.9 11.8 %collective-permute-start.12 = (bf16[1,128,512]{2,1,0:T(8,128)(2,1)S(1)}, bf16[1,128,512]{2,1,0:T(8,128)(2,1)S(1)}, u32[]{:S(2)}, u32[]{:S(2)}) collective-permute-start(bf16[1,128,512]{2,1,0:T(8,128)(2,1)S(1)} %get-tuple-element.88), channel_id=1, source_target_pairs={{0,6},{1,7},{2,4},{3,5},{4,2},{5,3},{6,0},{7,1},{8,14},{9,15},{10,... | collective-permute-start | bytes 393224 | tf_op jit(solution)/shard_map/ppermute | solution.py:58
  42.4 9.8 %collective-permute-start.14 = (bf16[1,128,512]{2,1,0:T(8,128)(2,1)S(1)}, bf16[1,128,512]{2,1,0:T(8,128)(2,1)S(1)}, u32[]{:S(2)}, u32[]{:S(2)}) collective-permute-start(bf16[1,128,512]{2,1,0:T(8,128)(2,1)S(1)} %slice.27), channel_id=1, source_target_pairs={{0,2},{1,3},{2,0},{3,1},{4,6},{5,7},{6,4},{7,5},{8,10},{9,11},{10,... | collective-permute-start | bytes 393224 | tf_op jit(solution)/shard_map/ppermute | solution.py:58
  42.5 12.9 %collective-permute-start.13 = (bf16[1,128,512]{2,1,0:T(8,128)(2,1)S(1)}, bf16[1,128,512]{2,1,0:T(8,128)(2,1)S(1)}, u32[]{:S(2)}, u32[]{:S(2)}) collective-permute-start(bf16[1,128,512]{2,1,0:T(8,128)(2,1)S(1)} %slice.26), channel_id=1, source_target_pairs={{0,6},{1,7},{2,4},{3,5},{4,2},{5,3},{6,0},{7,1},{8,14},{9,15},{10,... | collective-permute-start | bytes 393224 | tf_op jit(solution)/shard_map/ppermute | solution.py:58
  45.2 36.6 %collective-permute-start.17 = (bf16[512,512]{1,0:T(8,128)(2,1)S(1)}, bf16[512,512]{1,0:T(8,128)(2,1)S(1)}, u32[]{:S(2)}, u32[]{:S(2)}) collective-permute-start(bf16[512,512]{1,0:T(8,128)(2,1)S(1)} %bitcast.8), channel_id=1, source_target_pairs={{16,0},{24,8},{0,16},{8,24},{17,1},{25,9},{1,17},{9,25},{18,2},{26... | collective-permute-start | bytes 1572872 | tf_op jit(solution)/shard_map/ppermute | solution.py:250
  58.0 10.5 %collective-permute-start.16 = (bf16[2,128,512]{2,1,0:T(8,128)(2,1)S(1)}, bf16[2,128,512]{2,1,0:T(8,128)(2,1)S(1)}, u32[]{:S(2)}, u32[]{:S(2)}) collective-permute-start(bf16[2,128,512]{2,1,0:T(8,128)(2,1)S(1)} %get-tuple-element.90), channel_id=1, source_target_pairs={{0,7},{1,6},{2,5},{3,4},{4,3},{5,2},{6,1},{7,0},{8,15},{9,14},{10,... | collective-permute-start | bytes 786440 | tf_op jit(solution)/shard_map/ppermute | solution.py:58
  60.7 19.0 %collective-permute-start.18 = (bf16[1,128,512]{2,1,0:T(8,128)(2,1)S(1)}, bf16[1,128,512]{2,1,0:T(8,128)(2,1)S(1)}, u32[]{:S(2)}, u32[]{:S(2)}) collective-permute-start(bf16[1,128,512]{2,1,0:T(8,128)(2,1)S(1)} %get-tuple-element.98), channel_id=1, source_target_pairs={{0,1},{1,0},{2,3},{3,2},{4,5},{5,4},{6,7},{7,6},{8,9},{9,8},{10,11... | collective-permute-start | bytes 393224 | tf_op jit(solution)/shard_map/ppermute | solution.py:58
  61.3 19.5 %collective-permute-start.19 = (bf16[1,128,512]{2,1,0:T(8,128)(2,1)S(1)}, bf16[1,128,512]{2,1,0:T(8,128)(2,1)S(1)}, u32[]{:S(2)}, u32[]{:S(2)}) collective-permute-start(bf16[1,128,512]{2,1,0:T(8,128)(2,1)S(1)} %get-tuple-element.99), channel_id=1, source_target_pairs={{0,3},{1,2},{2,1},{3,0},{4,7},{5,6},{6,5},{7,4},{8,11},{9,10},{10,... | collective-permute-start | bytes 393224 | tf_op jit(solution)/shard_map/ppermute | solution.py:58
  63.5 18.2 %collective-permute-start.20 = (bf16[1,128,512]{2,1,0:T(8,128)(2,1)S(1)}, bf16[1,128,512]{2,1,0:T(8,128)(2,1)S(1)}, u32[]{:S(2)}, u32[]{:S(2)}) collective-permute-start(bf16[1,128,512]{2,1,0:T(8,128)(2,1)S(1)} %get-tuple-element.100), channel_id=1, source_target_pairs={{0,6},{1,7},{2,4},{3,5},{4,2},{5,3},{6,0},{7,1},{8,14},{9,15},{10,... | collective-permute-start | bytes 393224 | tf_op jit(solution)/shard_map/ppermute | solution.py:58
  68.5 29.1 %collective-permute-start.25 = (bf16[1024,512]{1,0:T(8,128)(2,1)S(1)}, bf16[1024,512]{1,0:T(8,128)(2,1)S(1)}, u32[]{:S(2)}, u32[]{:S(2)}) collective-permute-start(bf16[1024,512]{1,0:T(8,128)(2,1)S(1)} %get-tuple-element.104), channel_id=1, source_target_pairs={{24,0},{0,8},{8,16},{16,24},{25,1},{1,9},{9,17},{17,25},{26,2},{2,... | collective-permute-start | bytes 3145736 | tf_op jit(solution)/shard_map/ppermute | solution.py:250
  79.7 8.3 %collective-permute-start.22 = (bf16[1,128,512]{2,1,0:T(8,128)(2,1)S(1)}, bf16[1,128,512]{2,1,0:T(8,128)(2,1)S(1)}, u32[]{:S(2)}, u32[]{:S(2)}) collective-permute-start(bf16[1,128,512]{2,1,0:T(8,128)(2,1)S(1)} %slice.29), channel_id=1, source_target_pairs={{0,2},{1,3},{2,0},{3,1},{4,6},{5,7},{6,4},{7,5},{8,10},{9,11},{10,... | collective-permute-start | bytes 393224 | tf_op jit(solution)/shard_map/ppermute | solution.py:58
  80.8 7.2 %collective-permute-start.21 = (bf16[1,128,512]{2,1,0:T(8,128)(2,1)S(1)}, bf16[1,128,512]{2,1,0:T(8,128)(2,1)S(1)}, u32[]{:S(2)}, u32[]{:S(2)}) collective-permute-start(bf16[1,128,512]{2,1,0:T(8,128)(2,1)S(1)} %slice.28), channel_id=1, source_target_pairs={{0,6},{1,7},{2,4},{3,5},{4,2},{5,3},{6,0},{7,1},{8,14},{9,15},{10,... | collective-permute-start | bytes 393224 | tf_op jit(solution)/shard_map/ppermute | solution.py:58
  91.4 25.1 %collective-permute-start.26 = (bf16[1024,512]{1,0:T(8,128)(2,1)S(1)}, bf16[1024,512]{1,0:T(8,128)(2,1)S(1)}, u32[]{:S(2)}, u32[]{:S(2)}) collective-permute-start(bf16[1024,512]{1,0:T(8,128)(2,1)S(1)} %get-tuple-element.108), channel_id=1, source_target_pairs={{16,0},{24,8},{0,16},{8,24},{17,1},{25,9},{1,17},{9,25},{18,2},{26... | collective-permute-start | bytes 3145736 | tf_op jit(solution)/shard_map/ppermute | solution.py:250
  91.4 28.6 %collective-permute-start.27 = (bf16[512,512]{1,0:T(8,128)(2,1)S(1)}, bf16[512,512]{1,0:T(8,128)(2,1)S(1)}, u32[]{:S(2)}, u32[]{:S(2)}) collective-permute-start(bf16[512,512]{1,0:T(8,128)(2,1)S(1)} %bitcast.9), channel_id=1, source_target_pairs={{24,0},{0,8},{8,16},{16,24},{25,1},{1,9},{9,17},{17,25},{26,2},{2,... | collective-permute-start | bytes 1572872 | tf_op jit(solution)/shard_map/ppermute | solution.py:250
  92.7 8.6 %collective-permute-start.23 = (bf16[2,128,512]{2,1,0:T(8,128)(2,1)S(1)}, bf16[2,128,512]{2,1,0:T(8,128)(2,1)S(1)}, u32[]{:S(2)}, u32[]{:S(2)}) collective-permute-start(bf16[2,128,512]{2,1,0:T(8,128)(2,1)S(1)} %get-tuple-element.101), channel_id=1, source_target_pairs={{0,2},{1,3},{2,0},{3,1},{4,6},{5,7},{6,4},{7,5},{8,10},{9,11},{10,... | collective-permute-start | bytes 786440 | tf_op jit(solution)/shard_map/ppermute | solution.py:58
  94.2 15.5 %collective-permute-start.24 = (bf16[2,128,512]{2,1,0:T(8,128)(2,1)S(1)}, bf16[2,128,512]{2,1,0:T(8,128)(2,1)S(1)}, u32[]{:S(2)}, u32[]{:S(2)}) collective-permute-start(bf16[2,128,512]{2,1,0:T(8,128)(2,1)S(1)} %get-tuple-element.102), channel_id=1, source_target_pairs={{0,7},{1,6},{2,5},{3,4},{4,3},{5,2},{6,1},{7,0},{8,15},{9,14},{10,... | collective-permute-start | bytes 786440 | tf_op jit(solution)/shard_map/ppermute | solution.py:58
  97.6 13.0 %collective-permute-start.28 = (bf16[1,128,512]{2,1,0:T(8,128)(2,1)S(1)}, bf16[1,128,512]{2,1,0:T(8,128)(2,1)S(1)}, u32[]{:S(2)}, u32[]{:S(2)}) collective-permute-start(bf16[1,128,512]{2,1,0:T(8,128)(2,1)S(1)} %get-tuple-element.113), channel_id=1, source_target_pairs={{0,1},{1,0},{2,3},{3,2},{4,5},{5,4},{6,7},{7,6},{8,9},{9,8},{10,11... | collective-permute-start | bytes 393224 | tf_op jit(solution)/shard_map/ppermute | solution.py:58
  101.3 16.6 %collective-permute-start.29 = (bf16[1,128,512]{2,1,0:T(8,128)(2,1)S(1)}, bf16[1,128,512]{2,1,0:T(8,128)(2,1)S(1)}, u32[]{:S(2)}, u32[]{:S(2)}) collective-permute-start(bf16[1,128,512]{2,1,0:T(8,128)(2,1)S(1)} %get-tuple-element.114), channel_id=1, source_target_pairs={{0,3},{1,2},{2,1},{3,0},{4,7},{5,6},{6,5},{7,4},{8,11},{9,10},{10,... | collective-permute-start | bytes 393224 | tf_op jit(solution)/shard_map/ppermute | solution.py:58
  109.7 8.2 %collective-permute-start.30 = (bf16[1,128,512]{2,1,0:T(8,128)(2,1)S(1)}, bf16[1,128,512]{2,1,0:T(8,128)(2,1)S(1)}, u32[]{:S(2)}, u32[]{:S(2)}) collective-permute-start(bf16[1,128,512]{2,1,0:T(8,128)(2,1)S(1)} %get-tuple-element.115), channel_id=1, source_target_pairs={{0,6},{1,7},{2,4},{3,5},{4,2},{5,3},{6,0},{7,1},{8,14},{9,15},{10,... | collective-permute-start | bytes 393224 | tf_op jit(solution)/shard_map/ppermute | solution.py:58
  110.6 9.5 %collective-permute-start.32 = (bf16[1,128,512]{2,1,0:T(8,128)(2,1)S(1)}, bf16[1,128,512]{2,1,0:T(8,128)(2,1)S(1)}, u32[]{:S(2)}, u32[]{:S(2)}) collective-permute-start(bf16[1,128,512]{2,1,0:T(8,128)(2,1)S(1)} %slice.31), channel_id=1, source_target_pairs={{0,2},{1,3},{2,0},{3,1},{4,6},{5,7},{6,4},{7,5},{8,10},{9,11},{10,... | collective-permute-start | bytes 393224 | tf_op jit(solution)/shard_map/ppermute | solution.py:58
  125.2 14.5 %collective-permute-start.33 = (bf16[1024,512]{1,0:T(8,128)(2,1)S(1)}, bf16[1024,512]{1,0:T(8,128)(2,1)S(1)}, u32[]{:S(2)}, u32[]{:S(2)}) collective-permute-start(bf16[1024,512]{1,0:T(8,128)(2,1)S(1)} %shard_map.91), channel_id=1, source_target_pairs={{8,0},{16,8},{24,16},{0,24},{9,1},{17,9},{25,17},{1,25},{10,2},{18... | collective-permute-start | bytes 3145736 | tf_op jit(solution)/shard_map/ppermute | solution.py:250
  (6 other events, 18.9 us)

commit v4 on v3

--- a/solution.py
+++ b/solution.py
@@ -45,6 +45,13 @@
     return hops
 
 
+def column(offset, parts):
+    quarter = parts // 4
+    early = parts - 1 - quarter
+    late = early + offset - 2 * quarter
+    return jnp.where(offset < 2 * quarter, offset - 1, jnp.where(offset < 3 * quarter, late, offset - 1 - quarter))
+
+
 def bundles(parts):
     via = {}
     for k, (first, _) in relays(parts).items():
@@ -80,31 +87,31 @@
     return [pltpu.VMEM((len(carried), block, width), dtype) for _, carried in bundles(parts)]
 
 
-def first_kernel(parts, info, current, carried, x, h0, *rest):
+def first_kernel(parts, info, current, *rest):
     sent, sems = rest[:-1], rest[-1]
-    spans = [slice(at, at + TILE) for at in range(0, x.shape[0], TILE)]
-    copies = [pltpu.make_async_copy(current.at[rows], x.at[rows], sems.at[at]) for at, rows in enumerate(spans)]
-    anchor = pltpu.make_async_copy(carried, h0, sems.at[len(spans)])
+    block = sent[0].shape[1]
+    copies = []
+    for (_, carried), target in zip(bundles(parts), sent):
+        for place, k in enumerate(carried):
+            row = info[IDS + jnp.bitwise_xor(info[PART], k)]
+            rows = pl.ds(pl.multiple_of(row * block, block), block)
+            copies.append(pltpu.make_async_copy(current.at[rows], target.at[place], sems.at[k]))
     run(copies)
-    anchor.start()
-    pick(info, x, sent, parts)
-    anchor.wait()
-
-
-def first(info, current, carried, parts, block):
-    shapes = [pltpu.VMEM(current.shape, current.dtype)] * 2
-    shapes += sent_shapes(parts, block, current.shape[1], current.dtype)
+
+
+def first(info, current, parts, block):
+    shapes = sent_shapes(parts, block, current.shape[1], current.dtype)
     return pl.pallas_call(
         lambda *refs: first_kernel(parts, *refs),
         out_shape=shapes,
-        in_specs=[SMEM, HBM, HBM],
+        in_specs=[SMEM, HBM],
         out_specs=[VMEM] * len(shapes),
-        scratch_shapes=[pltpu.SemaphoreType.DMA((current.shape[0] // TILE + 1,))],
-        compiler_params=LIMIT,
-    )(info, far(current), far(carried))
-
-
-def merge_kernel(info, col, counts, adj, own, other, fetched, total, sems):
+        scratch_shapes=[pltpu.SemaphoreType.DMA((parts,))],
+        compiler_params=LIMIT,
+    )(info, far(current))
+
+
+def merge_kernel(parts, info, col, counts, adj, own, early, late, fetched, total, sems):
     rows, block = adj.shape[0], adj.shape[-1]
 
     def fetch(row):
@@ -120,7 +127,7 @@
         def add(k, carry):
             entry = col[row, k]
             offset = jnp.bitwise_xor(jnp.maximum(entry - rows, 0), info[PART])
-            afar = jnp.where(offset == 0, info[IDS + info[PART]], rows + offset - 1)
+            afar = jnp.where(offset == 0, info[IDS + info[PART]], rows + column(offset, parts))
             total[jnp.where(entry < rows, entry, afar)] += fetched[row % 2, k].astype(jnp.float32)
             return carry
 
@@ -130,20 +137,23 @@
             value = total[entry].astype(own.dtype)
             if entry < rows:
                 own[at, entry * block : (entry + 1) * block] = value
+            elif (entry - rows) * block < early.shape[1]:
+                early[at, (entry - rows) * block : (entry - rows + 1) * block] = value
             else:
-                other[at, (entry - rows) * block : (entry - rows + 1) * block] = value
+                place = (entry - rows) * block - early.shape[1]
+                late[at, place : place + block] = value
 
 
 def merged(info, col, counts, adj, parts):
     rows, slots, block, _ = adj.shape
-    return pl.pallas_call(
-        merge_kernel,
+    passed = len(relays(parts))
+    return pl.pallas_call(
+        lambda *refs: merge_kernel(parts, *refs),
         out_shape=[
-            pltpu.VMEM((rows * block, rows * block), adj.dtype),
-            pltpu.VMEM((rows * block, (parts - 1) * block), adj.dtype),
+            pltpu.VMEM((rows * block, count * block), adj.dtype) for count in (rows, parts - 1 - passed, passed)
         ],
         in_specs=[SMEM, SMEM, SMEM, HBM],
-        out_specs=[VMEM, VMEM],
+        out_specs=[VMEM] * 3,
         scratch_shapes=[
             pltpu.VMEM((2, slots, block, block), adj.dtype),
             pltpu.VMEM((rows + parts - 1, block, block), jnp.float32),
@@ -170,9 +180,36 @@
     )(fast(x), fast(h0), fast(adj))
 
 
-def layer_kernel(step, parts, offsets, info, beta, adj, partial, weight, new_h0, h0, *rest):
-    incoming, rest = rest[: len(offsets)], rest[len(offsets) :]
+def gather_table(incoming, table):
     block = incoming[0].shape[1]
+    for place, value in enumerate(incoming):
+        table[place * block : (place + 1) * block] = value[0]
+
+
+def arrived_kernel(adj, partial, *rest):
+    incoming, added, table = rest[:-2], rest[-2], rest[-1]
+    gather_table(incoming, table)
+    for at in range(0, added.shape[0], TILE):
+        rows = slice(at, at + TILE)
+        agg = jnp.dot(adj[rows], table[...], preferred_element_type=jnp.float32)
+        added[rows] = partial[rows] + (1.0 - teleport) * agg
+
+
+def arrived(adj, partial, incoming):
+    _, block, width = incoming[0].shape
+    return pl.pallas_call(
+        arrived_kernel,
+        out_shape=pltpu.VMEM(partial.shape, partial.dtype),
+        in_specs=[VMEM] * (2 + len(incoming)),
+        out_specs=VMEM,
+        scratch_shapes=[pltpu.VMEM((len(incoming) * block, width), incoming[0].dtype)],
+        input_output_aliases={1: 0},
+        compiler_params=LIMIT,
+    )(fast(adj), fast(partial), *[fast(value) for value in incoming])
+
+
+def layer_kernel(step, parts, number, info, beta, adj, partial, weight, new_h0, h0, *rest):
+    incoming, rest = rest[:number], rest[number:]
     more = step < STEPS - 1
     out, following, anchor, sent = rest[0], rest[1], rest[2], rest[3 : 3 + len(bundles(parts))]
     table, sem = rest[-2:]
@@ -183,8 +220,7 @@
         def _():
             fresh.start()
 
-    for offset, value in zip(offsets, incoming):
-        table[(offset - 1) * block : offset * block] = value[0]
+    gather_table(incoming, table)
     scale = beta[step]
     for at in range(0, out.shape[0], TILE):
         rows = slice(at, at + TILE)
@@ -204,24 +240,26 @@
     @pl.when(info[STARTS + step + 1] == 0)
     def _():
         following[...] = out[...]
+        if step == 0:
+            anchor[...] = h0[...]
 
     pick(info, following, sent, parts)
 
 
-def layer(step, parts, info, beta, adj, partial, weight, new_h0, h0, incoming, offsets):
+def layer(step, parts, info, beta, adj, partial, weight, new_h0, h0, incoming):
     _, block, width = incoming[0].shape
     made = pltpu.VMEM(partial.shape, incoming[0].dtype)
     shapes = [made]
     if step < STEPS - 1:
         shapes += [made, made] + sent_shapes(parts, block, width, made.dtype)
-    scratch = [pltpu.VMEM(((parts - 1) * block, width), made.dtype), pltpu.SemaphoreType.DMA]
-    return pl.pallas_call(
-        lambda *refs: layer_kernel(step, parts, offsets, *refs),
+    scratch = [pltpu.VMEM((len(incoming) * block, width), made.dtype), pltpu.SemaphoreType.DMA]
+    return pl.pallas_call(
+        lambda *refs: layer_kernel(step, parts, len(incoming), *refs),
         out_shape=shapes,
         in_specs=[SMEM, SMEM, VMEM, VMEM, VMEM, HBM, VMEM] + [VMEM] * len(incoming),
         out_specs=[VMEM] * len(shapes),
         scratch_shapes=scratch,
-        input_output_aliases={6: 2} if step < STEPS - 1 else {},
+        input_output_aliases={6: 2} if 0 < step < STEPS - 1 else {},
         compiler_params=LIMIT,
     )(info, beta, fast(adj), fast(partial), fast(weight), far(new_h0), fast(h0), *[fast(value) for value in incoming])
 
@@ -266,7 +304,8 @@
             lax.dynamic_index_in_dim(send_list, part, 0, keepdims=False),
         ]
     )
-    current, h0, *sent = first(info, carry_h[0], carry_h0[0], parts, block)
+    sent = first(info, carry_h[0], parts, block)
+    current, h0 = carry_h[0], carry_h0[0]
     hops = [hop for hop, _ in bundles(parts)]
     weight = weights[0]
     coming = {}
@@ -274,8 +313,8 @@
     for t in range(STEPS):
         got = [swapped(value, hop) for value, hop in zip(sent, hops)]
         if t == 0:
-            counts, current = lax.optimization_barrier((counts, current))
-            own_adj, other_adj = merged(info, col_index, counts, adj_blocks, parts)
+            counts, sent = lax.optimization_barrier((counts, sent))
+            own_adj, early_adj, late_adj = merged(info, col_index, counts, adj_blocks, parts)
         if t == 3:
             current, moving[1] = lax.optimization_barrier((current, moving[1]))
         partial = own_part(current, h0, own_adj)
@@ -290,7 +329,9 @@
             moving[t - 1] = moved(made, 1 - t)
             if t == 3:
                 partial, moving[t - 1] = lax.optimization_barrier((partial, moving[t - 1]))
-        made, *rest = layer(t, parts, info, beta, other_adj, partial, weight, new_h0, h0, got + passed, hops + offsets)
+        partial = arrived(early_adj, partial, [value for _, value in sorted(zip(hops, got), key=lambda pair: pair[0])])
+        passed = [value for _, value in sorted(zip(offsets, passed), key=lambda pair: pair[0])]
+        made, *rest = layer(t, parts, info, beta, late_adj, partial, weight, new_h0, h0, passed)
         if rest:
             current, h0, *sent = rest
             weight = coming[t + 1]

time: 142 us -> 138 us (0.972); the launches traced: 141 us -> 138 us
  starting transfers between devices: 56.1 us -> 49.6 us
  waiting for transfers between devices: 52.7 us -> 56.4 us
    ppermute x28, starting transfers between devices: 35.7 us -> 31.3 us  [swapped(): return lax.ppermute(value, 'dom', [(i, i ^ offset) for i in range(parts)])]
    ppermute x6, waiting for transfers between devices: 16.6 us -> 19.3 us  [moved(): lax.ppermute(value, 'section', [((i + by) % length, i) for i in range(len...]
    ppermute x6, starting transfers between devices: 20.4 us -> 18.3 us  [moved(): lax.ppermute(value, 'section', [((i + by) % length, i) for i in range(len...]
    pallas_call x5 -> x9, Pallas kernels: 17.4 us -> 18.6 us  [the longest x4 7.58 us: layer(): pl.pallas_call(lambda *refs: layer_kernel(step, parts, len(incoming), *re...]
  transfers between devices with their start and end apart: 34 -> 34, of which waited for: 15 -> 17; matrix products, arithmetic and copies ran while one was open for 0% -> 0% of each run, Pallas kernels for 16% -> 18%
where the time goes in v4:
time: 138 us
  waiting for transfers between devices  56.4 us (41%)
  starting transfers between devices  49.6 us (36%)
  Pallas kernels  29.5 us (21%)
  local copies, waits for them, and re-layouts  2.26 us (2%)
    ppermute x28, waiting for transfers between devices, swapped(): return lax.ppermute(value, 'dom', [(i, i ^ offset) for i in range(parts)])  37.1 us
    ppermute x28, starting transfers between devices, swapped(): return lax.ppermute(value, 'dom', [(i, i ^ offset) for i in range(parts)])  31.3 us
    ppermute x6, waiting for transfers between devices, moved(): lax.ppermute(value, 'section', [((i + by) % length, i) for i in range(len...  19.3 us
    ppermute x6, starting transfers between devices, moved(): lax.ppermute(value, 'section', [((i + by) % length, i) for i in range(len...  18.3 us
    pallas_call x4, Pallas kernels, layer(): pl.pallas_call(lambda *refs: layer_kernel(step, parts, len(incoming), *re...  7.58 us
    pallas_call x1, Pallas kernels, merged(): pl.pallas_call(lambda *refs: merge_kernel(parts, *refs), out_shape=[pltpu...  6.69 us
    pallas_call x4, Pallas kernels, own_part(): pl.pallas_call(own_kernel, out_shape=pltpu.VMEM(x.shape, jnp.float32), in...  5.09 us
    pallas_call x4, Pallas kernels, arrived(): pl.pallas_call(arrived_kernel, out_shape=pltpu.VMEM(partial.shape, partia...  4.34 us
  transfers between devices with their start and end apart: 34, of which 17 were waited for; matrix products, arithmetic and copies ran while one was open for 0% of the time, Pallas kernels for 18%

profile of v4, /device:TPU:1, one launch (start us, length us, event | category | flops | bytes accessed | tf_op | source)
XLA Modules:
  0.0 138.3 jit_solution(8492871263765696059)
XLA Ops:
  0.8 1.9 %shard_map.82 = (bf16[2,128,512]{2,1,0:T(8,128)(2,1)S(1)}, bf16[2,128,512]{2,1,0:T(8,128)(2,1)S(1)}, bf16[1,128,512]{2,1,0:T(8,128)(2,1)S(1)}, bf16[1,128,512]{2,1,0:T(8,128)(2,1)S(1)}, bf16[1,128,512]{2,1,0:T(8,128)(2,1)S(1)}) custom-call(s32[13]{0:T(128)S(1)} %pad_add_fusion.refs_0_, bf16[1024,512]{1,0:T(8,128)(2,1)} %bitcast.6), custom_call_target="tpu_custom_call" | custom-call | tf_op jit(solution)/shard_map/pallas_call | solution.py:104
  2.6 2.3 %collective-permute-start = (bf16[2,128,512]{2,1,0:T(8,128)(2,1)S(1)}, bf16[2,128,512]{2,1,0:T(8,128)(2,1)S(1)}, u32[]{:S(2)}, u32[]{:S(2)}) collective-permute-start(bf16[2,128,512]{2,1,0:T(8,128)(2,1)S(1)} %get-tuple-element.60), channel_id=1, source_target_pairs={{0,2},{1,3},{2,0},{3,1},{4,6},{5,7},{6,4},{7,5},{8,10},{9,11},{10,... | collective-permute-start | bytes 786440 | tf_op jit(solution)/shard_map/ppermute | solution.py:65
  4.9 3.1 %collective-permute-start.1 = (bf16[2,128,512]{2,1,0:T(8,128)(2,1)S(1)}, bf16[2,128,512]{2,1,0:T(8,128)(2,1)S(1)}, u32[]{:S(2)}, u32[]{:S(2)}) collective-permute-start(bf16[2,128,512]{2,1,0:T(8,128)(2,1)S(1)} %get-tuple-element.61), channel_id=1, source_target_pairs={{0,7},{1,6},{2,5},{3,4},{4,3},{5,2},{6,1},{7,0},{8,15},{9,14},{10,... | collective-permute-start | bytes 786440 | tf_op jit(solution)/shard_map/ppermute | solution.py:65
  8.2 1.3 collective-permute-start.3
  11.0 6.7 %shard_map.83 = (bf16[1024,1024]{1,0:T(8,128)(2,1)S(1)}, bf16[1024,640]{1,0:T(8,128)(2,1)S(1)}, bf16[1024,256]{1,0:T(8,128)(2,1)S(1)}) custom-call(s32[13]{0:T(128)S(1)} %pad_add_fusion.refs_0_, s32[8,24]{1,0:T(8,128)S(1)} %copy-done.4, s32[8]{0:T(128)S(1)} %copy-done.5, bf16[8,24,128,128]{3,2,1,0:T(8,128)(2,1)} %refs_3_.1), custom_call_target="tpu_custom_call" | custom-call | tf_op jit(solution)/shard_map/pallas_call | solution.py:150
  19.4 2.8 %collective-permute-start.5 = (bf16[1,128,512]{2,1,0:T(8,128)(2,1)S(1)}, bf16[1,128,512]{2,1,0:T(8,128)(2,1)S(1)}, u32[]{:S(2)}, u32[]{:S(2)}) collective-permute-start(bf16[1,128,512]{2,1,0:T(8,128)(2,1)S(1)} %slice.24), channel_id=1, source_target_pairs={{0,6},{1,7},{2,4},{3,5},{4,2},{5,3},{6,0},{7,1},{8,14},{9,15},{10,... | collective-permute-start | bytes 393224 | tf_op jit(solution)/shard_map/ppermute | solution.py:65
  22.2 4.3 %collective-permute-start.12 = (bf16[512,512]{1,0:T(8,128)(2,1)S(1)}, bf16[512,512]{1,0:T(8,128)(2,1)S(1)}, u32[]{:S(2)}, u32[]{:S(2)}) collective-permute-start(bf16[512,512]{1,0:T(8,128)(2,1)S(1)} %bitcast.10), channel_id=1, source_target_pairs={{8,0},{16,8},{24,16},{0,24},{9,1},{17,9},{25,17},{1,25},{10,2},{18... | collective-permute-start | bytes 1572872 | tf_op jit(solution)/shard_map/ppermute | solution.py:288
  27.6 2.4 %collective-permute-done.6.refs_8_ = bf16[1,128,512]{2,1,0:T(8,128)(2,1)S(1)} collective-permute-done((bf16[1,128,512]{2,1,0:T(8,128)(2,1)S(1)}, bf16[1,128,512]{2,1,0:T(8,128)(2,1)S(1)}, u32[]{:S(2)}, u32[]{:S(2)}) %collective-permute-start.6) | collective-permute-done | bytes 131104 | tf_op jit(solution)/shard_map/ppermute | solution.py:65
  30.1 1.8 %shard_map.86 = (bf16[1024,512]{1,0:T(8,128)(2,1)S(1)}, bf16[1024,512]{1,0:T(8,128)(2,1)S(1)}, bf16[1024,512]{1,0:T(8,128)(2,1)S(1)}, bf16[2,128,512]{2,1,0:T(8,...) custom-call(s32[13]{0:T(128)S(1)} %pad_add_fusion.refs_0_, ...), custom_call_target="tpu_custom_call" | custom-call | tf_op jit(solution)/shard_map/pallas_call | solution.py:256
  31.9 3.0 %collective-permute-start.8 = (bf16[2,128,512]{2,1,0:T(8,128)(2,1)S(1)}, bf16[2,128,512]{2,1,0:T(8,128)(2,1)S(1)}, u32[]{:S(2)}, u32[]{:S(2)}) collective-permute-start(bf16[2,128,512]{2,1,0:T(8,128)(2,1)S(1)} %get-tuple-element.74), channel_id=1, source_target_pairs={{0,7},{1,6},{2,5},{3,4},{4,3},{5,2},{6,1},{7,0},{8,15},{9,14},{10,... | collective-permute-start | bytes 786440 | tf_op jit(solution)/shard_map/ppermute | solution.py:65
  39.7 4.5 %collective-permute-done.8.rest_4_ = bf16[2,128,512]{2,1,0:T(8,128)(2,1)S(1)} collective-permute-done((bf16[2,128,512]{2,1,0:T(8,128)(2,1)S(1)}, bf16[2,128,512]{2,1,0:T(8,128)(2,1)S(1)}, u32[]{:S(2)}, u32[]{:S(2)}) %collective-permute-start.8) | collective-permute-done | bytes 262176 | tf_op jit(solution)/shard_map/ppermute | solution.py:65
  45.4 2.9 %collective-permute-start.20 = (bf16[512,512]{1,0:T(8,128)(2,1)S(1)}, bf16[512,512]{1,0:T(8,128)(2,1)S(1)}, u32[]{:S(2)}, u32[]{:S(2)}) collective-permute-start(bf16[512,512]{1,0:T(8,128)(2,1)S(1)} %bitcast.12), channel_id=1, source_target_pairs={{16,0},{24,8},{0,16},{8,24},{17,1},{25,9},{1,17},{9,25},{18,2},{26... | collective-permute-start | bytes 1572872 | tf_op jit(solution)/shard_map/ppermute | solution.py:288
  48.3 2.0 %collective-permute-done.11.rest_3_ = bf16[1,128,512]{2,1,0:T(8,128)(2,1)S(1)} collective-permute-done((bf16[1,128,512]{2,1,0:T(8,128)(2,1)S(1)}, bf16[1,128,512]{2,1,0:T(8,128)(2,1)S(1)}, u32[]{:S(2)}, u32[]{:S(2)}) %collective-permute-start.11) | collective-permute-done | bytes 131104 | tf_op jit(solution)/shard_map/ppermute | solution.py:65
  51.5 2.0 %collective-permute-done.13.refs_7_ = bf16[1,128,512]{2,1,0:T(8,128)(2,1)S(1)} collective-permute-done((bf16[1,128,512]{2,1,0:T(8,128)(2,1)S(1)}, bf16[1,128,512]{2,1,0:T(8,128)(2,1)S(1)}, u32[]{:S(2)}, u32[]{:S(2)}) %collective-permute-start.13) | collective-permute-done | bytes 131104 | tf_op jit(solution)/shard_map/ppermute | solution.py:65
  53.5 1.7 %shard_map.89 = (bf16[1024,512]{1,0:T(8,128)(2,1)S(1)}, bf16[1024,512]{1,0:T(8,128)(2,1)S(1)}, bf16[1024,512]{1,0:T(8,128)(2,1)S(1)}, bf16[2,128,512]{2,1,0:T(8,...) custom-call(s32[13]{0:T(128)S(1)} %pad_add_fusion.refs_0_, ...), custom_call_target="tpu_custom_call", output_to_operand_aliasing={{2}: (6, {})} | custom-call | tf_op jit(solution)/shard_map/pallas_call | solution.py:256
  55.2 4.2 %collective-permute-start.15 = (bf16[2,128,512]{2,1,0:T(8,128)(2,1)S(1)}, bf16[2,128,512]{2,1,0:T(8,128)(2,1)S(1)}, u32[]{:S(2)}, u32[]{:S(2)}) collective-permute-start(bf16[2,128,512]{2,1,0:T(8,128)(2,1)S(1)} %get-tuple-element.85), channel_id=1, source_target_pairs={{0,2},{1,3},{2,0},{3,1},{4,6},{5,7},{6,4},{7,5},{8,10},{9,11},{10,... | collective-permute-start | bytes 786440 | tf_op jit(solution)/shard_map/ppermute | solution.py:65
  61.9 2.9 %collective-permute-done.15.rest_1_ = bf16[2,128,512]{2,1,0:T(8,128)(2,1)S(1)} collective-permute-done((bf16[2,128,512]{2,1,0:T(8,128)(2,1)S(1)}, bf16[2,128,512]{2,1,0:T(8,128)(2,1)S(1)}, u32[]{:S(2)}, u32[]{:S(2)}) %collective-permute-start.15) | collective-permute-done | bytes 262176 | tf_op jit(solution)/shard_map/ppermute | solution.py:65
  65.1 4.4 %collective-permute-done.16.rest_4_ = bf16[2,128,512]{2,1,0:T(8,128)(2,1)S(1)} collective-permute-done((bf16[2,128,512]{2,1,0:T(8,128)(2,1)S(1)}, bf16[2,128,512]{2,1,0:T(8,128)(2,1)S(1)}, u32[]{:S(2)}, u32[]{:S(2)}) %collective-permute-start.16) | collective-permute-done | bytes 262176 | tf_op jit(solution)/shard_map/ppermute | solution.py:65
  69.5 9.0 %collective-permute-start.25 = (bf16[1024,512]{1,0:T(8,128)(2,1)S(1)}, bf16[1024,512]{1,0:T(8,128)(2,1)S(1)}, u32[]{:S(2)}, u32[]{:S(2)}) collective-permute-start(bf16[1024,512]{1,0:T(8,128)(2,1)S(1)} %get-tuple-element.100), channel_id=1, source_target_pairs={{24,0},{0,8},{8,16},{16,24},{25,1},{1,9},{9,17},{17,25},{26,2},{2,... | collective-permute-start | bytes 3145736 | tf_op jit(solution)/shard_map/ppermute | solution.py:288
  78.6 2.1 %collective-permute-start.21 = (bf16[1,128,512]{2,1,0:T(8,128)(2,1)S(1)}, bf16[1,128,512]{2,1,0:T(8,128)(2,1)S(1)}, u32[]{:S(2)}, u32[]{:S(2)}) collective-permute-start(bf16[1,128,512]{2,1,0:T(8,128)(2,1)S(1)} %slice.28), channel_id=1, source_target_pairs={{0,6},{1,7},{2,4},{3,5},{4,2},{5,3},{6,0},{7,1},{8,14},{9,15},{10,... | collective-permute-start | bytes 393224 | tf_op jit(solution)/shard_map/ppermute | solution.py:65
  81.8 3.6 %collective-permute-done.21.refs_7_ = bf16[1,128,512]{2,1,0:T(8,128)(2,1)S(1)} collective-permute-done((bf16[1,128,512]{2,1,0:T(8,128)(2,1)S(1)}, bf16[1,128,512]{2,1,0:T(8,128)(2,1)S(1)}, u32[]{:S(2)}, u32[]{:S(2)}) %collective-permute-start.21) | collective-permute-done | bytes 131104 | tf_op jit(solution)/shard_map/ppermute | solution.py:65
  85.5 1.7 %collective-permute-done.22.refs_8_ = bf16[1,128,512]{2,1,0:T(8,128)(2,1)S(1)} collective-permute-done((bf16[1,128,512]{2,1,0:T(8,128)(2,1)S(1)}, bf16[1,128,512]{2,1,0:T(8,128)(2,1)S(1)}, u32[]{:S(2)}, u32[]{:S(2)}) %collective-permute-start.22) | collective-permute-done | bytes 131104 | tf_op jit(solution)/shard_map/ppermute | solution.py:65
  87.2 2.6 %shard_map.92 = (bf16[1024,512]{1,0:T(8,128)(2,1)S(1)}, bf16[1024,512]{1,0:T(8,128)(2,1)S(1)}, bf16[1024,512]{1,0:T(8,128)(2,1)S(1)}, bf16[2,128,512]{2,1,0:T(8,...) custom-call(s32[13]{0:T(128)S(1)} %pad_add_fusion.refs_0_, ...), custom_call_target="tpu_custom_call", output_to_operand_aliasing={{2}: (6, {})} | custom-call | tf_op jit(solution)/shard_map/pallas_call | solution.py:256
  91.8 1.5 %collective-permute-start.27 = (bf16[1,128,512]{2,1,0:T(8,128)(2,1)S(1)}, bf16[1,128,512]{2,1,0:T(8,128)(2,1)S(1)}, u32[]{:S(2)}, u32[]{:S(2)}) collective-permute-start(bf16[1,128,512]{2,1,0:T(8,128)(2,1)S(1)} %get-tuple-element.106), channel_id=1, source_target_pairs={{0,1},{1,0},{2,3},{3,2},{4,5},{5,4},{6,7},{7,6},{8,9},{9,8},{10,11... | collective-permute-start | bytes 393224 | tf_op jit(solution)/shard_map/ppermute | solution.py:65
  94.6 3.9 %collective-permute-done.23.rest_1_ = bf16[2,128,512]{2,1,0:T(8,128)(2,1)S(1)} collective-permute-done((bf16[2,128,512]{2,1,0:T(8,128)(2,1)S(1)}, bf16[2,128,512]{2,1,0:T(8,128)(2,1)S(1)}, u32[]{:S(2)}, u32[]{:S(2)}) %collective-permute-start.23) | collective-permute-done | bytes 262176 | tf_op jit(solution)/shard_map/ppermute | solution.py:65
  99.0 5.0 %collective-permute-done.24.rest_4_ = bf16[2,128,512]{2,1,0:T(8,128)(2,1)S(1)} collective-permute-done((bf16[2,128,512]{2,1,0:T(8,128)(2,1)S(1)}, bf16[2,128,512]{2,1,0:T(8,128)(2,1)S(1)}, u32[]{:S(2)}, u32[]{:S(2)}) %collective-permute-start.24) | collective-permute-done | bytes 262176 | tf_op jit(solution)/shard_map/ppermute | solution.py:65
  104.0 2.5 %collective-permute-start.29 = (bf16[1,128,512]{2,1,0:T(8,128)(2,1)S(1)}, bf16[1,128,512]{2,1,0:T(8,128)(2,1)S(1)}, u32[]{:S(2)}, u32[]{:S(2)}) collective-permute-start(bf16[1,128,512]{2,1,0:T(8,128)(2,1)S(1)} %get-tuple-element.109), channel_id=1, source_target_pairs={{0,6},{1,7},{2,4},{3,5},{4,2},{5,3},{6,0},{7,1},{8,14},{9,15},{10,... | collective-permute-start | bytes 393224 | tf_op jit(solution)/shard_map/ppermute | solution.py:65
  106.8 7.5 %collective-permute-done.26.refs_0_ = bf16[1024,512]{1,0:T(8,128)(2,1)S(1)} collective-permute-done((bf16[1024,512]{1,0:T(8,128)(2,1)S(1)}, bf16[1024,512]{1,0:T(8,128)(2,1)S(1)}, u32[]{:S(2)}, u32[]{:S(2)}) %collective-permute-start.26) | collective-permute-done | bytes 1048608 | tf_op jit(solution)/shard_map/ppermute | solution.py:288
  114.3 1.7 %collective-permute-start.31 = (bf16[1,128,512]{2,1,0:T(8,128)(2,1)S(1)}, bf16[1,128,512]{2,1,0:T(8,128)(2,1)S(1)}, u32[]{:S(2)}, u32[]{:S(2)}) collective-permute-start(bf16[1,128,512]{2,1,0:T(8,128)(2,1)S(1)} %slice.30), channel_id=1, source_target_pairs={{0,6},{1,7},{2,4},{3,5},{4,2},{5,3},{6,0},{7,1},{8,14},{9,15},{10,... | collective-permute-start | bytes 393224 | tf_op jit(solution)/shard_map/ppermute | solution.py:65
  118.5 2.4 %collective-permute-done.31.refs_7_ = bf16[1,128,512]{2,1,0:T(8,128)(2,1)S(1)} collective-permute-done((bf16[1,128,512]{2,1,0:T(8,128)(2,1)S(1)}, bf16[1,128,512]{2,1,0:T(8,128)(2,1)S(1)}, u32[]{:S(2)}, u32[]{:S(2)}) %collective-permute-start.31) | collective-permute-done | bytes 131104 | tf_op jit(solution)/shard_map/ppermute | solution.py:65
  120.9 1.6 %shard_map.95 = bf16[1024,512]{1,0:T(8,128)(2,1)S(1)} custom-call(s32[13]{0:T(128)S(1)} %pad_add_fusion.refs_0_, f32[4]{0:T(128)S(1)} %fusion.4.refs_1_, bf16[1024,256]{1,0:T(8,128)(2,1)S(1)} %get-tuple-element.66.refs_2_, f32[1024,512]{1,0:T(8,128)S(1)} %shard_map.94.refs_3_, bf16[512,512]{1,0:T(8,128)(2,1)S(1)} %collective-permute-done.30.refs_4_, ...), custom_call_target="tpu_custom_call" | custom-call | tf_op jit(solution)/shard_map/pallas_call | solution.py:256
  126.7 10.5 %collective-permute-done.33.refs_0_ = bf16[1024,512]{1,0:T(8,128)(2,1)S(1)} collective-permute-done((bf16[1024,512]{1,0:T(8,128)(2,1)S(1)}, bf16[1024,512]{1,0:T(8,128)(2,1)S(1)}, u32[]{:S(2)}, u32[]{:S(2)}) %collective-permute-start.33) | collective-permute-done | bytes 1048608 | tf_op jit(solution)/shard_map/ppermute | solution.py:288
  (78 shorter events, 28.1 us)
Async XLA Ops:
  2.6 16.4 %collective-permute-start = (bf16[2,128,512]{2,1,0:T(8,128)(2,1)S(1)}, bf16[2,128,512]{2,1,0:T(8,128)(2,1)S(1)}, u32[]{:S(2)}, u32[]{:S(2)}) collective-permute-start(bf16[2,128,512]{2,1,0:T(8,128)(2,1)S(1)} %get-tuple-element.60), channel_id=1, source_target_pairs={{0,2},{1,3},{2,0},{3,1},{4,6},{5,7},{6,4},{7,5},{8,10},{9,11},{10,... | collective-permute-start | bytes 786440 | tf_op jit(solution)/shard_map/ppermute | solution.py:65
  4.9 14.5 %collective-permute-start.1 = (bf16[2,128,512]{2,1,0:T(8,128)(2,1)S(1)}, bf16[2,128,512]{2,1,0:T(8,128)(2,1)S(1)}, u32[]{:S(2)}, u32[]{:S(2)}) collective-permute-start(bf16[2,128,512]{2,1,0:T(8,128)(2,1)S(1)} %get-tuple-element.61), channel_id=1, source_target_pairs={{0,7},{1,6},{2,5},{3,4},{4,3},{5,2},{6,1},{7,0},{8,15},{9,14},{10,... | collective-permute-start | bytes 786440 | tf_op jit(solution)/shard_map/ppermute | solution.py:65
  8.0 14.2 %collective-permute-start.2 = (bf16[1,128,512]{2,1,0:T(8,128)(2,1)S(1)}, bf16[1,128,512]{2,1,0:T(8,128)(2,1)S(1)}, u32[]{:S(2)}, u32[]{:S(2)}) collective-permute-start(bf16[1,128,512]{2,1,0:T(8,128)(2,1)S(1)} %get-tuple-element.62), channel_id=1, source_target_pairs={{0,1},{1,0},{2,3},{3,2},{4,5},{5,4},{6,7},{7,6},{8,9},{9,8},{10,11... | collective-permute-start | bytes 393224 | tf_op jit(solution)/shard_map/ppermute | solution.py:65
  8.2 18.3 %collective-permute-start.3 = (bf16[1,128,512]{2,1,0:T(8,128)(2,1)S(1)}, bf16[1,128,512]{2,1,0:T(8,128)(2,1)S(1)}, u32[]{:S(2)}, u32[]{:S(2)}) collective-permute-start(bf16[1,128,512]{2,1,0:T(8,128)(2,1)S(1)} %get-tuple-element.63), channel_id=1, source_target_pairs={{0,3},{1,2},{2,1},{3,0},{4,7},{5,6},{6,5},{7,4},{8,11},{9,10},{10,... | collective-permute-start | bytes 393224 | tf_op jit(solution)/shard_map/ppermute | solution.py:65
  9.5 17.0 %collective-permute-start.4 = (bf16[1,128,512]{2,1,0:T(8,128)(2,1)S(1)}, bf16[1,128,512]{2,1,0:T(8,128)(2,1)S(1)}, u32[]{:S(2)}, u32[]{:S(2)}) collective-permute-start(bf16[1,128,512]{2,1,0:T(8,128)(2,1)S(1)} %get-tuple-element.64), channel_id=1, source_target_pairs={{0,6},{1,7},{2,4},{3,5},{4,2},{5,3},{6,0},{7,1},{8,14},{9,15},{10,... | collective-permute-start | bytes 393224 | tf_op jit(solution)/shard_map/ppermute | solution.py:65
  19.4 8.2 %collective-permute-start.5 = (bf16[1,128,512]{2,1,0:T(8,128)(2,1)S(1)}, bf16[1,128,512]{2,1,0:T(8,128)(2,1)S(1)}, u32[]{:S(2)}, u32[]{:S(2)}) collective-permute-start(bf16[1,128,512]{2,1,0:T(8,128)(2,1)S(1)} %slice.24), channel_id=1, source_target_pairs={{0,6},{1,7},{2,4},{3,5},{4,2},{5,3},{6,0},{7,1},{8,14},{9,15},{10,... | collective-permute-start | bytes 393224 | tf_op jit(solution)/shard_map/ppermute | solution.py:65
  22.2 7.9 %collective-permute-start.6 = (bf16[1,128,512]{2,1,0:T(8,128)(2,1)S(1)}, bf16[1,128,512]{2,1,0:T(8,128)(2,1)S(1)}, u32[]{:S(2)}, u32[]{:S(2)}) collective-permute-start(bf16[1,128,512]{2,1,0:T(8,128)(2,1)S(1)} %slice.25), channel_id=1, source_target_pairs={{0,2},{1,3},{2,0},{3,1},{4,6},{5,7},{6,4},{7,5},{8,10},{9,11},{10,... | collective-permute-start | bytes 393224 | tf_op jit(solution)/shard_map/ppermute | solution.py:65
  22.2 29.3 %collective-permute-start.12 = (bf16[512,512]{1,0:T(8,128)(2,1)S(1)}, bf16[512,512]{1,0:T(8,128)(2,1)S(1)}, u32[]{:S(2)}, u32[]{:S(2)}) collective-permute-start(bf16[512,512]{1,0:T(8,128)(2,1)S(1)} %bitcast.10), channel_id=1, source_target_pairs={{8,0},{16,8},{24,16},{0,24},{9,1},{17,9},{25,17},{1,25},{10,2},{18... | collective-permute-start | bytes 1572872 | tf_op jit(solution)/shard_map/ppermute | solution.py:288
  31.8 6.6 %collective-permute-start.7 = (bf16[2,128,512]{2,1,0:T(8,128)(2,1)S(1)}, bf16[2,128,512]{2,1,0:T(8,128)(2,1)S(1)}, u32[]{:S(2)}, u32[]{:S(2)}) collective-permute-start(bf16[2,128,512]{2,1,0:T(8,128)(2,1)S(1)} %get-tuple-element.73), channel_id=1, source_target_pairs={{0,2},{1,3},{2,0},{3,1},{4,6},{5,7},{6,4},{7,5},{8,10},{9,11},{10,... | collective-permute-start | bytes 786440 | tf_op jit(solution)/shard_map/ppermute | solution.py:65
  31.9 12.3 %collective-permute-start.8 = (bf16[2,128,512]{2,1,0:T(8,128)(2,1)S(1)}, bf16[2,128,512]{2,1,0:T(8,128)(2,1)S(1)}, u32[]{:S(2)}, u32[]{:S(2)}) collective-permute-start(bf16[2,128,512]{2,1,0:T(8,128)(2,1)S(1)} %get-tuple-element.74), channel_id=1, source_target_pairs={{0,7},{1,6},{2,5},{3,4},{4,3},{5,2},{6,1},{7,0},{8,15},{9,14},{10,... | collective-permute-start | bytes 786440 | tf_op jit(solution)/shard_map/ppermute | solution.py:65
  34.9 9.8 %collective-permute-start.9 = (bf16[1,128,512]{2,1,0:T(8,128)(2,1)S(1)}, bf16[1,128,512]{2,1,0:T(8,128)(2,1)S(1)}, u32[]{:S(2)}, u32[]{:S(2)}) collective-permute-start(bf16[1,128,512]{2,1,0:T(8,128)(2,1)S(1)} %get-tuple-element.81), channel_id=1, source_target_pairs={{0,1},{1,0},{2,3},{3,2},{4,5},{5,4},{6,7},{7,6},{8,9},{9,8},{10,11... | collective-permute-start | bytes 393224 | tf_op jit(solution)/shard_map/ppermute | solution.py:65
  36.1 9.3 %collective-permute-start.10 = (bf16[1,128,512]{2,1,0:T(8,128)(2,1)S(1)}, bf16[1,128,512]{2,1,0:T(8,128)(2,1)S(1)}, u32[]{:S(2)}, u32[]{:S(2)}) collective-permute-start(bf16[1,128,512]{2,1,0:T(8,128)(2,1)S(1)} %get-tuple-element.82), channel_id=1, source_target_pairs={{0,3},{1,2},{2,1},{3,0},{4,7},{5,6},{6,5},{7,4},{8,11},{9,10},{10,... | collective-permute-start | bytes 393224 | tf_op jit(solution)/shard_map/ppermute | solution.py:65
  38.5 11.9 %collective-permute-start.11 = (bf16[1,128,512]{2,1,0:T(8,128)(2,1)S(1)}, bf16[1,128,512]{2,1,0:T(8,128)(2,1)S(1)}, u32[]{:S(2)}, u32[]{:S(2)}) collective-permute-start(bf16[1,128,512]{2,1,0:T(8,128)(2,1)S(1)} %get-tuple-element.83), channel_id=1, source_target_pairs={{0,6},{1,7},{2,4},{3,5},{4,2},{5,3},{6,0},{7,1},{8,14},{9,15},{10,... | collective-permute-start | bytes 393224 | tf_op jit(solution)/shard_map/ppermute | solution.py:65
  44.3 9.2 %collective-permute-start.13 = (bf16[1,128,512]{2,1,0:T(8,128)(2,1)S(1)}, bf16[1,128,512]{2,1,0:T(8,128)(2,1)S(1)}, u32[]{:S(2)}, u32[]{:S(2)}) collective-permute-start(bf16[1,128,512]{2,1,0:T(8,128)(2,1)S(1)} %slice.26), channel_id=1, source_target_pairs={{0,6},{1,7},{2,4},{3,5},{4,2},{5,3},{6,0},{7,1},{8,14},{9,15},{10,... | collective-permute-start | bytes 393224 | tf_op jit(solution)/shard_map/ppermute | solution.py:65
  44.7 8.8 %collective-permute-start.14 = (bf16[1,128,512]{2,1,0:T(8,128)(2,1)S(1)}, bf16[1,128,512]{2,1,0:T(8,128)(2,1)S(1)}, u32[]{:S(2)}, u32[]{:S(2)}) collective-permute-start(bf16[1,128,512]{2,1,0:T(8,128)(2,1)S(1)} %slice.27), channel_id=1, source_target_pairs={{0,2},{1,3},{2,0},{3,1},{4,6},{5,7},{6,4},{7,5},{8,10},{9,11},{10,... | collective-permute-start | bytes 393224 | tf_op jit(solution)/shard_map/ppermute | solution.py:65
  45.4 36.4 %collective-permute-start.20 = (bf16[512,512]{1,0:T(8,128)(2,1)S(1)}, bf16[512,512]{1,0:T(8,128)(2,1)S(1)}, u32[]{:S(2)}, u32[]{:S(2)}) collective-permute-start(bf16[512,512]{1,0:T(8,128)(2,1)S(1)} %bitcast.12), channel_id=1, source_target_pairs={{16,0},{24,8},{0,16},{8,24},{17,1},{25,9},{1,17},{9,25},{18,2},{26... | collective-permute-start | bytes 1572872 | tf_op jit(solution)/shard_map/ppermute | solution.py:288
  55.2 9.6 %collective-permute-start.15 = (bf16[2,128,512]{2,1,0:T(8,128)(2,1)S(1)}, bf16[2,128,512]{2,1,0:T(8,128)(2,1)S(1)}, u32[]{:S(2)}, u32[]{:S(2)}) collective-permute-start(bf16[2,128,512]{2,1,0:T(8,128)(2,1)S(1)} %get-tuple-element.85), channel_id=1, source_target_pairs={{0,2},{1,3},{2,0},{3,1},{4,6},{5,7},{6,4},{7,5},{8,10},{9,11},{10,... | collective-permute-start | bytes 786440 | tf_op jit(solution)/shard_map/ppermute | solution.py:65
  59.3 10.2 %collective-permute-start.16 = (bf16[2,128,512]{2,1,0:T(8,128)(2,1)S(1)}, bf16[2,128,512]{2,1,0:T(8,128)(2,1)S(1)}, u32[]{:S(2)}, u32[]{:S(2)}) collective-permute-start(bf16[2,128,512]{2,1,0:T(8,128)(2,1)S(1)} %get-tuple-element.86), channel_id=1, source_target_pairs={{0,7},{1,6},{2,5},{3,4},{4,3},{5,2},{6,1},{7,0},{8,15},{9,14},{10,... | collective-permute-start | bytes 786440 | tf_op jit(solution)/shard_map/ppermute | solution.py:65
  59.3 19.3 %collective-permute-start.17 = (bf16[1,128,512]{2,1,0:T(8,128)(2,1)S(1)}, bf16[1,128,512]{2,1,0:T(8,128)(2,1)S(1)}, u32[]{:S(2)}, u32[]{:S(2)}) collective-permute-start(bf16[1,128,512]{2,1,0:T(8,128)(2,1)S(1)} %get-tuple-element.93), channel_id=1, source_target_pairs={{0,1},{1,0},{2,3},{3,2},{4,5},{5,4},{6,7},{7,6},{8,9},{9,8},{10,11... | collective-permute-start | bytes 393224 | tf_op jit(solution)/shard_map/ppermute | solution.py:65
  60.3 20.4 %collective-permute-start.18 = (bf16[1,128,512]{2,1,0:T(8,128)(2,1)S(1)}, bf16[1,128,512]{2,1,0:T(8,128)(2,1)S(1)}, u32[]{:S(2)}, u32[]{:S(2)}) collective-permute-start(bf16[1,128,512]{2,1,0:T(8,128)(2,1)S(1)} %get-tuple-element.94), channel_id=1, source_target_pairs={{0,3},{1,2},{2,1},{3,0},{4,7},{5,6},{6,5},{7,4},{8,11},{9,10},{10,... | collective-permute-start | bytes 393224 | tf_op jit(solution)/shard_map/ppermute | solution.py:65
  64.8 15.9 %collective-permute-start.19 = (bf16[1,128,512]{2,1,0:T(8,128)(2,1)S(1)}, bf16[1,128,512]{2,1,0:T(8,128)(2,1)S(1)}, u32[]{:S(2)}, u32[]{:S(2)}) collective-permute-start(bf16[1,128,512]{2,1,0:T(8,128)(2,1)S(1)} %get-tuple-element.95), channel_id=1, source_target_pairs={{0,6},{1,7},{2,4},{3,5},{4,2},{5,3},{6,0},{7,1},{8,14},{9,15},{10,... | collective-permute-start | bytes 393224 | tf_op jit(solution)/shard_map/ppermute | solution.py:65
  69.5 22.3 %collective-permute-start.25 = (bf16[1024,512]{1,0:T(8,128)(2,1)S(1)}, bf16[1024,512]{1,0:T(8,128)(2,1)S(1)}, u32[]{:S(2)}, u32[]{:S(2)}) collective-permute-start(bf16[1024,512]{1,0:T(8,128)(2,1)S(1)} %get-tuple-element.100), channel_id=1, source_target_pairs={{24,0},{0,8},{8,16},{16,24},{25,1},{1,9},{9,17},{17,25},{26,2},{2,... | collective-permute-start | bytes 3145736 | tf_op jit(solution)/shard_map/ppermute | solution.py:288
  78.6 6.9 %collective-permute-start.21 = (bf16[1,128,512]{2,1,0:T(8,128)(2,1)S(1)}, bf16[1,128,512]{2,1,0:T(8,128)(2,1)S(1)}, u32[]{:S(2)}, u32[]{:S(2)}) collective-permute-start(bf16[1,128,512]{2,1,0:T(8,128)(2,1)S(1)} %slice.28), channel_id=1, source_target_pairs={{0,6},{1,7},{2,4},{3,5},{4,2},{5,3},{6,0},{7,1},{8,14},{9,15},{10,... | collective-permute-start | bytes 393224 | tf_op jit(solution)/shard_map/ppermute | solution.py:65
  89.8 24.5 %collective-permute-start.26 = (bf16[1024,512]{1,0:T(8,128)(2,1)S(1)}, bf16[1024,512]{1,0:T(8,128)(2,1)S(1)}, u32[]{:S(2)}, u32[]{:S(2)}) collective-permute-start(bf16[1024,512]{1,0:T(8,128)(2,1)S(1)} %get-tuple-element.104), channel_id=1, source_target_pairs={{16,0},{24,8},{0,16},{8,24},{17,1},{25,9},{1,17},{9,25},{18,2},{26... | collective-permute-start | bytes 3145736 | tf_op jit(solution)/shard_map/ppermute | solution.py:288
  89.9 28.6 %collective-permute-start.30 = (bf16[512,512]{1,0:T(8,128)(2,1)S(1)}, bf16[512,512]{1,0:T(8,128)(2,1)S(1)}, u32[]{:S(2)}, u32[]{:S(2)}) collective-permute-start(bf16[512,512]{1,0:T(8,128)(2,1)S(1)} %bitcast.13), channel_id=1, source_target_pairs={{24,0},{0,8},{8,16},{16,24},{25,1},{1,9},{9,17},{17,25},{26,2},{2,... | collective-permute-start | bytes 1572872 | tf_op jit(solution)/shard_map/ppermute | solution.py:288
  90.6 7.9 %collective-permute-start.23 = (bf16[2,128,512]{2,1,0:T(8,128)(2,1)S(1)}, bf16[2,128,512]{2,1,0:T(8,128)(2,1)S(1)}, u32[]{:S(2)}, u32[]{:S(2)}) collective-permute-start(bf16[2,128,512]{2,1,0:T(8,128)(2,1)S(1)} %get-tuple-element.97), channel_id=1, source_target_pairs={{0,2},{1,3},{2,0},{3,1},{4,6},{5,7},{6,4},{7,5},{8,10},{9,11},{10,... | collective-permute-start | bytes 786440 | tf_op jit(solution)/shard_map/ppermute | solution.py:65
  90.8 13.2 %collective-permute-start.24 = (bf16[2,128,512]{2,1,0:T(8,128)(2,1)S(1)}, bf16[2,128,512]{2,1,0:T(8,128)(2,1)S(1)}, u32[]{:S(2)}, u32[]{:S(2)}) collective-permute-start(bf16[2,128,512]{2,1,0:T(8,128)(2,1)S(1)} %get-tuple-element.98), channel_id=1, source_target_pairs={{0,7},{1,6},{2,5},{3,4},{4,3},{5,2},{6,1},{7,0},{8,15},{9,14},{10,... | collective-permute-start | bytes 786440 | tf_op jit(solution)/shard_map/ppermute | solution.py:65
  91.8 14.8 %collective-permute-start.27 = (bf16[1,128,512]{2,1,0:T(8,128)(2,1)S(1)}, bf16[1,128,512]{2,1,0:T(8,128)(2,1)S(1)}, u32[]{:S(2)}, u32[]{:S(2)}) collective-permute-start(bf16[1,128,512]{2,1,0:T(8,128)(2,1)S(1)} %get-tuple-element.106), channel_id=1, source_target_pairs={{0,1},{1,0},{2,3},{3,2},{4,5},{5,4},{6,7},{7,6},{8,9},{9,8},{10,11... | collective-permute-start | bytes 393224 | tf_op jit(solution)/shard_map/ppermute | solution.py:65
  98.5 17.5 %collective-permute-start.28 = (bf16[1,128,512]{2,1,0:T(8,128)(2,1)S(1)}, bf16[1,128,512]{2,1,0:T(8,128)(2,1)S(1)}, u32[]{:S(2)}, u32[]{:S(2)}) collective-permute-start(bf16[1,128,512]{2,1,0:T(8,128)(2,1)S(1)} %get-tuple-element.108), channel_id=1, source_target_pairs={{0,3},{1,2},{2,1},{3,0},{4,7},{5,6},{6,5},{7,4},{8,11},{9,10},{10,... | collective-permute-start | bytes 393224 | tf_op jit(solution)/shard_map/ppermute | solution.py:65
  104.0 12.0 %collective-permute-start.29 = (bf16[1,128,512]{2,1,0:T(8,128)(2,1)S(1)}, bf16[1,128,512]{2,1,0:T(8,128)(2,1)S(1)}, u32[]{:S(2)}, u32[]{:S(2)}) collective-permute-start(bf16[1,128,512]{2,1,0:T(8,128)(2,1)S(1)} %get-tuple-element.109), channel_id=1, source_target_pairs={{0,6},{1,7},{2,4},{3,5},{4,2},{5,3},{6,0},{7,1},{8,14},{9,15},{10,... | collective-permute-start | bytes 393224 | tf_op jit(solution)/shard_map/ppermute | solution.py:65
  106.6 11.9 %collective-permute-start.32 = (bf16[1,128,512]{2,1,0:T(8,128)(2,1)S(1)}, bf16[1,128,512]{2,1,0:T(8,128)(2,1)S(1)}, u32[]{:S(2)}, u32[]{:S(2)}) collective-permute-start(bf16[1,128,512]{2,1,0:T(8,128)(2,1)S(1)} %slice.31), channel_id=1, source_target_pairs={{0,2},{1,3},{2,0},{3,1},{4,6},{5,7},{6,4},{7,5},{8,10},{9,11},{10,... | collective-permute-start | bytes 393224 | tf_op jit(solution)/shard_map/ppermute | solution.py:65
  122.5 14.7 %collective-permute-start.33 = (bf16[1024,512]{1,0:T(8,128)(2,1)S(1)}, bf16[1024,512]{1,0:T(8,128)(2,1)S(1)}, u32[]{:S(2)}, u32[]{:S(2)}) collective-permute-start(bf16[1024,512]{1,0:T(8,128)(2,1)S(1)} %shard_map.95), channel_id=1, source_target_pairs={{8,0},{16,8},{24,16},{0,24},{9,1},{17,9},{25,17},{1,25},{10,2},{18... | collective-permute-start | bytes 3145736 | tf_op jit(solution)/shard_map/ppermute | solution.py:288
  (8 other events, 36.1 us)

commit v5 on v4

--- a/solution.py
+++ b/solution.py
@@ -7,11 +7,13 @@
 
 STEPS = 4
 TILE = 512
+H0_FROM, H0_BY = 0, 0
+OUT1 = True
 
 teleport = 0.2
 strength = 1.5
 
-PART, STARTS, IDS = 0, 1, 1 + STEPS
+PART, ANCHOR, STAYS, STARTS, IDS = 0, 1, 2, 3, 3 + STEPS
 
 VMEM = pl.BlockSpec(memory_space=pltpu.VMEM)
 SMEM = pl.BlockSpec(memory_space=pltpu.SMEM)
@@ -60,9 +62,31 @@
     return [(hop, [hop] + via.get(hop, [])) for hop in order]
 
 
+def places(sections, step):
+    at = list(range(sections))
+    if sections == STEPS and step == STEPS - 1:
+        half = sections // 2
+        at[0], at[half] = half, 0
+    return at
+
+
+def layers_at(sections, step):
+    at = places(sections, step)
+    return [(at.index(s) + step) % sections for s in range(sections)]
+
+
 def swapped(value, offset):
     parts = lax.axis_size("dom")
     return lax.ppermute(value, "dom", [(i, i ^ offset) for i in range(parts)])
+
+
+def crossing(value, offset, step):
+    sections, parts = lax.axis_size("section"), lax.axis_size("dom")
+    to = places(sections, step)
+    if to == places(sections, 0):
+        return swapped(value, offset)
+    pairs = [(s * parts + i, to[s] * parts + (i ^ offset)) for s in range(sections) for i in range(parts)]
+    return lax.ppermute(value, ("section", "dom"), pairs)
 
 
 def passed_on(got, parts):
@@ -180,6 +204,46 @@
     )(fast(x), fast(h0), fast(adj))
 
 
+def changed_kernel(fresh, info, x, kept_h0, sent_h0, new_h0, adj, partial, h0, sem):
+    local = pltpu.make_async_copy(new_h0.at[fresh], h0, sem)
+
+    @pl.when(info[ANCHOR] == 2)
+    def _():
+        local.start()
+
+    spans = [slice(at, at + TILE) for at in range(0, x.shape[0], TILE)]
+    for rows in spans:
+        partial[rows] = (1.0 - teleport) * jnp.dot(adj[rows], x[...], preferred_element_type=jnp.float32)
+
+    def add(source):
+        for rows in spans:
+            partial[rows] += teleport * source[rows].astype(jnp.float32)
+
+    @pl.when(info[ANCHOR] == 0)
+    def _():
+        add(kept_h0)
+
+    @pl.when(info[ANCHOR] == 1)
+    def _():
+        add(sent_h0)
+
+    @pl.when(info[ANCHOR] == 2)
+    def _():
+        local.wait()
+        add(h0)
+
+
+def changed_part(fresh, info, x, kept_h0, sent_h0, new_h0, adj):
+    return pl.pallas_call(
+        lambda *refs: changed_kernel(fresh, *refs),
+        out_shape=pltpu.VMEM(x.shape, jnp.float32),
+        in_specs=[SMEM, VMEM, VMEM, VMEM, HBM, VMEM],
+        out_specs=VMEM,
+        scratch_shapes=[pltpu.VMEM(x.shape, x.dtype), pltpu.SemaphoreType.DMA],
+        compiler_params=LIMIT,
+    )(info, fast(x), fast(kept_h0), fast(sent_h0), far(new_h0), fast(adj))
+
+
 def gather_table(incoming, table):
     block = incoming[0].shape[1]
     for place, value in enumerate(incoming):
@@ -281,11 +345,30 @@
     )(*([fast(value)] if held is None else [fast(value), held]))
 
 
-def moved(value, by):
-    length = lax.axis_size("section")
-    if by % length == 0:
+def keep_one_kernel(step, info, first_value, second_value, _, held, sem):
+    for choice, value in enumerate((first_value, second_value)):
+
+        @pl.when(info[STAYS] == choice)
+        def _():
+            run([pltpu.make_async_copy(value, held.at[0, step], sem)])
+
+
+def kept_one(step, info, first_value, second_value, held):
+    return pl.pallas_call(
+        lambda *refs: keep_one_kernel(step, *refs),
+        out_shape=pltpu.HBM(held.shape, held.dtype),
+        in_specs=[SMEM, VMEM, VMEM, HBM],
+        out_specs=HBM,
+        scratch_shapes=[pltpu.SemaphoreType.DMA],
+        input_output_aliases={3: 0},
+        compiler_params=LIMIT,
+    )(info, fast(first_value), fast(second_value), held)
+
+
+def routed(value, pairs):
+    if all(source == target for source, target in pairs):
         return value
-    return lax.ppermute(value, "section", [((i + by) % length, i) for i in range(length)])
+    return lax.ppermute(value, "section", pairs)
 
 
 def body(carry_h, carry_h0, new_h0, weights, adj_blocks, col_index, counts, send_list):
@@ -294,12 +377,23 @@
     part = lax.axis_index("dom")
     parts = send_list.shape[0]
     block = adj_blocks.shape[-1]
-    place = section + jnp.arange(STEPS, dtype=jnp.int32)
-    layers = place % sections
+    tables = [layers_at(sections, t) for t in range(STEPS)]
+    last = STEPS - 1
+    at_last = places(sections, last)
+    changes = at_last != places(sections, 0)
+    steps = jnp.arange(STEPS, dtype=jnp.int32)
+    place = section + steps
+    half = sections // 2
+    leaves, enters = place == steps, place == steps + half
+    ahead = jnp.where(leaves, half, jnp.where(enters, -half, 0)) if changes else jnp.zeros_like(place)
+    layers = (place + jnp.where(steps == last, ahead, 0)) % sections
     beta = jnp.log(1.0 + strength / (layers.astype(jnp.float32) + 1.0))
+    stays = [int(at_last[s] == s) for s in range(sections)]
     info = jnp.concatenate(
         [
-            jnp.stack([part]).astype(jnp.int32),
+            part.astype(jnp.int32)[None],
+            jnp.where(leaves, 2, jnp.where(enters, 1, 0))[:1],
+            jnp.where(leaves | enters, 0, 1)[:1],
             (place == sections).astype(jnp.int32),
             lax.dynamic_index_in_dim(send_list, part, 0, keepdims=False),
         ]
@@ -311,34 +405,52 @@
     coming = {}
     moving = {}
     for t in range(STEPS):
-        got = [swapped(value, hop) for value, hop in zip(sent, hops)]
+        change = changes and t == last
+        got = [crossing(value, hop, t) for value, hop in zip(sent, hops)]
         if t == 0:
             counts, sent = lax.optimization_barrier((counts, sent))
             own_adj, early_adj, late_adj = merged(info, col_index, counts, adj_blocks, parts)
-        if t == 3:
-            current, moving[1] = lax.optimization_barrier((current, moving[1]))
-        partial = own_part(current, h0, own_adj)
+        if t == last and not change:
+            current, moving[t - 2] = lax.optimization_barrier((current, moving[t - 2]))
         passing = sum(len(carried) > 1 for _, carried in bundles(parts))
-        early, partial = lax.optimization_barrier((got[:passing], partial))
-        got = early + got[passing:]
+        early = got[:passing]
+        if change:
+            current = lax.ppermute(current, "section", [(s, at_last[s]) for s in range(sections)])
+            partial = changed_part(sections // 2 - 1, info, current, h0, other_h0, new_h0, own_adj)
+        else:
+            partial = own_part(current, h0, own_adj)
+            early, partial = lax.optimization_barrier((early, partial))
+            got = early + got[passing:]
         passed, offsets = passed_on(got, parts)
-        if t + 1 < STEPS:
+        if t < last:
             held_back, early, partial = lax.optimization_barrier((weights[0], early, partial))
-            coming[t + 1] = moved(held_back, t + 1)
+            coming[t + 1] = routed(held_back, [(layer_at, s) for s, layer_at in enumerate(tables[t + 1])])
+        if changes and t == H0_FROM:
+            other_h0 = lax.ppermute(carry_h0[0], "section", [(0, sections // 2)])
+        if changes and t == H0_BY:
+            partial, other_h0 = lax.optimization_barrier((partial, other_h0))
         if t > 0:
-            moving[t - 1] = moved(made, 1 - t)
-            if t == 3:
+            pairs = list(enumerate(tables[t - 1]))
+            if change:
+                pairs = [(s, to) for s, to in pairs if stays[s]]
+            moving[t - 1] = routed(made, pairs)
+            if t == last and not change:
                 partial, moving[t - 1] = lax.optimization_barrier((partial, moving[t - 1]))
+            if change and OUT1:
+                partial, moving[t - 2] = lax.optimization_barrier((partial, moving[t - 2]))
         partial = arrived(early_adj, partial, [value for _, value in sorted(zip(hops, got), key=lambda pair: pair[0])])
         passed = [value for _, value in sorted(zip(offsets, passed), key=lambda pair: pair[0])]
         made, *rest = layer(t, parts, info, beta, late_adj, partial, weight, new_h0, h0, passed)
         if rest:
             current, h0, *sent = rest
             weight = coming[t + 1]
-    moving[STEPS - 1] = moved(made, 1 - STEPS)
+    moving[last] = routed(made, list(enumerate(tables[last])))
     held = None
     for t in range(STEPS):
-        held = kept(t, moving[t], held)
+        if changes and t == last - 1:
+            held = kept_one(t, info, current, moving[t], held)
+        else:
+            held = kept(t, moving[t], held)
     return held
 
 

time: 138 us -> 134 us (0.971)
  waiting for transfers between devices: 56.4 us -> 25.8 us
  starting transfers between devices: 49.6 us -> 75.3 us
    ppermute x6 -> x13, starting transfers between devices: 18.3 us -> 49.4 us  [the longest x6 37.4 us: routed(): return lax.ppermute(value, 'section', pairs)]
    ppermute x28 -> x23, waiting for transfers between devices: 37.1 us -> 13.2 us  [swapped(): return lax.ppermute(value, 'dom', [(i, i ^ offset) for i in range(parts)])]
    ppermute x6 -> x13, waiting for transfers between devices: 19.3 us -> 12.6 us  [the longest x5 7.89 us: crossing(): return lax.ppermute(value, ('section', 'dom'), pairs)]
    ppermute x28 -> x23, starting transfers between devices: 31.3 us -> 25.9 us  [swapped(): return lax.ppermute(value, 'dom', [(i, i ^ offset) for i in range(parts)])]
    pallas_call x0 -> x2, Pallas kernels: none -> 3.56 us  [the longest x1 2.04 us: changed_part(): pl.pallas_call(lambda *refs: changed_kernel(fresh, *refs), out_shape=pltp...]
    pallas_call x4 -> x3, Pallas kernels: 5.09 us -> 3.83 us  [own_part(): pl.pallas_call(own_kernel, out_shape=pltpu.VMEM(x.shape, jnp.float32), in...]
    pallas_call x4 -> x3, Pallas kernels: 3.92 us -> 2.94 us  [kept(): pl.pallas_call(lambda *refs: keep_kernel(step, *refs), out_shape=pltpu.HB...]
  transfers between devices with their start and end apart: 34 -> 36, of which waited for: 17 -> 9; matrix products, arithmetic and copies ran while one was open for 0% -> 0% of each run, Pallas kernels for 18% -> 22%
where the time goes in v5:
time: 134 us
  starting transfers between devices  75.3 us (56%)
  Pallas kernels  30.6 us (23%)
  waiting for transfers between devices  25.8 us (19%)
  local copies, waits for them, and re-layouts  1.56 us (1%)
    ppermute x6, starting transfers between devices, routed(): return lax.ppermute(value, 'section', pairs)  37.4 us
    ppermute x23, starting transfers between devices, swapped(): return lax.ppermute(value, 'dom', [(i, i ^ offset) for i in range(parts)])  25.9 us
    ppermute x23, waiting for transfers between devices, swapped(): return lax.ppermute(value, 'dom', [(i, i ^ offset) for i in range(parts)])  13.2 us
    ppermute x5, starting transfers between devices, crossing(): return lax.ppermute(value, ('section', 'dom'), pairs)  10.2 us
    ppermute x5, waiting for transfers between devices, crossing(): return lax.ppermute(value, ('section', 'dom'), pairs)  7.89 us
    pallas_call x4, Pallas kernels, layer(): pl.pallas_call(lambda *refs: layer_kernel(step, parts, len(incoming), *re...  7.64 us
    pallas_call x1, Pallas kernels, merged(): pl.pallas_call(lambda *refs: merge_kernel(parts, *refs), out_shape=[pltpu...  6.45 us
    ppermute x6, waiting for transfers between devices, routed(): return lax.ppermute(value, 'section', pairs)  4.73 us
  transfers between devices with their start and end apart: 36, of which 9 were waited for; matrix products, arithmetic and copies ran while one was open for 0% of the time, Pallas kernels for 22%

profile of v5, /device:TPU:1, one launch (start us, length us, event | category | flops | bytes accessed | tf_op | source)
XLA Modules:
  0.0 133.9 jit_solution(14371530104551449220)
XLA Ops:
  1.0 1.9 %shard_map.82 = (bf16[2,128,512]{2,1,0:T(8,128)(2,1)S(1)}, bf16[2,128,512]{2,1,0:T(8,128)(2,1)S(1)}, bf16[1,128,512]{2,1,0:T(8,128)(2,1)S(1)}, bf16[1,128,512]{2,1,0:T(8,128)(2,1)S(1)}, bf16[1,128,512]{2,1,0:T(8,128)(2,1)S(1)}) custom-call(s32[15]{0:T(128)S(1)} %concatenate.3.refs_0_, bf16[1024,512]{1,0:T(8,128)(2,1)} %bitcast.8), custom_call_target="tpu_custom_call" | custom-call | tf_op jit(solution)/shard_map/pallas_call | solution.py:128
  2.9 2.2 %collective-permute-start = (bf16[2,128,512]{2,1,0:T(8,128)(2,1)S(1)}, bf16[2,128,512]{2,1,0:T(8,128)(2,1)S(1)}, u32[]{:S(2)}, u32[]{:S(2)}) collective-permute-start(bf16[2,128,512]{2,1,0:T(8,128)(2,1)S(1)} %get-tuple-element.57), channel_id=1, source_target_pairs={{0,2},{1,3},{2,0},{3,1},{4,6},{5,7},{6,4},{7,5},{8,10},{9,11},{10,... | collective-permute-start | bytes 786440 | tf_op jit(solution)/shard_map/ppermute | solution.py:80
  5.1 3.1 %collective-permute-start.1 = (bf16[2,128,512]{2,1,0:T(8,128)(2,1)S(1)}, bf16[2,128,512]{2,1,0:T(8,128)(2,1)S(1)}, u32[]{:S(2)}, u32[]{:S(2)}) collective-permute-start(bf16[2,128,512]{2,1,0:T(8,128)(2,1)S(1)} %get-tuple-element.58), channel_id=1, source_target_pairs={{0,7},{1,6},{2,5},{3,4},{4,3},{5,2},{6,1},{7,0},{8,15},{9,14},{10,... | collective-permute-start | bytes 786440 | tf_op jit(solution)/shard_map/ppermute | solution.py:80
  11.2 6.5 %shard_map.83 = (bf16[1024,1024]{1,0:T(8,128)(2,1)S(1)}, bf16[1024,640]{1,0:T(8,128)(2,1)S(1)}, bf16[1024,256]{1,0:T(8,128)(2,1)S(1)}) custom-call(s32[15]{0:T(128)S(1)} %concatenate.3.refs_0_, s32[8,24]{1,0:T(8,128)S(1)} %copy-done.4, s32[8]{0:T(128)S(1)} %copy-done.5, bf16[8,24,128,128]{3,2,1,0:T(8,128)(2,1)} %refs_3_.1), custom_call_target="tpu_custom_call" | custom-call | tf_op jit(solution)/shard_map/pallas_call | solution.py:174
  19.4 3.0 %collective-permute-start.6 = (bf16[1,128,512]{2,1,0:T(8,128)(2,1)S(1)}, bf16[1,128,512]{2,1,0:T(8,128)(2,1)S(1)}, u32[]{:S(2)}, u32[]{:S(2)}) collective-permute-start(bf16[1,128,512]{2,1,0:T(8,128)(2,1)S(1)} %slice.32), channel_id=1, source_target_pairs={{0,6},{1,7},{2,4},{3,5},{4,2},{5,3},{6,0},{7,1},{8,14},{9,15},{10,... | collective-permute-start | bytes 393224 | tf_op jit(solution)/shard_map/ppermute | solution.py:80
  22.4 5.2 %collective-permute-start.13 = (bf16[512,512]{1,0:T(8,128)(2,1)S(1)}, bf16[512,512]{1,0:T(8,128)(2,1)S(1)}, u32[]{:S(2)}, u32[]{:S(2)}) collective-permute-start(bf16[512,512]{1,0:T(8,128)(2,1)S(1)} %bitcast.13), channel_id=1, source_target_pairs={{8,0},{16,8},{24,16},{0,24},{9,1},{17,9},{25,17},{1,25},{10,2},{18... | collective-permute-start | bytes 1572872 | tf_op jit(solution)/shard_map/ppermute | solution.py:371
  28.8 1.8 %shard_map.86 = (bf16[1024,512]{1,0:T(8,128)(2,1)S(1)}, bf16[1024,512]{1,0:T(8,128)(2,1)S(1)}, bf16[1024,512]{1,0:T(8,128)(2,1)S(1)}, bf16[2,128,512]{2,1,0:T(8,...) custom-call(s32[15]{0:T(128)S(1)} %concatenate.3.refs_0_, ...), custom_call_target="tpu_custom_call" | custom-call | tf_op jit(solution)/shard_map/pallas_call | solution.py:320
  30.5 3.2 %collective-permute-start.8 = (bf16[2,128,512]{2,1,0:T(8,128)(2,1)S(1)}, bf16[2,128,512]{2,1,0:T(8,128)(2,1)S(1)}, u32[]{:S(2)}, u32[]{:S(2)}) collective-permute-start(bf16[2,128,512]{2,1,0:T(8,128)(2,1)S(1)} %get-tuple-element.71), channel_id=1, source_target_pairs={{0,2},{1,3},{2,0},{3,1},{4,6},{5,7},{6,4},{7,5},{8,10},{9,11},{10,... | collective-permute-start | bytes 786440 | tf_op jit(solution)/shard_map/ppermute | solution.py:80
  37.8 1.7 %collective-permute-start.12 = (bf16[1,128,512]{2,1,0:T(8,128)(2,1)S(1)}, bf16[1,128,512]{2,1,0:T(8,128)(2,1)S(1)}, u32[]{:S(2)}, u32[]{:S(2)}) collective-permute-start(bf16[1,128,512]{2,1,0:T(8,128)(2,1)S(1)} %get-tuple-element.81), channel_id=1, source_target_pairs={{0,6},{1,7},{2,4},{3,5},{4,2},{5,3},{6,0},{7,1},{8,14},{9,15},{10,... | collective-permute-start | bytes 393224 | tf_op jit(solution)/shard_map/ppermute | solution.py:80
  39.5 4.8 %collective-permute-done.9.rest_4_ = bf16[2,128,512]{2,1,0:T(8,128)(2,1)S(1)} collective-permute-done((bf16[2,128,512]{2,1,0:T(8,128)(2,1)S(1)}, bf16[2,128,512]{2,1,0:T(8,128)(2,1)S(1)}, u32[]{:S(2)}, u32[]{:S(2)}) %collective-permute-start.9) | collective-permute-done | bytes 262176 | tf_op jit(solution)/shard_map/ppermute | solution.py:80
  45.1 5.4 %collective-permute-start.21 = (bf16[512,512]{1,0:T(8,128)(2,1)S(1)}, bf16[512,512]{1,0:T(8,128)(2,1)S(1)}, u32[]{:S(2)}, u32[]{:S(2)}) collective-permute-start(bf16[512,512]{1,0:T(8,128)(2,1)S(1)} %bitcast.15), channel_id=1, source_target_pairs={{16,0},{24,8},{0,16},{8,24},{17,1},{25,9},{1,17},{9,25},{18,2},{26... | collective-permute-start | bytes 1572872 | tf_op jit(solution)/shard_map/ppermute | solution.py:371
  51.8 2.7 %collective-permute-done.15.refs_8_ = bf16[1,128,512]{2,1,0:T(8,128)(2,1)S(1)} collective-permute-done((bf16[1,128,512]{2,1,0:T(8,128)(2,1)S(1)}, bf16[1,128,512]{2,1,0:T(8,128)(2,1)S(1)}, u32[]{:S(2)}, u32[]{:S(2)}) %collective-permute-start.15) | collective-permute-done | bytes 131104 | tf_op jit(solution)/shard_map/ppermute | solution.py:80
  54.5 1.7 %shard_map.89 = (bf16[1024,512]{1,0:T(8,128)(2,1)S(1)}, bf16[1024,512]{1,0:T(8,128)(2,1)S(1)}, bf16[1024,512]{1,0:T(8,128)(2,1)S(1)}, bf16[2,128,512]{2,1,0:T(8,...) custom-call(s32[15]{0:T(128)S(1)} %concatenate.3.refs_0_, ...), custom_call_target="tpu_custom_call", output_to_operand_aliasing={{2}: (6, {})} | custom-call | tf_op jit(solution)/shard_map/pallas_call | solution.py:320
  57.2 1.9 %collective-permute-start.17 = (bf16[2,128,512]{2,1,0:T(8,128)(2,1)S(1)}, bf16[2,128,512]{2,1,0:T(8,128)(2,1)S(1)}, u32[]{:S(2)}, u32[]{:S(2)}) collective-permute-start(bf16[2,128,512]{2,1,0:T(8,128)(2,1)S(1)} %get-tuple-element.84), channel_id=1, source_target_pairs={{0,7},{1,6},{2,5},{3,4},{4,3},{5,2},{6,1},{7,0},{8,15},{9,14},{10,... | collective-permute-start | bytes 786440 | tf_op jit(solution)/shard_map/ppermute | solution.py:80
  61.8 1.8 %collective-permute-start.20 = (bf16[1,128,512]{2,1,0:T(8,128)(2,1)S(1)}, bf16[1,128,512]{2,1,0:T(8,128)(2,1)S(1)}, u32[]{:S(2)}, u32[]{:S(2)}) collective-permute-start(bf16[1,128,512]{2,1,0:T(8,128)(2,1)S(1)} %get-tuple-element.93), channel_id=1, source_target_pairs={{0,6},{1,7},{2,4},{3,5},{4,2},{5,3},{6,0},{7,1},{8,14},{9,15},{10,... | collective-permute-start | bytes 393224 | tf_op jit(solution)/shard_map/ppermute | solution.py:80
  63.6 2.9 %collective-permute-done.17.rest_4_ = bf16[2,128,512]{2,1,0:T(8,128)(2,1)S(1)} collective-permute-done((bf16[2,128,512]{2,1,0:T(8,128)(2,1)S(1)}, bf16[2,128,512]{2,1,0:T(8,128)(2,1)S(1)}, u32[]{:S(2)}, u32[]{:S(2)}) %collective-permute-start.17) | collective-permute-done | bytes 262176 | tf_op jit(solution)/shard_map/ppermute | solution.py:80
  66.5 1.9 %collective-permute-start.22 = (bf16[1,128,512]{2,1,0:T(8,128)(2,1)S(1)}, bf16[1,128,512]{2,1,0:T(8,128)(2,1)S(1)}, u32[]{:S(2)}, u32[]{:S(2)}) collective-permute-start(bf16[1,128,512]{2,1,0:T(8,128)(2,1)S(1)} %slice.36), channel_id=1, source_target_pairs={{0,6},{1,7},{2,4},{3,5},{4,2},{5,3},{6,0},{7,1},{8,14},{9,15},{10,... | collective-permute-start | bytes 393224 | tf_op jit(solution)/shard_map/ppermute | solution.py:80
  68.4 14.7 %collective-permute-start.25 = (bf16[1024,512]{1,0:T(8,128)(2,1)S(1)}, bf16[1024,512]{1,0:T(8,128)(2,1)S(1)}, u32[]{:S(2)}, u32[]{:S(2)}) collective-permute-start(bf16[1024,512]{1,0:T(8,128)(2,1)S(1)} %get-tuple-element.98), channel_id=1, source_target_pairs={{0,8},{8,16},{16,24},{24,0},{1,9},{9,17},{17,25},{25,1},{2,10},{10... | collective-permute-start | bytes 3145736 | tf_op jit(solution)/shard_map/ppermute | solution.py:371
  84.3 2.6 %shard_map.92 = (bf16[1024,512]{1,0:T(8,128)(2,1)S(1)}, bf16[1024,512]{1,0:T(8,128)(2,1)S(1)}, bf16[1024,512]{1,0:T(8,128)(2,1)S(1)}, bf16[2,128,512]{2,1,0:T(8,...) custom-call(s32[15]{0:T(128)S(1)} %concatenate.3.refs_0_, ...), custom_call_target="tpu_custom_call", output_to_operand_aliasing={{2}: (6, {})} | custom-call | tf_op jit(solution)/shard_map/pallas_call | solution.py:320
  87.8 1.8 %collective-permute-start.27 = (bf16[2,128,512]{2,1,0:T(8,128)(2,1)S(1)}, bf16[2,128,512]{2,1,0:T(8,128)(2,1)S(1)}, u32[]{:S(2)}, u32[]{:S(2)}) collective-permute-start(bf16[2,128,512]{2,1,0:T(8,128)(2,1)S(1)} %get-tuple-element.101), channel_id=1, source_target_pairs={{0,18},{1,19},{2,16},{3,17},{4,22},{5,23},{6,20},{7,21},{8,10},{9,... | collective-permute-start | bytes 786440 | tf_op jit(solution)/shard_map/ppermute | solution.py:89
  89.6 3.7 %collective-permute-start.31 = (bf16[512,512]{1,0:T(8,128)(2,1)S(1)}, bf16[512,512]{1,0:T(8,128)(2,1)S(1)}, u32[]{:S(2)}, u32[]{:S(2)}) collective-permute-start(bf16[512,512]{1,0:T(8,128)(2,1)S(1)} %bitcast.16), channel_id=1, source_target_pairs={{8,0},{0,8},{24,16},{16,24},{9,1},{1,9},{25,17},{17,25},{10,2},{2,... | collective-permute-start | bytes 1572872 | tf_op jit(solution)/shard_map/ppermute | solution.py:371
  93.2 1.8 %collective-permute-start.30 = (bf16[2,128,512]{2,1,0:T(8,128)(2,1)S(1)}, bf16[2,128,512]{2,1,0:T(8,128)(2,1)S(1)}, u32[]{:S(2)}, u32[]{:S(2)}) collective-permute-start(bf16[2,128,512]{2,1,0:T(8,128)(2,1)S(1)} %get-tuple-element.104), channel_id=1, source_target_pairs={{0,23},{1,22},{2,21},{3,20},{4,19},{5,18},{6,17},{7,16},{8,15},{9,... | collective-permute-start | bytes 786440 | tf_op jit(solution)/shard_map/ppermute | solution.py:89
  95.7 7.9 %collective-permute-done.30.rest_4_ = bf16[2,128,512]{2,1,0:T(8,128)(2,1)S(1)} collective-permute-done((bf16[2,128,512]{2,1,0:T(8,128)(2,1)S(1)}, bf16[2,128,512]{2,1,0:T(8,128)(2,1)S(1)}, u32[]{:S(2)}, u32[]{:S(2)}) %collective-permute-start.30) | collective-permute-done | bytes 262176 | tf_op jit(solution)/shard_map/ppermute | solution.py:89
  103.6 4.3 %collective-permute-start.28 = (bf16[1,128,512]{2,1,0:T(8,128)(2,1)S(1)}, bf16[1,128,512]{2,1,0:T(8,128)(2,1)S(1)}, u32[]{:S(2)}, u32[]{:S(2)}) collective-permute-start(bf16[1,128,512]{2,1,0:T(8,128)(2,1)S(1)} %get-tuple-element.102), channel_id=1, source_target_pairs={{0,19},{1,18},{2,17},{3,16},{4,23},{5,22},{6,21},{7,20},{8,11},{9,... | collective-permute-start | bytes 393224 | tf_op jit(solution)/shard_map/ppermute | solution.py:89
  107.9 1.7 %collective-permute-start.29 = (bf16[1,128,512]{2,1,0:T(8,128)(2,1)S(1)}, bf16[1,128,512]{2,1,0:T(8,128)(2,1)S(1)}, u32[]{:S(2)}, u32[]{:S(2)}) collective-permute-start(bf16[1,128,512]{2,1,0:T(8,128)(2,1)S(1)} %get-tuple-element.103), channel_id=1, source_target_pairs={{0,22},{1,23},{2,20},{3,21},{4,18},{5,19},{6,16},{7,17},{8,14},{9,... | collective-permute-start | bytes 393224 | tf_op jit(solution)/shard_map/ppermute | solution.py:89
  109.6 1.7 %collective-permute-start.32 = (bf16[1,128,512]{2,1,0:T(8,128)(2,1)S(1)}, bf16[1,128,512]{2,1,0:T(8,128)(2,1)S(1)}, u32[]{:S(2)}, u32[]{:S(2)}) collective-permute-start(bf16[1,128,512]{2,1,0:T(8,128)(2,1)S(1)} %slice.40), channel_id=1, source_target_pairs={{0,6},{1,7},{2,4},{3,5},{4,2},{5,3},{6,0},{7,1},{8,14},{9,15},{10,... | collective-permute-start | bytes 393224 | tf_op jit(solution)/shard_map/ppermute | solution.py:80
  111.2 2.0 %shard_map.93.partial = f32[1024,512]{1,0:T(8,128)S(1)} custom-call(s32[15]{0:T(128)S(1)} %concatenate.3.refs_0_, bf16[1024,512]{1,0:T(8,128)(2,1)S(1)} %collective-permute-done.24.refs_1_, bf16[1024,512]{1,0:T(8,128)(2,1)S(1)} %get-tuple-element.96.refs_2_.refs_6_, bf16[1024,512]{1,0:T(8,128)(2,1)S(1)} %collective-permute-done.2.refs_3_, ...), custom_call_target="tpu_custom_call" | custom-call | tf_op jit(solution)/shard_map/pallas_call | solution.py:237
  113.3 5.1 %collective-permute-start.35 = (bf16[1024,512]{1,0:T(8,128)(2,1)S(1)}, bf16[1024,512]{1,0:T(8,128)(2,1)S(1)}, u32[]{:S(2)}, u32[]{:S(2)}) collective-permute-start(bf16[1024,512]{1,0:T(8,128)(2,1)S(1)} %get-tuple-element.106), channel_id=1, source_target_pairs={{8,24},{24,8},{9,25},{25,9},{10,26},{26,10},{11,27},{27,11},{12,28... | collective-permute-start | bytes 3145736 | tf_op jit(solution)/shard_map/ppermute | solution.py:371
  119.5 1.6 %shard_map.95 = bf16[1024,512]{1,0:T(8,128)(2,1)S(1)} custom-call(s32[15]{0:T(128)S(1)} %concatenate.3.refs_0_, f32[4]{0:T(128)S(1)} %fusion.5.refs_1_, bf16[1024,256]{1,0:T(8,128)(2,1)S(1)} %get-tuple-element.63.refs_2_, f32[1024,512]{1,0:T(8,128)S(1)} %shard_map.94.refs_3_, bf16[512,512]{1,0:T(8,128)(2,1)S(1)} %collective-permute-done.31.refs_4_, ...), custom_call_target="tpu_custom_call" | custom-call | tf_op jit(solution)/shard_map/pallas_call | solution.py:320
  121.1 3.5 %collective-permute-start.34 = (bf16[1024,512]{1,0:T(8,128)(2,1)S(1)}, bf16[1024,512]{1,0:T(8,128)(2,1)S(1)}, u32[]{:S(2)}, u32[]{:S(2)}) collective-permute-start(bf16[1024,512]{1,0:T(8,128)(2,1)S(1)} %shard_map.95), channel_id=1, source_target_pairs={{0,8},{8,0},{16,24},{24,16},{1,9},{9,1},{17,25},{25,17},{2,10},{10... | collective-permute-start | bytes 3145736 | tf_op jit(solution)/shard_map/ppermute | solution.py:371
  126.5 4.7 %collective-permute-done.35.refs_2_ = bf16[1024,512]{1,0:T(8,128)(2,1)S(1)} collective-permute-done((bf16[1024,512]{1,0:T(8,128)(2,1)S(1)}, bf16[1024,512]{1,0:T(8,128)(2,1)S(1)}, u32[]{:S(2)}, u32[]{:S(2)}) %collective-permute-start.35) | collective-permute-done | bytes 1048608 | tf_op jit(solution)/shard_map/ppermute | solution.py:371
  131.2 1.5 %shard_map.98.refs_1_ = bf16[1,4,1024,512]{3,2,1,0:T(8,128)(2,1)} custom-call(s32[15]{0:T(128)S(1)} %concatenate.3.refs_0_, bf16[1024,512]{1,0:T(8,128)(2,1)S(1)} %collective-permute-done.24.refs_1_, bf16[1024,512]{1,0:T(8,128)(2,1)S(1)} %collective-permute-done.35.refs_2_, bf16[1,4,1024,512]{3,2,1,0:T(8,128)(2,1)} %shard_map.97.refs_3_), custom_call_target="tpu_custom_call", output_to_operand_aliasing={{}: (3, {})} | custom-call | tf_op jit(solution)/shard_map/pallas_call | solution.py:357
  (83 shorter events, 23.3 us)
Async XLA Ops:
  0.0 22.4 %collective-permute-start.2 = (bf16[1024,512]{1,0:T(8,128)(2,1)}, bf16[1024,512]{1,0:T(8,128)(2,1)S(1)}, u32[]{:S(2)}, u32[]{:S(2)}) collective-permute-start(bf16[1024,512]{1,0:T(8,128)(2,1)} %bitcast.10), channel_id=1, source_target_pairs={{0,16},{1,17},{2,18},{3,19},{4,20},{5,21},{6,22},{7,23}} | collective-permute-start | bytes 3145736 | tf_op jit(solution)/shard_map/ppermute | solution.py:429
  2.9 16.1 %collective-permute-start = (bf16[2,128,512]{2,1,0:T(8,128)(2,1)S(1)}, bf16[2,128,512]{2,1,0:T(8,128)(2,1)S(1)}, u32[]{:S(2)}, u32[]{:S(2)}) collective-permute-start(bf16[2,128,512]{2,1,0:T(8,128)(2,1)S(1)} %get-tuple-element.57), channel_id=1, source_target_pairs={{0,2},{1,3},{2,0},{3,1},{4,6},{5,7},{6,4},{7,5},{8,10},{9,11},{10,... | collective-permute-start | bytes 786440 | tf_op jit(solution)/shard_map/ppermute | solution.py:80
  5.1 14.2 %collective-permute-start.1 = (bf16[2,128,512]{2,1,0:T(8,128)(2,1)S(1)}, bf16[2,128,512]{2,1,0:T(8,128)(2,1)S(1)}, u32[]{:S(2)}, u32[]{:S(2)}) collective-permute-start(bf16[2,128,512]{2,1,0:T(8,128)(2,1)S(1)} %get-tuple-element.58), channel_id=1, source_target_pairs={{0,7},{1,6},{2,5},{3,4},{4,3},{5,2},{6,1},{7,0},{8,15},{9,14},{10,... | collective-permute-start | bytes 786440 | tf_op jit(solution)/shard_map/ppermute | solution.py:80
  8.2 14.2 %collective-permute-start.3 = (bf16[1,128,512]{2,1,0:T(8,128)(2,1)S(1)}, bf16[1,128,512]{2,1,0:T(8,128)(2,1)S(1)}, u32[]{:S(2)}, u32[]{:S(2)}) collective-permute-start(bf16[1,128,512]{2,1,0:T(8,128)(2,1)S(1)} %get-tuple-element.59), channel_id=1, source_target_pairs={{0,1},{1,0},{2,3},{3,2},{4,5},{5,4},{6,7},{7,6},{8,9},{9,8},{10,11... | collective-permute-start | bytes 393224 | tf_op jit(solution)/shard_map/ppermute | solution.py:80
  8.5 19.2 %collective-permute-start.4 = (bf16[1,128,512]{2,1,0:T(8,128)(2,1)S(1)}, bf16[1,128,512]{2,1,0:T(8,128)(2,1)S(1)}, u32[]{:S(2)}, u32[]{:S(2)}) collective-permute-start(bf16[1,128,512]{2,1,0:T(8,128)(2,1)S(1)} %get-tuple-element.60), channel_id=1, source_target_pairs={{0,3},{1,2},{2,1},{3,0},{4,7},{5,6},{6,5},{7,4},{8,11},{9,10},{10,... | collective-permute-start | bytes 393224 | tf_op jit(solution)/shard_map/ppermute | solution.py:80
  19.0 8.7 %collective-permute-start.5 = (bf16[1,128,512]{2,1,0:T(8,128)(2,1)S(1)}, bf16[1,128,512]{2,1,0:T(8,128)(2,1)S(1)}, u32[]{:S(2)}, u32[]{:S(2)}) collective-permute-start(bf16[1,128,512]{2,1,0:T(8,128)(2,1)S(1)} %get-tuple-element.61), channel_id=1, source_target_pairs={{0,6},{1,7},{2,4},{3,5},{4,2},{5,3},{6,0},{7,1},{8,14},{9,15},{10,... | collective-permute-start | bytes 393224 | tf_op jit(solution)/shard_map/ppermute | solution.py:80
  19.4 9.4 %collective-permute-start.6 = (bf16[1,128,512]{2,1,0:T(8,128)(2,1)S(1)}, bf16[1,128,512]{2,1,0:T(8,128)(2,1)S(1)}, u32[]{:S(2)}, u32[]{:S(2)}) collective-permute-start(bf16[1,128,512]{2,1,0:T(8,128)(2,1)S(1)} %slice.32), channel_id=1, source_target_pairs={{0,6},{1,7},{2,4},{3,5},{4,2},{5,3},{6,0},{7,1},{8,14},{9,15},{10,... | collective-permute-start | bytes 393224 | tf_op jit(solution)/shard_map/ppermute | solution.py:80
  22.4 29.1 %collective-permute-start.13 = (bf16[512,512]{1,0:T(8,128)(2,1)S(1)}, bf16[512,512]{1,0:T(8,128)(2,1)S(1)}, u32[]{:S(2)}, u32[]{:S(2)}) collective-permute-start(bf16[512,512]{1,0:T(8,128)(2,1)S(1)} %bitcast.13), channel_id=1, source_target_pairs={{8,0},{16,8},{24,16},{0,24},{9,1},{17,9},{25,17},{1,25},{10,2},{18... | collective-permute-start | bytes 1572872 | tf_op jit(solution)/shard_map/ppermute | solution.py:371
  33.7 10.6 %collective-permute-start.9 = (bf16[2,128,512]{2,1,0:T(8,128)(2,1)S(1)}, bf16[2,128,512]{2,1,0:T(8,128)(2,1)S(1)}, u32[]{:S(2)}, u32[]{:S(2)}) collective-permute-start(bf16[2,128,512]{2,1,0:T(8,128)(2,1)S(1)} %get-tuple-element.72), channel_id=1, source_target_pairs={{0,7},{1,6},{2,5},{3,4},{4,3},{5,2},{6,1},{7,0},{8,15},{9,14},{10,... | collective-permute-start | bytes 786440 | tf_op jit(solution)/shard_map/ppermute | solution.py:80
  33.7 10.7 %collective-permute-start.10 = (bf16[1,128,512]{2,1,0:T(8,128)(2,1)S(1)}, bf16[1,128,512]{2,1,0:T(8,128)(2,1)S(1)}, u32[]{:S(2)}, u32[]{:S(2)}) collective-permute-start(bf16[1,128,512]{2,1,0:T(8,128)(2,1)S(1)} %get-tuple-element.79), channel_id=1, source_target_pairs={{0,1},{1,0},{2,3},{3,2},{4,5},{5,4},{6,7},{7,6},{8,9},{9,8},{10,11... | collective-permute-start | bytes 393224 | tf_op jit(solution)/shard_map/ppermute | solution.py:80
  34.8 10.3 %collective-permute-start.11 = (bf16[1,128,512]{2,1,0:T(8,128)(2,1)S(1)}, bf16[1,128,512]{2,1,0:T(8,128)(2,1)S(1)}, u32[]{:S(2)}, u32[]{:S(2)}) collective-permute-start(bf16[1,128,512]{2,1,0:T(8,128)(2,1)S(1)} %get-tuple-element.80), channel_id=1, source_target_pairs={{0,3},{1,2},{2,1},{3,0},{4,7},{5,6},{6,5},{7,4},{8,11},{9,10},{10,... | collective-permute-start | bytes 393224 | tf_op jit(solution)/shard_map/ppermute | solution.py:80
  37.8 12.7 %collective-permute-start.12 = (bf16[1,128,512]{2,1,0:T(8,128)(2,1)S(1)}, bf16[1,128,512]{2,1,0:T(8,128)(2,1)S(1)}, u32[]{:S(2)}, u32[]{:S(2)}) collective-permute-start(bf16[1,128,512]{2,1,0:T(8,128)(2,1)S(1)} %get-tuple-element.81), channel_id=1, source_target_pairs={{0,6},{1,7},{2,4},{3,5},{4,2},{5,3},{6,0},{7,1},{8,14},{9,15},{10,... | collective-permute-start | bytes 393224 | tf_op jit(solution)/shard_map/ppermute | solution.py:80
  44.4 7.4 %collective-permute-start.14 = (bf16[1,128,512]{2,1,0:T(8,128)(2,1)S(1)}, bf16[1,128,512]{2,1,0:T(8,128)(2,1)S(1)}, u32[]{:S(2)}, u32[]{:S(2)}) collective-permute-start(bf16[1,128,512]{2,1,0:T(8,128)(2,1)S(1)} %slice.34), channel_id=1, source_target_pairs={{0,6},{1,7},{2,4},{3,5},{4,2},{5,3},{6,0},{7,1},{8,14},{9,15},{10,... | collective-permute-start | bytes 393224 | tf_op jit(solution)/shard_map/ppermute | solution.py:80
  44.5 10.1 %collective-permute-start.15 = (bf16[1,128,512]{2,1,0:T(8,128)(2,1)S(1)}, bf16[1,128,512]{2,1,0:T(8,128)(2,1)S(1)}, u32[]{:S(2)}, u32[]{:S(2)}) collective-permute-start(bf16[1,128,512]{2,1,0:T(8,128)(2,1)S(1)} %slice.35), channel_id=1, source_target_pairs={{0,2},{1,3},{2,0},{3,1},{4,6},{5,7},{6,4},{7,5},{8,10},{9,11},{10,... | collective-permute-start | bytes 393224 | tf_op jit(solution)/shard_map/ppermute | solution.py:80
  45.1 39.2 %collective-permute-start.21 = (bf16[512,512]{1,0:T(8,128)(2,1)S(1)}, bf16[512,512]{1,0:T(8,128)(2,1)S(1)}, u32[]{:S(2)}, u32[]{:S(2)}) collective-permute-start(bf16[512,512]{1,0:T(8,128)(2,1)S(1)} %bitcast.15), channel_id=1, source_target_pairs={{16,0},{24,8},{0,16},{8,24},{17,1},{25,9},{1,17},{9,25},{18,2},{26... | collective-permute-start | bytes 1572872 | tf_op jit(solution)/shard_map/ppermute | solution.py:371
  57.2 9.3 %collective-permute-start.17 = (bf16[2,128,512]{2,1,0:T(8,128)(2,1)S(1)}, bf16[2,128,512]{2,1,0:T(8,128)(2,1)S(1)}, u32[]{:S(2)}, u32[]{:S(2)}) collective-permute-start(bf16[2,128,512]{2,1,0:T(8,128)(2,1)S(1)} %get-tuple-element.84), channel_id=1, source_target_pairs={{0,7},{1,6},{2,5},{3,4},{4,3},{5,2},{6,1},{7,0},{8,15},{9,14},{10,... | collective-permute-start | bytes 786440 | tf_op jit(solution)/shard_map/ppermute | solution.py:80
  59.1 9.4 %collective-permute-start.18 = (bf16[1,128,512]{2,1,0:T(8,128)(2,1)S(1)}, bf16[1,128,512]{2,1,0:T(8,128)(2,1)S(1)}, u32[]{:S(2)}, u32[]{:S(2)}) collective-permute-start(bf16[1,128,512]{2,1,0:T(8,128)(2,1)S(1)} %get-tuple-element.91), channel_id=1, source_target_pairs={{0,1},{1,0},{2,3},{3,2},{4,5},{5,4},{6,7},{7,6},{8,9},{9,8},{10,11... | collective-permute-start | bytes 393224 | tf_op jit(solution)/shard_map/ppermute | solution.py:80
  59.7 8.7 %collective-permute-start.19 = (bf16[1,128,512]{2,1,0:T(8,128)(2,1)S(1)}, bf16[1,128,512]{2,1,0:T(8,128)(2,1)S(1)}, u32[]{:S(2)}, u32[]{:S(2)}) collective-permute-start(bf16[1,128,512]{2,1,0:T(8,128)(2,1)S(1)} %get-tuple-element.92), channel_id=1, source_target_pairs={{0,3},{1,2},{2,1},{3,0},{4,7},{5,6},{6,5},{7,4},{8,11},{9,10},{10,... | collective-permute-start | bytes 393224 | tf_op jit(solution)/shard_map/ppermute | solution.py:80
  61.8 21.4 %collective-permute-start.20 = (bf16[1,128,512]{2,1,0:T(8,128)(2,1)S(1)}, bf16[1,128,512]{2,1,0:T(8,128)(2,1)S(1)}, u32[]{:S(2)}, u32[]{:S(2)}) collective-permute-start(bf16[1,128,512]{2,1,0:T(8,128)(2,1)S(1)} %get-tuple-element.93), channel_id=1, source_target_pairs={{0,6},{1,7},{2,4},{3,5},{4,2},{5,3},{6,0},{7,1},{8,14},{9,15},{10,... | collective-permute-start | bytes 393224 | tf_op jit(solution)/shard_map/ppermute | solution.py:80
  66.5 17.7 %collective-permute-start.22 = (bf16[1,128,512]{2,1,0:T(8,128)(2,1)S(1)}, bf16[1,128,512]{2,1,0:T(8,128)(2,1)S(1)}, u32[]{:S(2)}, u32[]{:S(2)}) collective-permute-start(bf16[1,128,512]{2,1,0:T(8,128)(2,1)S(1)} %slice.36), channel_id=1, source_target_pairs={{0,6},{1,7},{2,4},{3,5},{4,2},{5,3},{6,0},{7,1},{8,14},{9,15},{10,... | collective-permute-start | bytes 393224 | tf_op jit(solution)/shard_map/ppermute | solution.py:80
  68.4 15.9 %collective-permute-start.23 = (bf16[1,128,512]{2,1,0:T(8,128)(2,1)S(1)}, bf16[1,128,512]{2,1,0:T(8,128)(2,1)S(1)}, u32[]{:S(2)}, u32[]{:S(2)}) collective-permute-start(bf16[1,128,512]{2,1,0:T(8,128)(2,1)S(1)} %slice.37), channel_id=1, source_target_pairs={{0,2},{1,3},{2,0},{3,1},{4,6},{5,7},{6,4},{7,5},{8,10},{9,11},{10,... | collective-permute-start | bytes 393224 | tf_op jit(solution)/shard_map/ppermute | solution.py:80
  68.4 41.1 %collective-permute-start.25 = (bf16[1024,512]{1,0:T(8,128)(2,1)S(1)}, bf16[1024,512]{1,0:T(8,128)(2,1)S(1)}, u32[]{:S(2)}, u32[]{:S(2)}) collective-permute-start(bf16[1024,512]{1,0:T(8,128)(2,1)S(1)} %get-tuple-element.98), channel_id=1, source_target_pairs={{0,8},{8,16},{16,24},{24,0},{1,9},{9,17},{17,25},{25,1},{2,10},{10... | collective-permute-start | bytes 3145736 | tf_op jit(solution)/shard_map/ppermute | solution.py:371
  86.9 24.3 %collective-permute-start.24 = (bf16[1024,512]{1,0:T(8,128)(2,1)S(1)}, bf16[1024,512]{1,0:T(8,128)(2,1)S(1)}, u32[]{:S(2)}, u32[]{:S(2)}) collective-permute-start(bf16[1024,512]{1,0:T(8,128)(2,1)S(1)} %get-tuple-element.95), channel_id=1, source_target_pairs={{0,16},{8,8},{16,0},{24,24},{1,17},{9,9},{17,1},{25,25},{2,18},{10... | collective-permute-start | bytes 3145736 | tf_op jit(solution)/shard_map/ppermute | solution.py:418
  89.6 29.9 %collective-permute-start.31 = (bf16[512,512]{1,0:T(8,128)(2,1)S(1)}, bf16[512,512]{1,0:T(8,128)(2,1)S(1)}, u32[]{:S(2)}, u32[]{:S(2)}) collective-permute-start(bf16[512,512]{1,0:T(8,128)(2,1)S(1)} %bitcast.16), channel_id=1, source_target_pairs={{8,0},{0,8},{24,16},{16,24},{9,1},{1,9},{25,17},{17,25},{10,2},{2,... | collective-permute-start | bytes 1572872 | tf_op jit(solution)/shard_map/ppermute | solution.py:371
  93.2 10.4 %collective-permute-start.30 = (bf16[2,128,512]{2,1,0:T(8,128)(2,1)S(1)}, bf16[2,128,512]{2,1,0:T(8,128)(2,1)S(1)}, u32[]{:S(2)}, u32[]{:S(2)}) collective-permute-start(bf16[2,128,512]{2,1,0:T(8,128)(2,1)S(1)} %get-tuple-element.104), channel_id=1, source_target_pairs={{0,23},{1,22},{2,21},{3,20},{4,19},{5,18},{6,17},{7,16},{8,15},{9,... | collective-permute-start | bytes 786440 | tf_op jit(solution)/shard_map/ppermute | solution.py:89
  95.1 12.8 %collective-permute-start.26 = (bf16[1,128,512]{2,1,0:T(8,128)(2,1)S(1)}, bf16[1,128,512]{2,1,0:T(8,128)(2,1)S(1)}, u32[]{:S(2)}, u32[]{:S(2)}) collective-permute-start(bf16[1,128,512]{2,1,0:T(8,128)(2,1)S(1)} %get-tuple-element.100), channel_id=1, source_target_pairs={{0,17},{1,16},{2,19},{3,18},{4,21},{5,20},{6,23},{7,22},{8,9},{9,8... | collective-permute-start | bytes 393224 | tf_op jit(solution)/shard_map/ppermute | solution.py:89
  103.6 9.7 %collective-permute-start.28 = (bf16[1,128,512]{2,1,0:T(8,128)(2,1)S(1)}, bf16[1,128,512]{2,1,0:T(8,128)(2,1)S(1)}, u32[]{:S(2)}, u32[]{:S(2)}) collective-permute-start(bf16[1,128,512]{2,1,0:T(8,128)(2,1)S(1)} %get-tuple-element.102), channel_id=1, source_target_pairs={{0,19},{1,18},{2,17},{3,16},{4,23},{5,22},{6,21},{7,20},{8,11},{9,... | collective-permute-start | bytes 393224 | tf_op jit(solution)/shard_map/ppermute | solution.py:89
  107.9 10.5 %collective-permute-start.29 = (bf16[1,128,512]{2,1,0:T(8,128)(2,1)S(1)}, bf16[1,128,512]{2,1,0:T(8,128)(2,1)S(1)}, u32[]{:S(2)}, u32[]{:S(2)}) collective-permute-start(bf16[1,128,512]{2,1,0:T(8,128)(2,1)S(1)} %get-tuple-element.103), channel_id=1, source_target_pairs={{0,22},{1,23},{2,20},{3,21},{4,18},{5,19},{6,16},{7,17},{8,14},{9,... | collective-permute-start | bytes 393224 | tf_op jit(solution)/shard_map/ppermute | solution.py:89
  109.6 9.9 %collective-permute-start.32 = (bf16[1,128,512]{2,1,0:T(8,128)(2,1)S(1)}, bf16[1,128,512]{2,1,0:T(8,128)(2,1)S(1)}, u32[]{:S(2)}, u32[]{:S(2)}) collective-permute-start(bf16[1,128,512]{2,1,0:T(8,128)(2,1)S(1)} %slice.40), channel_id=1, source_target_pairs={{0,6},{1,7},{2,4},{3,5},{4,2},{5,3},{6,0},{7,1},{8,14},{9,15},{10,... | collective-permute-start | bytes 393224 | tf_op jit(solution)/shard_map/ppermute | solution.py:80
  111.2 8.2 %collective-permute-start.33 = (bf16[1,128,512]{2,1,0:T(8,128)(2,1)S(1)}, bf16[1,128,512]{2,1,0:T(8,128)(2,1)S(1)}, u32[]{:S(2)}, u32[]{:S(2)}) collective-permute-start(bf16[1,128,512]{2,1,0:T(8,128)(2,1)S(1)} %slice.41), channel_id=1, source_target_pairs={{0,2},{1,3},{2,0},{3,1},{4,6},{5,7},{6,4},{7,5},{8,10},{9,11},{10,... | collective-permute-start | bytes 393224 | tf_op jit(solution)/shard_map/ppermute | solution.py:80
  113.3 17.9 %collective-permute-start.35 = (bf16[1024,512]{1,0:T(8,128)(2,1)S(1)}, bf16[1024,512]{1,0:T(8,128)(2,1)S(1)}, u32[]{:S(2)}, u32[]{:S(2)}) collective-permute-start(bf16[1024,512]{1,0:T(8,128)(2,1)S(1)} %get-tuple-element.106), channel_id=1, source_target_pairs={{8,24},{24,8},{9,25},{25,9},{10,26},{26,10},{11,27},{27,11},{12,28... | collective-permute-start | bytes 3145736 | tf_op jit(solution)/shard_map/ppermute | solution.py:371
  121.1 11.7 %collective-permute-start.34 = (bf16[1024,512]{1,0:T(8,128)(2,1)S(1)}, bf16[1024,512]{1,0:T(8,128)(2,1)S(1)}, u32[]{:S(2)}, u32[]{:S(2)}) collective-permute-start(bf16[1024,512]{1,0:T(8,128)(2,1)S(1)} %shard_map.95), channel_id=1, source_target_pairs={{0,8},{8,0},{16,24},{24,16},{1,9},{9,1},{17,25},{25,17},{2,10},{10... | collective-permute-start | bytes 3145736 | tf_op jit(solution)/shard_map/ppermute | solution.py:371
  (10 other events, 46.3 us)

commit v6 on v5

--- a/solution.py
+++ b/solution.py
@@ -200,6 +200,7 @@
         out_shape=pltpu.VMEM(x.shape, jnp.float32),
         in_specs=[VMEM, VMEM, VMEM],
         out_specs=VMEM,
+        cost_estimate=pl.CostEstimate(flops=2 * adj.size * x.shape[1], bytes_accessed=0, transcendentals=0),
         compiler_params=LIMIT,
     )(fast(x), fast(h0), fast(adj))
 
@@ -240,6 +241,7 @@
         in_specs=[SMEM, VMEM, VMEM, VMEM, HBM, VMEM],
         out_specs=VMEM,
         scratch_shapes=[pltpu.VMEM(x.shape, x.dtype), pltpu.SemaphoreType.DMA],
+        cost_estimate=pl.CostEstimate(flops=2 * adj.size * x.shape[1], bytes_accessed=0, transcendentals=0),
         compiler_params=LIMIT,
     )(info, fast(x), fast(kept_h0), fast(sent_h0), far(new_h0), fast(adj))
 
@@ -268,6 +270,7 @@
         out_specs=VMEM,
         scratch_shapes=[pltpu.VMEM((len(incoming) * block, width), incoming[0].dtype)],
         input_output_aliases={1: 0},
+        cost_estimate=pl.CostEstimate(flops=2 * adj.size * partial.shape[1], bytes_accessed=0, transcendentals=0),
         compiler_params=LIMIT,
     )(fast(adj), fast(partial), *[fast(value) for value in incoming])
 
@@ -324,6 +327,7 @@
         out_specs=[VMEM] * len(shapes),
         scratch_shapes=scratch,
         input_output_aliases={6: 2} if 0 < step < STEPS - 1 else {},
+        cost_estimate=pl.CostEstimate(flops=2 * (adj.size + weight.size * 2) * partial.shape[1], bytes_accessed=0, transcendentals=0),
         compiler_params=LIMIT,
     )(info, beta, fast(adj), fast(partial), fast(weight), far(new_h0), fast(h0), *[fast(value) for value in incoming])
 

time: 134 us -> 132 us (0.985)
  waiting for transfers between devices: 25.8 us -> 19.7 us
  starting transfers between devices: 75.3 us -> 79.6 us
    ppermute x6, starting transfers between devices: 37.4 us -> 42.9 us  [routed(): return lax.ppermute(value, 'section', pairs)]
    ppermute x6, waiting for transfers between devices: 4.73 us -> 0.59 us  [routed(): return lax.ppermute(value, 'section', pairs)]
    ppermute x5, starting transfers between devices: 10.2 us -> 7.76 us  [crossing(): return lax.ppermute(value, ('section', 'dom'), pairs)]
    ppermute x23, waiting for transfers between devices: 13.2 us -> 10.8 us  [swapped(): return lax.ppermute(value, 'dom', [(i, i ^ offset) for i in range(parts)])]
  transfers between devices with their start and end apart: 36 -> 36, of which waited for: 9 -> 8; matrix products, arithmetic and copies ran while one was open for 0% -> 0% of each run, Pallas kernels for 22% -> 22%
where the time goes in v6:
time: 132 us
  starting transfers between devices  79.6 us (60%)
  Pallas kernels  30.4 us (23%)
  waiting for transfers between devices  19.7 us (15%)
  local copies, waits for them, and re-layouts  1.56 us (1%)
    ppermute x6, starting transfers between devices, routed(): return lax.ppermute(value, 'section', pairs)  42.9 us
    ppermute x23, starting transfers between devices, swapped(): return lax.ppermute(value, 'dom', [(i, i ^ offset) for i in range(parts)])  27.2 us
    ppermute x23, waiting for transfers between devices, swapped(): return lax.ppermute(value, 'dom', [(i, i ^ offset) for i in range(parts)])  10.8 us
    ppermute x5, waiting for transfers between devices, crossing(): return lax.ppermute(value, ('section', 'dom'), pairs)  8.33 us
    ppermute x5, starting transfers between devices, crossing(): return lax.ppermute(value, ('section', 'dom'), pairs)  7.76 us
    pallas_call x4, Pallas kernels, layer(): pl.pallas_call(lambda *refs: layer_kernel(step, parts, len(incoming), *re...  7.64 us
    pallas_call x1, Pallas kernels, merged(): pl.pallas_call(lambda *refs: merge_kernel(parts, *refs), out_shape=[pltpu...  6.26 us
    pallas_call x4, Pallas kernels, arrived(): pl.pallas_call(arrived_kernel, out_shape=pltpu.VMEM(partial.shape, partia...  4.34 us
  transfers between devices with their start and end apart: 36, of which 8 were waited for; matrix products, arithmetic and copies ran while one was open for 0% of the time, Pallas kernels for 22%

profile of v6, /device:TPU:1, one launch (start us, length us, event | category | flops | bytes accessed | tf_op | source)
XLA Modules:
  0.0 131.9 jit_solution(6703859885920185034)
XLA Ops:
  1.0 1.9 %shard_map.82 = (bf16[2,128,512]{2,1,0:T(8,128)(2,1)S(1)}, bf16[2,128,512]{2,1,0:T(8,128)(2,1)S(1)}, bf16[1,128,512]{2,1,0:T(8,128)(2,1)S(1)}, bf16[1,128,512]{2,1,0:T(8,128)(2,1)S(1)}, bf16[1,128,512]{2,1,0:T(8,128)(2,1)S(1)}) custom-call(s32[15]{0:T(128)S(1)} %concatenate.3.refs_0_, bf16[1024,512]{1,0:T(8,128)(2,1)} %bitcast.8), custom_call_target="tpu_custom_call" | custom-call | tf_op jit(solution)/shard_map/pallas_call | solution.py:128
  2.9 2.2 %collective-permute-start = (bf16[2,128,512]{2,1,0:T(8,128)(2,1)S(1)}, bf16[2,128,512]{2,1,0:T(8,128)(2,1)S(1)}, u32[]{:S(2)}, u32[]{:S(2)}) collective-permute-start(bf16[2,128,512]{2,1,0:T(8,128)(2,1)S(1)} %get-tuple-element.57), channel_id=1, source_target_pairs={{0,2},{1,3},{2,0},{3,1},{4,6},{5,7},{6,4},{7,5},{8,10},{9,11},{10,... | collective-permute-start | bytes 786440 | tf_op jit(solution)/shard_map/ppermute | solution.py:80
  5.1 3.1 %collective-permute-start.1 = (bf16[2,128,512]{2,1,0:T(8,128)(2,1)S(1)}, bf16[2,128,512]{2,1,0:T(8,128)(2,1)S(1)}, u32[]{:S(2)}, u32[]{:S(2)}) collective-permute-start(bf16[2,128,512]{2,1,0:T(8,128)(2,1)S(1)} %get-tuple-element.58), channel_id=1, source_target_pairs={{0,7},{1,6},{2,5},{3,4},{4,3},{5,2},{6,1},{7,0},{8,15},{9,14},{10,... | collective-permute-start | bytes 786440 | tf_op jit(solution)/shard_map/ppermute | solution.py:80
  11.1 6.3 %shard_map.83 = (bf16[1024,1024]{1,0:T(8,128)(2,1)S(1)}, bf16[1024,640]{1,0:T(8,128)(2,1)S(1)}, bf16[1024,256]{1,0:T(8,128)(2,1)S(1)}) custom-call(s32[15]{0:T(128)S(1)} %concatenate.3.refs_0_, s32[8,24]{1,0:T(8,128)S(1)} %copy-done.4, s32[8]{0:T(128)S(1)} %copy-done.5, bf16[8,24,128,128]{3,2,1,0:T(8,128)(2,1)} %refs_3_.1), custom_call_target="tpu_custom_call" | custom-call | tf_op jit(solution)/shard_map/pallas_call | solution.py:174
  19.3 2.9 %collective-permute-start.6 = (bf16[1,128,512]{2,1,0:T(8,128)(2,1)S(1)}, bf16[1,128,512]{2,1,0:T(8,128)(2,1)S(1)}, u32[]{:S(2)}, u32[]{:S(2)}) collective-permute-start(bf16[1,128,512]{2,1,0:T(8,128)(2,1)S(1)} %slice.32), channel_id=1, source_target_pairs={{0,6},{1,7},{2,4},{3,5},{4,2},{5,3},{6,0},{7,1},{8,14},{9,15},{10,... | collective-permute-start | bytes 393224 | tf_op jit(solution)/shard_map/ppermute | solution.py:80
  22.5 5.5 %collective-permute-start.13 = (bf16[512,512]{1,0:T(8,128)(2,1)S(1)}, bf16[512,512]{1,0:T(8,128)(2,1)S(1)}, u32[]{:S(2)}, u32[]{:S(2)}) collective-permute-start(bf16[512,512]{1,0:T(8,128)(2,1)S(1)} %bitcast.13), channel_id=1, source_target_pairs={{8,0},{16,8},{24,16},{0,24},{9,1},{17,9},{25,17},{1,25},{10,2},{18... | collective-permute-start | bytes 1572872 | tf_op jit(solution)/shard_map/ppermute | solution.py:375
  29.0 1.8 %shard_map.86 = (bf16[1024,512]{1,0:T(8,128)(2,1)S(1)}, bf16[1024,512]{1,0:T(8,128)(2,1)S(1)}, bf16[1024,512]{1,0:T(8,128)(2,1)S(1)}, bf16[2,128,512]{2,1,0:T(8,...) custom-call(s32[15]{0:T(128)S(1)} %concatenate.3.refs_0_, ...), custom_call_target="tpu_custom_call" | custom-call | flops 805306368 | tf_op jit(solution)/shard_map/pallas_call | solution.py:323
  30.8 2.2 %collective-permute-start.8 = (bf16[2,128,512]{2,1,0:T(8,128)(2,1)S(1)}, bf16[2,128,512]{2,1,0:T(8,128)(2,1)S(1)}, u32[]{:S(2)}, u32[]{:S(2)}) collective-permute-start(bf16[2,128,512]{2,1,0:T(8,128)(2,1)S(1)} %get-tuple-element.71), channel_id=1, source_target_pairs={{0,2},{1,3},{2,0},{3,1},{4,6},{5,7},{6,4},{7,5},{8,10},{9,11},{10,... | collective-permute-start | bytes 786440 | tf_op jit(solution)/shard_map/ppermute | solution.py:80
  34.6 2.2 %collective-permute-done.8.rest_1_ = bf16[2,128,512]{2,1,0:T(8,128)(2,1)S(1)} collective-permute-done((bf16[2,128,512]{2,1,0:T(8,128)(2,1)S(1)}, bf16[2,128,512]{2,1,0:T(8,128)(2,1)S(1)}, u32[]{:S(2)}, u32[]{:S(2)}) %collective-permute-start.8) | collective-permute-done | bytes 262176 | tf_op jit(solution)/shard_map/ppermute | solution.py:80
  38.8 4.4 %collective-permute-done.9.rest_4_ = bf16[2,128,512]{2,1,0:T(8,128)(2,1)S(1)} collective-permute-done((bf16[2,128,512]{2,1,0:T(8,128)(2,1)S(1)}, bf16[2,128,512]{2,1,0:T(8,128)(2,1)S(1)}, u32[]{:S(2)}, u32[]{:S(2)}) %collective-permute-start.9) | collective-permute-done | bytes 262176 | tf_op jit(solution)/shard_map/ppermute | solution.py:80
  43.2 1.6 %collective-permute-start.14 = (bf16[1,128,512]{2,1,0:T(8,128)(2,1)S(1)}, bf16[1,128,512]{2,1,0:T(8,128)(2,1)S(1)}, u32[]{:S(2)}, u32[]{:S(2)}) collective-permute-start(bf16[1,128,512]{2,1,0:T(8,128)(2,1)S(1)} %slice.34), channel_id=1, source_target_pairs={{0,6},{1,7},{2,4},{3,5},{4,2},{5,3},{6,0},{7,1},{8,14},{9,15},{10,... | collective-permute-start | bytes 393224 | tf_op jit(solution)/shard_map/ppermute | solution.py:80
  44.8 5.2 %collective-permute-start.21 = (bf16[512,512]{1,0:T(8,128)(2,1)S(1)}, bf16[512,512]{1,0:T(8,128)(2,1)S(1)}, u32[]{:S(2)}, u32[]{:S(2)}) collective-permute-start(bf16[512,512]{1,0:T(8,128)(2,1)S(1)} %bitcast.15), channel_id=1, source_target_pairs={{16,0},{24,8},{0,16},{8,24},{17,1},{25,9},{1,17},{9,25},{18,2},{26... | collective-permute-start | bytes 1572872 | tf_op jit(solution)/shard_map/ppermute | solution.py:375
  51.2 2.1 %collective-permute-done.15.refs_8_ = bf16[1,128,512]{2,1,0:T(8,128)(2,1)S(1)} collective-permute-done((bf16[1,128,512]{2,1,0:T(8,128)(2,1)S(1)}, bf16[1,128,512]{2,1,0:T(8,128)(2,1)S(1)}, u32[]{:S(2)}, u32[]{:S(2)}) %collective-permute-start.15) | collective-permute-done | bytes 131104 | tf_op jit(solution)/shard_map/ppermute | solution.py:80
  53.2 1.7 %shard_map.89 = (bf16[1024,512]{1,0:T(8,128)(2,1)S(1)}, bf16[1024,512]{1,0:T(8,128)(2,1)S(1)}, bf16[1024,512]{1,0:T(8,128)(2,1)S(1)}, bf16[2,128,512]{2,1,0:T(8,...) custom-call(s32[15]{0:T(128)S(1)} %concatenate.3.refs_0_, ...), custom_call_target="tpu_custom_call", output_to_operand_aliasing={{2}: (6, {})} | custom-call | flops 805306368 | tf_op jit(solution)/shard_map/pallas_call | solution.py:323
  54.9 1.9 %collective-permute-start.16 = (bf16[2,128,512]{2,1,0:T(8,128)(2,1)S(1)}, bf16[2,128,512]{2,1,0:T(8,128)(2,1)S(1)}, u32[]{:S(2)}, u32[]{:S(2)}) collective-permute-start(bf16[2,128,512]{2,1,0:T(8,128)(2,1)S(1)} %get-tuple-element.83), channel_id=1, source_target_pairs={{0,2},{1,3},{2,0},{3,1},{4,6},{5,7},{6,4},{7,5},{8,10},{9,11},{10,... | collective-permute-start | bytes 786440 | tf_op jit(solution)/shard_map/ppermute | solution.py:80
  58.2 1.7 %collective-permute-start.19 = (bf16[1,128,512]{2,1,0:T(8,128)(2,1)S(1)}, bf16[1,128,512]{2,1,0:T(8,128)(2,1)S(1)}, u32[]{:S(2)}, u32[]{:S(2)}) collective-permute-start(bf16[1,128,512]{2,1,0:T(8,128)(2,1)S(1)} %get-tuple-element.92), channel_id=1, source_target_pairs={{0,3},{1,2},{2,1},{3,0},{4,7},{5,6},{6,5},{7,4},{8,11},{9,10},{10,... | collective-permute-start | bytes 393224 | tf_op jit(solution)/shard_map/ppermute | solution.py:80
  59.9 1.6 %collective-permute-done.16.rest_1_ = bf16[2,128,512]{2,1,0:T(8,128)(2,1)S(1)} collective-permute-done((bf16[2,128,512]{2,1,0:T(8,128)(2,1)S(1)}, bf16[2,128,512]{2,1,0:T(8,128)(2,1)S(1)}, u32[]{:S(2)}, u32[]{:S(2)}) %collective-permute-start.16) | collective-permute-done | bytes 262176 | tf_op jit(solution)/shard_map/ppermute | solution.py:80
  61.5 1.9 %collective-permute-start.20 = (bf16[1,128,512]{2,1,0:T(8,128)(2,1)S(1)}, bf16[1,128,512]{2,1,0:T(8,128)(2,1)S(1)}, u32[]{:S(2)}, u32[]{:S(2)}) collective-permute-start(bf16[1,128,512]{2,1,0:T(8,128)(2,1)S(1)} %get-tuple-element.93), channel_id=1, source_target_pairs={{0,6},{1,7},{2,4},{3,5},{4,2},{5,3},{6,0},{7,1},{8,14},{9,15},{10,... | collective-permute-start | bytes 393224 | tf_op jit(solution)/shard_map/ppermute | solution.py:80
  65.3 2.6 %collective-permute-start.22 = (bf16[1,128,512]{2,1,0:T(8,128)(2,1)S(1)}, bf16[1,128,512]{2,1,0:T(8,128)(2,1)S(1)}, u32[]{:S(2)}, u32[]{:S(2)}) collective-permute-start(bf16[1,128,512]{2,1,0:T(8,128)(2,1)S(1)} %slice.36), channel_id=1, source_target_pairs={{0,6},{1,7},{2,4},{3,5},{4,2},{5,3},{6,0},{7,1},{8,14},{9,15},{10,... | collective-permute-start | bytes 393224 | tf_op jit(solution)/shard_map/ppermute | solution.py:80
  67.8 17.3 %collective-permute-start.25 = (bf16[1024,512]{1,0:T(8,128)(2,1)S(1)}, bf16[1024,512]{1,0:T(8,128)(2,1)S(1)}, u32[]{:S(2)}, u32[]{:S(2)}) collective-permute-start(bf16[1024,512]{1,0:T(8,128)(2,1)S(1)} %get-tuple-element.98), channel_id=1, source_target_pairs={{0,8},{8,16},{16,24},{24,0},{1,9},{9,17},{17,25},{25,1},{2,10},{10... | collective-permute-start | bytes 3145736 | tf_op jit(solution)/shard_map/ppermute | solution.py:375
  86.3 2.6 %shard_map.92 = (bf16[1024,512]{1,0:T(8,128)(2,1)S(1)}, bf16[1024,512]{1,0:T(8,128)(2,1)S(1)}, bf16[1024,512]{1,0:T(8,128)(2,1)S(1)}, bf16[2,128,512]{2,1,0:T(8,...) custom-call(s32[15]{0:T(128)S(1)} %concatenate.3.refs_0_, ...), custom_call_target="tpu_custom_call", output_to_operand_aliasing={{2}: (6, {})} | custom-call | flops 805306368 | tf_op jit(solution)/shard_map/pallas_call | solution.py:323
  89.9 2.9 %collective-permute-start.31 = (bf16[512,512]{1,0:T(8,128)(2,1)S(1)}, bf16[512,512]{1,0:T(8,128)(2,1)S(1)}, u32[]{:S(2)}, u32[]{:S(2)}) collective-permute-start(bf16[512,512]{1,0:T(8,128)(2,1)S(1)} %bitcast.16), channel_id=1, source_target_pairs={{8,0},{0,8},{24,16},{16,24},{9,1},{1,9},{25,17},{17,25},{10,2},{2,... | collective-permute-start | bytes 1572872 | tf_op jit(solution)/shard_map/ppermute | solution.py:375
  94.2 1.8 %collective-permute-start.30 = (bf16[2,128,512]{2,1,0:T(8,128)(2,1)S(1)}, bf16[2,128,512]{2,1,0:T(8,128)(2,1)S(1)}, u32[]{:S(2)}, u32[]{:S(2)}) collective-permute-start(bf16[2,128,512]{2,1,0:T(8,128)(2,1)S(1)} %get-tuple-element.104), channel_id=1, source_target_pairs={{0,23},{1,22},{2,21},{3,20},{4,19},{5,18},{6,17},{7,16},{8,15},{9,... | collective-permute-start | bytes 786440 | tf_op jit(solution)/shard_map/ppermute | solution.py:89
  96.0 3.1 %collective-permute-done.27.rest_1_ = bf16[2,128,512]{2,1,0:T(8,128)(2,1)S(1)} collective-permute-done((bf16[2,128,512]{2,1,0:T(8,128)(2,1)S(1)}, bf16[2,128,512]{2,1,0:T(8,128)(2,1)S(1)}, u32[]{:S(2)}, u32[]{:S(2)}) %collective-permute-start.27) | collective-permute-done | bytes 262176 | tf_op jit(solution)/shard_map/ppermute | solution.py:89
  99.2 2.2 %collective-permute-start.28 = (bf16[1,128,512]{2,1,0:T(8,128)(2,1)S(1)}, bf16[1,128,512]{2,1,0:T(8,128)(2,1)S(1)}, u32[]{:S(2)}, u32[]{:S(2)}) collective-permute-start(bf16[1,128,512]{2,1,0:T(8,128)(2,1)S(1)} %get-tuple-element.102), channel_id=1, source_target_pairs={{0,19},{1,18},{2,17},{3,16},{4,23},{5,22},{6,21},{7,20},{8,11},{9,... | collective-permute-start | bytes 393224 | tf_op jit(solution)/shard_map/ppermute | solution.py:89
  101.4 5.2 %collective-permute-done.30.rest_4_ = bf16[2,128,512]{2,1,0:T(8,128)(2,1)S(1)} collective-permute-done((bf16[2,128,512]{2,1,0:T(8,128)(2,1)S(1)}, bf16[2,128,512]{2,1,0:T(8,128)(2,1)S(1)}, u32[]{:S(2)}, u32[]{:S(2)}) %collective-permute-start.30) | collective-permute-done | bytes 262176 | tf_op jit(solution)/shard_map/ppermute | solution.py:89
  106.6 2.3 %collective-permute-start.29 = (bf16[1,128,512]{2,1,0:T(8,128)(2,1)S(1)}, bf16[1,128,512]{2,1,0:T(8,128)(2,1)S(1)}, u32[]{:S(2)}, u32[]{:S(2)}) collective-permute-start(bf16[1,128,512]{2,1,0:T(8,128)(2,1)S(1)} %get-tuple-element.103), channel_id=1, source_target_pairs={{0,22},{1,23},{2,20},{3,21},{4,18},{5,19},{6,16},{7,17},{8,14},{9,... | collective-permute-start | bytes 393224 | tf_op jit(solution)/shard_map/ppermute | solution.py:89
  110.0 2.0 %shard_map.93.partial = f32[1024,512]{1,0:T(8,128)S(1)} custom-call(s32[15]{0:T(128)S(1)} %concatenate.3.refs_0_, bf16[1024,512]{1,0:T(8,128)(2,1)S(1)} %collective-permute-done.24.refs_1_, bf16[1024,512]{1,0:T(8,128)(2,1)S(1)} %get-tuple-element.96.refs_2_.refs_6_, bf16[1024,512]{1,0:T(8,128)(2,1)S(1)} %collective-permute-done.2.refs_3_, ...), custom_call_target="tpu_custom_call" | custom-call | flops 1073741824 | tf_op jit(solution)/shard_map/pallas_call | solution.py:238
  112.0 3.6 %collective-permute-start.35 = (bf16[1024,512]{1,0:T(8,128)(2,1)S(1)}, bf16[1024,512]{1,0:T(8,128)(2,1)S(1)}, u32[]{:S(2)}, u32[]{:S(2)}) collective-permute-start(bf16[1024,512]{1,0:T(8,128)(2,1)S(1)} %get-tuple-element.106), channel_id=1, source_target_pairs={{8,24},{24,8},{9,25},{25,9},{10,26},{26,10},{11,27},{27,11},{12,28... | collective-permute-start | bytes 3145736 | tf_op jit(solution)/shard_map/ppermute | solution.py:375
  116.7 1.6 %shard_map.95 = bf16[1024,512]{1,0:T(8,128)(2,1)S(1)} custom-call(s32[15]{0:T(128)S(1)} %concatenate.3.refs_0_, f32[4]{0:T(128)S(1)} %fusion.5.refs_1_, bf16[1024,256]{1,0:T(8,128)(2,1)S(1)} %get-tuple-element.63.refs_2_, f32[1024,512]{1,0:T(8,128)S(1)} %shard_map.94.refs_3_, bf16[512,512]{1,0:T(8,128)(2,1)S(1)} %collective-permute-done.31.refs_4_, ...), custom_call_target="tpu_custom_call" | custom-call | flops 805306368 | tf_op jit(solution)/shard_map/pallas_call | solution.py:323
  118.3 8.4 %collective-permute-start.34 = (bf16[1024,512]{1,0:T(8,128)(2,1)S(1)}, bf16[1024,512]{1,0:T(8,128)(2,1)S(1)}, u32[]{:S(2)}, u32[]{:S(2)}) collective-permute-start(bf16[1024,512]{1,0:T(8,128)(2,1)S(1)} %shard_map.95), channel_id=1, source_target_pairs={{0,8},{8,0},{16,24},{24,16},{1,9},{9,1},{17,25},{25,17},{2,10},{10... | collective-permute-start | bytes 3145736 | tf_op jit(solution)/shard_map/ppermute | solution.py:375
  129.2 1.5 %shard_map.98.refs_1_ = bf16[1,4,1024,512]{3,2,1,0:T(8,128)(2,1)} custom-call(s32[15]{0:T(128)S(1)} %concatenate.3.refs_0_, bf16[1024,512]{1,0:T(8,128)(2,1)S(1)} %collective-permute-done.24.refs_1_, bf16[1024,512]{1,0:T(8,128)(2,1)S(1)} %collective-permute-done.35.refs_2_, bf16[1,4,1024,512]{3,2,1,0:T(8,128)(2,1)} %shard_map.97.refs_3_), custom_call_target="tpu_custom_call", output_to_operand_aliasing={{}: (3, {})} | custom-call | tf_op jit(solution)/shard_map/pallas_call | solution.py:361
  (83 shorter events, 24.2 us)
Async XLA Ops:
  0.0 22.2 %collective-permute-start.2 = (bf16[1024,512]{1,0:T(8,128)(2,1)}, bf16[1024,512]{1,0:T(8,128)(2,1)S(1)}, u32[]{:S(2)}, u32[]{:S(2)}) collective-permute-start(bf16[1024,512]{1,0:T(8,128)(2,1)} %bitcast.10), channel_id=1, source_target_pairs={{0,16},{1,17},{2,18},{3,19},{4,20},{5,21},{6,22},{7,23}} | collective-permute-start | bytes 3145736 | tf_op jit(solution)/shard_map/ppermute | solution.py:433
  2.9 14.5 %collective-permute-start = (bf16[2,128,512]{2,1,0:T(8,128)(2,1)S(1)}, bf16[2,128,512]{2,1,0:T(8,128)(2,1)S(1)}, u32[]{:S(2)}, u32[]{:S(2)}) collective-permute-start(bf16[2,128,512]{2,1,0:T(8,128)(2,1)S(1)} %get-tuple-element.57), channel_id=1, source_target_pairs={{0,2},{1,3},{2,0},{3,1},{4,6},{5,7},{6,4},{7,5},{8,10},{9,11},{10,... | collective-permute-start | bytes 786440 | tf_op jit(solution)/shard_map/ppermute | solution.py:80
  5.1 14.1 %collective-permute-start.1 = (bf16[2,128,512]{2,1,0:T(8,128)(2,1)S(1)}, bf16[2,128,512]{2,1,0:T(8,128)(2,1)S(1)}, u32[]{:S(2)}, u32[]{:S(2)}) collective-permute-start(bf16[2,128,512]{2,1,0:T(8,128)(2,1)S(1)} %get-tuple-element.58), channel_id=1, source_target_pairs={{0,7},{1,6},{2,5},{3,4},{4,3},{5,2},{6,1},{7,0},{8,15},{9,14},{10,... | collective-permute-start | bytes 786440 | tf_op jit(solution)/shard_map/ppermute | solution.py:80
  8.2 14.2 %collective-permute-start.3 = (bf16[1,128,512]{2,1,0:T(8,128)(2,1)S(1)}, bf16[1,128,512]{2,1,0:T(8,128)(2,1)S(1)}, u32[]{:S(2)}, u32[]{:S(2)}) collective-permute-start(bf16[1,128,512]{2,1,0:T(8,128)(2,1)S(1)} %get-tuple-element.59), channel_id=1, source_target_pairs={{0,1},{1,0},{2,3},{3,2},{4,5},{5,4},{6,7},{7,6},{8,9},{9,8},{10,11... | collective-permute-start | bytes 393224 | tf_op jit(solution)/shard_map/ppermute | solution.py:80
  8.5 19.4 %collective-permute-start.4 = (bf16[1,128,512]{2,1,0:T(8,128)(2,1)S(1)}, bf16[1,128,512]{2,1,0:T(8,128)(2,1)S(1)}, u32[]{:S(2)}, u32[]{:S(2)}) collective-permute-start(bf16[1,128,512]{2,1,0:T(8,128)(2,1)S(1)} %get-tuple-element.60), channel_id=1, source_target_pairs={{0,3},{1,2},{2,1},{3,0},{4,7},{5,6},{6,5},{7,4},{8,11},{9,10},{10,... | collective-permute-start | bytes 393224 | tf_op jit(solution)/shard_map/ppermute | solution.py:80
  17.4 10.5 %collective-permute-start.5 = (bf16[1,128,512]{2,1,0:T(8,128)(2,1)S(1)}, bf16[1,128,512]{2,1,0:T(8,128)(2,1)S(1)}, u32[]{:S(2)}, u32[]{:S(2)}) collective-permute-start(bf16[1,128,512]{2,1,0:T(8,128)(2,1)S(1)} %get-tuple-element.61), channel_id=1, source_target_pairs={{0,6},{1,7},{2,4},{3,5},{4,2},{5,3},{6,0},{7,1},{8,14},{9,15},{10,... | collective-permute-start | bytes 393224 | tf_op jit(solution)/shard_map/ppermute | solution.py:80
  19.3 9.7 %collective-permute-start.6 = (bf16[1,128,512]{2,1,0:T(8,128)(2,1)S(1)}, bf16[1,128,512]{2,1,0:T(8,128)(2,1)S(1)}, u32[]{:S(2)}, u32[]{:S(2)}) collective-permute-start(bf16[1,128,512]{2,1,0:T(8,128)(2,1)S(1)} %slice.32), channel_id=1, source_target_pairs={{0,6},{1,7},{2,4},{3,5},{4,2},{5,3},{6,0},{7,1},{8,14},{9,15},{10,... | collective-permute-start | bytes 393224 | tf_op jit(solution)/shard_map/ppermute | solution.py:80
  22.2 6.9 %collective-permute-start.7 = (bf16[1,128,512]{2,1,0:T(8,128)(2,1)S(1)}, bf16[1,128,512]{2,1,0:T(8,128)(2,1)S(1)}, u32[]{:S(2)}, u32[]{:S(2)}) collective-permute-start(bf16[1,128,512]{2,1,0:T(8,128)(2,1)S(1)} %slice.33), channel_id=1, source_target_pairs={{0,2},{1,3},{2,0},{3,1},{4,6},{5,7},{6,4},{7,5},{8,10},{9,11},{10,... | collective-permute-start | bytes 393224 | tf_op jit(solution)/shard_map/ppermute | solution.py:80
  22.5 28.7 %collective-permute-start.13 = (bf16[512,512]{1,0:T(8,128)(2,1)S(1)}, bf16[512,512]{1,0:T(8,128)(2,1)S(1)}, u32[]{:S(2)}, u32[]{:S(2)}) collective-permute-start(bf16[512,512]{1,0:T(8,128)(2,1)S(1)} %bitcast.13), channel_id=1, source_target_pairs={{8,0},{16,8},{24,16},{0,24},{9,1},{17,9},{25,17},{1,25},{10,2},{18... | collective-permute-start | bytes 1572872 | tf_op jit(solution)/shard_map/ppermute | solution.py:375
  33.0 10.1 %collective-permute-start.9 = (bf16[2,128,512]{2,1,0:T(8,128)(2,1)S(1)}, bf16[2,128,512]{2,1,0:T(8,128)(2,1)S(1)}, u32[]{:S(2)}, u32[]{:S(2)}) collective-permute-start(bf16[2,128,512]{2,1,0:T(8,128)(2,1)S(1)} %get-tuple-element.72), channel_id=1, source_target_pairs={{0,7},{1,6},{2,5},{3,4},{4,3},{5,2},{6,1},{7,0},{8,15},{9,14},{10,... | collective-permute-start | bytes 786440 | tf_op jit(solution)/shard_map/ppermute | solution.py:80
  34.3 10.5 %collective-permute-start.10 = (bf16[1,128,512]{2,1,0:T(8,128)(2,1)S(1)}, bf16[1,128,512]{2,1,0:T(8,128)(2,1)S(1)}, u32[]{:S(2)}, u32[]{:S(2)}) collective-permute-start(bf16[1,128,512]{2,1,0:T(8,128)(2,1)S(1)} %get-tuple-element.79), channel_id=1, source_target_pairs={{0,1},{1,0},{2,3},{3,2},{4,5},{5,4},{6,7},{7,6},{8,9},{9,8},{10,11... | collective-permute-start | bytes 393224 | tf_op jit(solution)/shard_map/ppermute | solution.py:80
  34.5 10.3 %collective-permute-start.11 = (bf16[1,128,512]{2,1,0:T(8,128)(2,1)S(1)}, bf16[1,128,512]{2,1,0:T(8,128)(2,1)S(1)}, u32[]{:S(2)}, u32[]{:S(2)}) collective-permute-start(bf16[1,128,512]{2,1,0:T(8,128)(2,1)S(1)} %get-tuple-element.80), channel_id=1, source_target_pairs={{0,3},{1,2},{2,1},{3,0},{4,7},{5,6},{6,5},{7,4},{8,11},{9,10},{10,... | collective-permute-start | bytes 393224 | tf_op jit(solution)/shard_map/ppermute | solution.py:80
  36.8 13.2 %collective-permute-start.12 = (bf16[1,128,512]{2,1,0:T(8,128)(2,1)S(1)}, bf16[1,128,512]{2,1,0:T(8,128)(2,1)S(1)}, u32[]{:S(2)}, u32[]{:S(2)}) collective-permute-start(bf16[1,128,512]{2,1,0:T(8,128)(2,1)S(1)} %get-tuple-element.81), channel_id=1, source_target_pairs={{0,6},{1,7},{2,4},{3,5},{4,2},{5,3},{6,0},{7,1},{8,14},{9,15},{10,... | collective-permute-start | bytes 393224 | tf_op jit(solution)/shard_map/ppermute | solution.py:80
  43.2 8.0 %collective-permute-start.14 = (bf16[1,128,512]{2,1,0:T(8,128)(2,1)S(1)}, bf16[1,128,512]{2,1,0:T(8,128)(2,1)S(1)}, u32[]{:S(2)}, u32[]{:S(2)}) collective-permute-start(bf16[1,128,512]{2,1,0:T(8,128)(2,1)S(1)} %slice.34), channel_id=1, source_target_pairs={{0,6},{1,7},{2,4},{3,5},{4,2},{5,3},{6,0},{7,1},{8,14},{9,15},{10,... | collective-permute-start | bytes 393224 | tf_op jit(solution)/shard_map/ppermute | solution.py:80
  44.8 8.4 %collective-permute-start.15 = (bf16[1,128,512]{2,1,0:T(8,128)(2,1)S(1)}, bf16[1,128,512]{2,1,0:T(8,128)(2,1)S(1)}, u32[]{:S(2)}, u32[]{:S(2)}) collective-permute-start(bf16[1,128,512]{2,1,0:T(8,128)(2,1)S(1)} %slice.35), channel_id=1, source_target_pairs={{0,2},{1,3},{2,0},{3,1},{4,6},{5,7},{6,4},{7,5},{8,10},{9,11},{10,... | collective-permute-start | bytes 393224 | tf_op jit(solution)/shard_map/ppermute | solution.py:80
  44.8 41.5 %collective-permute-start.21 = (bf16[512,512]{1,0:T(8,128)(2,1)S(1)}, bf16[512,512]{1,0:T(8,128)(2,1)S(1)}, u32[]{:S(2)}, u32[]{:S(2)}) collective-permute-start(bf16[512,512]{1,0:T(8,128)(2,1)S(1)} %bitcast.15), channel_id=1, source_target_pairs={{16,0},{24,8},{0,16},{8,24},{17,1},{25,9},{1,17},{9,25},{18,2},{26... | collective-permute-start | bytes 1572872 | tf_op jit(solution)/shard_map/ppermute | solution.py:375
  56.8 8.4 %collective-permute-start.17 = (bf16[2,128,512]{2,1,0:T(8,128)(2,1)S(1)}, bf16[2,128,512]{2,1,0:T(8,128)(2,1)S(1)}, u32[]{:S(2)}, u32[]{:S(2)}) collective-permute-start(bf16[2,128,512]{2,1,0:T(8,128)(2,1)S(1)} %get-tuple-element.84), channel_id=1, source_target_pairs={{0,7},{1,6},{2,5},{3,4},{4,3},{5,2},{6,1},{7,0},{8,15},{9,14},{10,... | collective-permute-start | bytes 786440 | tf_op jit(solution)/shard_map/ppermute | solution.py:80
  58.2 9.6 %collective-permute-start.18 = (bf16[1,128,512]{2,1,0:T(8,128)(2,1)S(1)}, bf16[1,128,512]{2,1,0:T(8,128)(2,1)S(1)}, u32[]{:S(2)}, u32[]{:S(2)}) collective-permute-start(bf16[1,128,512]{2,1,0:T(8,128)(2,1)S(1)} %get-tuple-element.91), channel_id=1, source_target_pairs={{0,1},{1,0},{2,3},{3,2},{4,5},{5,4},{6,7},{7,6},{8,9},{9,8},{10,11... | collective-permute-start | bytes 393224 | tf_op jit(solution)/shard_map/ppermute | solution.py:80
  58.2 9.6 %collective-permute-start.19 = (bf16[1,128,512]{2,1,0:T(8,128)(2,1)S(1)}, bf16[1,128,512]{2,1,0:T(8,128)(2,1)S(1)}, u32[]{:S(2)}, u32[]{:S(2)}) collective-permute-start(bf16[1,128,512]{2,1,0:T(8,128)(2,1)S(1)} %get-tuple-element.92), channel_id=1, source_target_pairs={{0,3},{1,2},{2,1},{3,0},{4,7},{5,6},{6,5},{7,4},{8,11},{9,10},{10,... | collective-permute-start | bytes 393224 | tf_op jit(solution)/shard_map/ppermute | solution.py:80
  61.5 23.7 %collective-permute-start.20 = (bf16[1,128,512]{2,1,0:T(8,128)(2,1)S(1)}, bf16[1,128,512]{2,1,0:T(8,128)(2,1)S(1)}, u32[]{:S(2)}, u32[]{:S(2)}) collective-permute-start(bf16[1,128,512]{2,1,0:T(8,128)(2,1)S(1)} %get-tuple-element.93), channel_id=1, source_target_pairs={{0,6},{1,7},{2,4},{3,5},{4,2},{5,3},{6,0},{7,1},{8,14},{9,15},{10,... | collective-permute-start | bytes 393224 | tf_op jit(solution)/shard_map/ppermute | solution.py:80
  65.3 21.0 %collective-permute-start.22 = (bf16[1,128,512]{2,1,0:T(8,128)(2,1)S(1)}, bf16[1,128,512]{2,1,0:T(8,128)(2,1)S(1)}, u32[]{:S(2)}, u32[]{:S(2)}) collective-permute-start(bf16[1,128,512]{2,1,0:T(8,128)(2,1)S(1)} %slice.36), channel_id=1, source_target_pairs={{0,6},{1,7},{2,4},{3,5},{4,2},{5,3},{6,0},{7,1},{8,14},{9,15},{10,... | collective-permute-start | bytes 393224 | tf_op jit(solution)/shard_map/ppermute | solution.py:80
  67.8 18.5 %collective-permute-start.23 = (bf16[1,128,512]{2,1,0:T(8,128)(2,1)S(1)}, bf16[1,128,512]{2,1,0:T(8,128)(2,1)S(1)}, u32[]{:S(2)}, u32[]{:S(2)}) collective-permute-start(bf16[1,128,512]{2,1,0:T(8,128)(2,1)S(1)} %slice.37), channel_id=1, source_target_pairs={{0,2},{1,3},{2,0},{3,1},{4,6},{5,7},{6,4},{7,5},{8,10},{9,11},{10,... | collective-permute-start | bytes 393224 | tf_op jit(solution)/shard_map/ppermute | solution.py:80
  67.8 41.0 %collective-permute-start.25 = (bf16[1024,512]{1,0:T(8,128)(2,1)S(1)}, bf16[1024,512]{1,0:T(8,128)(2,1)S(1)}, u32[]{:S(2)}, u32[]{:S(2)}) collective-permute-start(bf16[1024,512]{1,0:T(8,128)(2,1)S(1)} %get-tuple-element.98), channel_id=1, source_target_pairs={{0,8},{8,16},{16,24},{24,0},{1,9},{9,17},{17,25},{25,1},{2,10},{10... | collective-permute-start | bytes 3145736 | tf_op jit(solution)/shard_map/ppermute | solution.py:375
  88.9 21.0 %collective-permute-start.24 = (bf16[1024,512]{1,0:T(8,128)(2,1)S(1)}, bf16[1024,512]{1,0:T(8,128)(2,1)S(1)}, u32[]{:S(2)}, u32[]{:S(2)}) collective-permute-start(bf16[1024,512]{1,0:T(8,128)(2,1)S(1)} %get-tuple-element.95), channel_id=1, source_target_pairs={{0,16},{8,8},{16,0},{24,24},{1,17},{9,9},{17,1},{25,25},{2,18},{10... | collective-permute-start | bytes 3145736 | tf_op jit(solution)/shard_map/ppermute | solution.py:422
  89.9 26.8 %collective-permute-start.31 = (bf16[512,512]{1,0:T(8,128)(2,1)S(1)}, bf16[512,512]{1,0:T(8,128)(2,1)S(1)}, u32[]{:S(2)}, u32[]{:S(2)}) collective-permute-start(bf16[512,512]{1,0:T(8,128)(2,1)S(1)} %bitcast.16), channel_id=1, source_target_pairs={{8,0},{0,8},{24,16},{16,24},{9,1},{1,9},{25,17},{17,25},{10,2},{2,... | collective-permute-start | bytes 1572872 | tf_op jit(solution)/shard_map/ppermute | solution.py:375
  94.2 12.4 %collective-permute-start.30 = (bf16[2,128,512]{2,1,0:T(8,128)(2,1)S(1)}, bf16[2,128,512]{2,1,0:T(8,128)(2,1)S(1)}, u32[]{:S(2)}, u32[]{:S(2)}) collective-permute-start(bf16[2,128,512]{2,1,0:T(8,128)(2,1)S(1)} %get-tuple-element.104), channel_id=1, source_target_pairs={{0,23},{1,22},{2,21},{3,20},{4,19},{5,18},{6,17},{7,16},{8,15},{9,... | collective-permute-start | bytes 786440 | tf_op jit(solution)/shard_map/ppermute | solution.py:89
  99.2 12.8 %collective-permute-start.28 = (bf16[1,128,512]{2,1,0:T(8,128)(2,1)S(1)}, bf16[1,128,512]{2,1,0:T(8,128)(2,1)S(1)}, u32[]{:S(2)}, u32[]{:S(2)}) collective-permute-start(bf16[1,128,512]{2,1,0:T(8,128)(2,1)S(1)} %get-tuple-element.102), channel_id=1, source_target_pairs={{0,19},{1,18},{2,17},{3,16},{4,23},{5,22},{6,21},{7,20},{8,11},{9,... | collective-permute-start | bytes 393224 | tf_op jit(solution)/shard_map/ppermute | solution.py:89
  106.6 9.0 %collective-permute-start.29 = (bf16[1,128,512]{2,1,0:T(8,128)(2,1)S(1)}, bf16[1,128,512]{2,1,0:T(8,128)(2,1)S(1)}, u32[]{:S(2)}, u32[]{:S(2)}) collective-permute-start(bf16[1,128,512]{2,1,0:T(8,128)(2,1)S(1)} %get-tuple-element.103), channel_id=1, source_target_pairs={{0,22},{1,23},{2,20},{3,21},{4,18},{5,19},{6,16},{7,17},{8,14},{9,... | collective-permute-start | bytes 393224 | tf_op jit(solution)/shard_map/ppermute | solution.py:89
  108.9 7.8 %collective-permute-start.32 = (bf16[1,128,512]{2,1,0:T(8,128)(2,1)S(1)}, bf16[1,128,512]{2,1,0:T(8,128)(2,1)S(1)}, u32[]{:S(2)}, u32[]{:S(2)}) collective-permute-start(bf16[1,128,512]{2,1,0:T(8,128)(2,1)S(1)} %slice.40), channel_id=1, source_target_pairs={{0,6},{1,7},{2,4},{3,5},{4,2},{5,3},{6,0},{7,1},{8,14},{9,15},{10,... | collective-permute-start | bytes 393224 | tf_op jit(solution)/shard_map/ppermute | solution.py:80
  110.0 6.7 %collective-permute-start.33 = (bf16[1,128,512]{2,1,0:T(8,128)(2,1)S(1)}, bf16[1,128,512]{2,1,0:T(8,128)(2,1)S(1)}, u32[]{:S(2)}, u32[]{:S(2)}) collective-permute-start(bf16[1,128,512]{2,1,0:T(8,128)(2,1)S(1)} %slice.41), channel_id=1, source_target_pairs={{0,2},{1,3},{2,0},{3,1},{4,6},{5,7},{6,4},{7,5},{8,10},{9,11},{10,... | collective-permute-start | bytes 393224 | tf_op jit(solution)/shard_map/ppermute | solution.py:80
  112.0 17.2 %collective-permute-start.35 = (bf16[1024,512]{1,0:T(8,128)(2,1)S(1)}, bf16[1024,512]{1,0:T(8,128)(2,1)S(1)}, u32[]{:S(2)}, u32[]{:S(2)}) collective-permute-start(bf16[1024,512]{1,0:T(8,128)(2,1)S(1)} %get-tuple-element.106), channel_id=1, source_target_pairs={{8,24},{24,8},{9,25},{25,9},{10,26},{26,10},{11,27},{27,11},{12,28... | collective-permute-start | bytes 3145736 | tf_op jit(solution)/shard_map/ppermute | solution.py:375
  118.3 12.5 %collective-permute-start.34 = (bf16[1024,512]{1,0:T(8,128)(2,1)S(1)}, bf16[1024,512]{1,0:T(8,128)(2,1)S(1)}, u32[]{:S(2)}, u32[]{:S(2)}) collective-permute-start(bf16[1024,512]{1,0:T(8,128)(2,1)S(1)} %shard_map.95), channel_id=1, source_target_pairs={{0,8},{8,0},{16,24},{24,16},{1,9},{9,1},{17,25},{25,17},{2,10},{10... | collective-permute-start | bytes 3145736 | tf_op jit(solution)/shard_map/ppermute | solution.py:375
  (10 other events, 43.7 us)
